TPU v7x, 32 devices: a whole 2x2x4 slice. The times are simulated.
32 devices in a mesh: groups: 1, expert: 8 (over z, y), dp: 4 (over x, core).
Axes of the slice: x: 2, y: 2, z: 4, core: 2. Of those that a mesh axis runs over, the one named last changes fastest.
Arguments:
- tokens: bfloat16 [4096, 2048], P(('groups', 'expert', 'dp')), may hold values from -6 to 6
- expert_ids: int32 [4096, 10], P(('groups', 'expert', 'dp')), may hold values from 0 to 31, all different within a row; in each aligned block of 128 rows (0 to 127, 128 to 255, ...) at most 48 rows name the same one
- route_weight: bfloat16 [4096, 10], P(('groups', 'expert', 'dp')), may hold values from 0.019897461 to 0.29882812
- expert_gate: bfloat16 [32, 2048, 512], P(('expert', 'dp')), may hold values from -0.125 to 0.125
- expert_up: bfloat16 [32, 2048, 512], P(('expert', 'dp')), may hold values from -0.125 to 0.125
- expert_down: bfloat16 [32, 512, 2048], P(('expert', 'dp')), may hold values from -0.25 to 0.25
- shared_gate_up: bfloat16 [2048, 1024], P('dp'), may hold values from -0.125 to 0.125
- shared_down: bfloat16 [512, 2048], P(None, 'dp'), may hold values from -0.25 to 0.25
- shared_switch: bfloat16 [2048], replicated, may hold values from -0.125 to 0.125
Outputs:
- mixed: bfloat16 [4096, 2048], P(('groups', 'expert', 'dp'))
Inputs may be any that keep to these rules, and one draw needn't show every extreme that they name: `expert_ids`: each row names 10 different experts. Within the 128 rows of one device no expert is named by more than 48 rows, and in some device's rows one expert is named exactly 48 times.
All inputs are finite; a program needn't handle non-finite values.
Results may differ from a plain program's by a relative error of at most 0.0053.
Values may be sent and summed in bfloat16 or wider, within the bound.
No kernel may reach another device: no remote copies, remote signals or barrier semaphores. Data moves between devices by JAX's collectives and lax.ppermute only.
A program may use at most 128 MiB of HBM per device.

v0:
```python
import jax
import jax.numpy as jnp
from jax import lax
from jax.sharding import PartitionSpec as P


def shards(
    tokens,
    expert_ids,
    route_weight,
    expert_gate,
    expert_up,
    expert_down,
    shared_gate_up,
    shared_down,
    shared_switch,
):
    tok_count, width = tokens.shape
    top_count = expert_ids.shape[1]
    device_count = lax.axis_size(("expert", "dp"))
    capacity = tok_count * top_count * 6 // (5 * device_count)
    assign_count = tok_count * top_count
    flat_ids = expert_ids.reshape(-1)
    one_hot = (flat_ids[:, None] == jnp.arange(device_count, dtype=jnp.int32)[None, :]).astype(
        jnp.int32
    )
    before = jnp.cumsum(one_hot, axis=0) - one_hot
    slot_rank = jnp.sum(before * one_hot, axis=1)
    slot_index = flat_ids * capacity + slot_rank
    filler = jnp.full((device_count * capacity,), assign_count, jnp.int32)
    owner = filler.at[slot_index].set(jnp.arange(assign_count, dtype=jnp.int32))
    filled = owner < assign_count
    picked = jnp.minimum(owner, assign_count - 1)
    outgoing = jnp.where(filled[:, None], tokens[picked // top_count], jnp.bfloat16(0.0))
    outgoing = outgoing.reshape(device_count, capacity, width)
    out_weight = jnp.where(filled, route_weight.reshape(-1)[picked], jnp.bfloat16(0.0))
    out_weight = out_weight.reshape(device_count, capacity)
    arrived = lax.all_to_all(outgoing, ("expert", "dp"), split_axis=0, concat_axis=0, tiled=True)
    shape = arrived.shape
    inputs = arrived.reshape(-1, width)
    gate = jnp.dot(inputs, expert_gate[0], preferred_element_type=jnp.float32)
    upper = jnp.dot(inputs, expert_up[0], preferred_element_type=jnp.float32)
    hidden = (jax.nn.silu(gate) * upper).astype(jnp.bfloat16)
    answer = jnp.dot(hidden, expert_down[0], preferred_element_type=jnp.float32)
    answer = answer * lax.all_to_all(
        out_weight, ("expert", "dp"), split_axis=0, concat_axis=0, tiled=True
    ).reshape(-1, 1).astype(jnp.float32)
    returned = lax.all_to_all(
        answer.astype(jnp.bfloat16).reshape(shape),
        ("expert", "dp"),
        split_axis=0,
        concat_axis=0,
        tiled=True,
    )
    returned = returned.reshape(device_count * capacity, width)
    gathered = returned[slot_index].reshape(tok_count, top_count, width)
    routed = jnp.zeros((tok_count, width), jnp.float32)
    for column in range(top_count):
        routed = routed + gathered[:, column].astype(jnp.float32)
    both = jnp.dot(
        tokens,
        lax.all_gather(shared_gate_up, "dp", axis=0, tiled=True),
        preferred_element_type=jnp.float32,
    )
    half_width = both.shape[1] // 2
    shared_hidden = (jax.nn.silu(both[:, :half_width]) * both[:, half_width:]).astype(jnp.bfloat16)
    shared_out = jnp.dot(
        shared_hidden,
        lax.all_gather(shared_down, "dp", axis=1, tiled=True),
        preferred_element_type=jnp.float32,
    )
    switch = jax.nn.sigmoid(jnp.dot(tokens, shared_switch, preferred_element_type=jnp.float32))
    return (routed + switch[:, None] * shared_out).astype(jnp.bfloat16)


def solution(mesh):
    in_specs = (
        P(("groups", "expert", "dp"), None),
        P(("groups", "expert", "dp"), None),
        P(("groups", "expert", "dp"), None),
        P(("expert", "dp"), None, None),
        P(("expert", "dp"), None, None),
        P(("expert", "dp"), None, None),
        P("dp", None),
        P(None, "dp"),
        P(),
    )
    out_specs = P(("groups", "expert", "dp"), None)
    return jax.shard_map(shards, mesh=mesh, in_specs=in_specs, out_specs=out_specs, check_vma=False)
```

profile of v0, /device:TPU:0, one launch (start us, length us, event | category | flops | bytes accessed | tf_op | source)
XLA Modules:
  0.0 426.5 jit_solution(4685738078305310624)
XLA Ops:
  6.5 0.0 copy-start
  6.5 1.0 copy.27
  7.5 0.1 eq.29
  7.6 0.1 eq.25
  7.8 0.7 broadcast_multiply_fusion
  8.5 9.1 %reduce-window.6 = s32[32,10,128]{2,1,0:T(8,128)S(1)} reduce-window(s32[32,10,128]{2,1,0:T(8,128)S(1)} %fusion.14, s32[]{:T(128)} %constant.13.clone.1), window={size=1x1x128 pad=0_0x0_0x127_0}, to_apply=%region_0.0 | reduce-window | flops 5201920 | bytes 327684 | tf_op jit(solution)/shard_map/reduce-window
  17.6 0.1 slice.62
  17.7 0.2 copy.29
  17.9 0.1 copy.30
  18.0 0.1 broadcast_add_fusion
  18.2 0.1 copy.26
  18.3 0.1 mul.51
  18.4 0.1 fusion.17
  18.5 5.2 %scatter_custom_fusion = s32[1536]{0:T(1024)S(1)} fusion(s32[1280]{0:T(1024)S(1)} %fusion.21, s32[1280]{0:T(1024)S(1)} %iota.11, s32[]{:T(128)} %constant.11.clone.1), kind=kCustom, calls=%fused_computation.45 | custom fusion | bytes 6148 | tf_op jit(solution)/shard_map/scatter | solution.py:31
  23.8 0.8 copy.31
  24.6 0.1 reshape.106
  24.8 9.5 %gather_fusion.1 = bf16[1536]{0:T(1024)(128)(2,1)S(1)} fusion(bf16[1280]{0:T(1024)(128)(2,1)S(1)} %reshape.106, s32[2048]{0:T(1024)S(1)} %get-tuple-element.19), kind=kCustom, calls=%fused_computation.1 | custom fusion | bytes 12288 | tf_op jit(solution)/shard_map/gather | solution.py:36
  34.3 0.7 all_to_all.16
  35.0 7.3 %all-to-all-start.1 = ((bf16[32,1,48]{2,1,0:T(2,128)(2,1)}), bf16[32,1,48]{2,1,0:T(2,128)(2,1)S(1)}, u32[]{:S(2)}, u32[]{:S(2)}) async-start(bf16[32,1,48]{2,1,0:T(2,128)(2,1)} %all_to_all.16), calls=%async_computation.1 | async-start | bytes 32768 | tf_op jit(solution)/shard_map/all_to_all | solution.py:45
  42.3 0.1 broadcast_in_dim.29
  42.4 0.0 copy-done.2
  42.4 7.1 %gather_fusion = bf16[1536,2048]{1,0:T(8,128)(2,1)} fusion(bf16[128,2048]{1,0:T(8,128)(2,1)S(1)} %copy-done.2, s32[2048]{0:T(1024)S(1)} %get-tuple-element.20), kind=kCustom, calls=%fused_computation | custom fusion | bytes 12589056 | tf_op jit(solution)/shard_map/gather | solution.py:34
  49.5 5.9 %broadcast_select_fusion = bf16[32,48,2048]{2,1,0:T(8,128)(2,1)} fusion(bf16[32,48,2048]{2,1,0:T(8,128)(2,1)} %bitcast.53, pred[32,48]{1,0:T(8,128)(4,1)S(1)} %broadcast_in_dim.29), kind=kLoop, calls=%fused_computation.5 | loop fusion | flops 3145728 | bytes 12584448 | tf_op jit(solution)/shard_map/jit(_where)/select_n | solution.py:34
  55.4 0.0 all-to-all-done.1
  55.4 5.9 %all-to-all-start = ((bf16[32,48,2048]{2,1,0:T(8,128)(2,1)}), bf16[32,48,2048]{2,1,0:T(8,128)(2,1)}, u32[]{:S(2)}, u32[]{:S(2)}) async-start(bf16[32,48,2048]{2,1,0:T(8,128)(2,1)} %broadcast_select_fusion), calls=%async_computation | async-start | bytes 12582912 | tf_op jit(solution)/shard_map/all_to_all | solution.py:38
  61.4 0.1 convert_reduce_fusion
  61.4 0.1 reshape.110
  61.5 139.9 %all-to-all-done = bf16[32,48,2048]{2,1,0:T(8,128)(2,1)} async-done(((bf16[32,48,2048]{2,1,0:T(8,128)(2,1)}), bf16[32,48,2048]{2,1,0:T(8,128)(2,1)}, u32[]{:S(2)}, u32[]{:S(2)}) %all-to-all-start) | async-done | bytes 6291488 | tf_op jit(solution)/shard_map/all_to_all | solution.py:38
  201.4 8.5 %fusion.5 = f32[1536,512]{1,0:T(8,128)} fusion(bf16[1536,2048]{1,0:T(8,128)(2,1)} %bitcast.3, bf16[1,2048,512]{2,1,0:T(8,128)(2,1)} %param.12), kind=kOutput, calls=%fused_computation.13 | convolution fusion | flops 3221225472 | bytes 11534336 | tf_op jit(solution)/shard_map/dot_general | solution.py:41
  209.9 0.0 copy-done
  209.9 11.7 %multiply_convert_fusion = bf16[1536,2048]{1,0:T(8,128)(2,1)} fusion(f32[1536]{0:T(1024)S(1)} %reshape.110, bf16[1,512,2048]{2,1,0:T(8,128)(2,1)S(1)} %copy-done, bf16[1536,2048]{1,0:T(8,128)(2,1)} %bitcast.3, f32[1536,512]{1,0:T(8,128)} %fusion.5, bf16[1,2048,512]{2,1,0:T(8,128)(2,1)} %param.13), kind=kOutput, calls=%fused_computation.4 | convolution fusion | flops 6453460992 | bytes 19929088 | tf_op jit(solution)/shard_map/dot_general | solution.py:44
  221.6 3.8 all-to-all-start.2
  225.4 0.0 all-gather.3.cloned.1.call-start
  225.4 0.7 all-gather.3.cloned.1.call-update
  226.1 0.2 all-gather.5.cloned.1.call-start
  226.4 0.5 all-gather.5.cloned.1.call-update
  226.9 0.0 copy-done.3
  226.9 0.2 fusion.10
  227.2 85.8 %all-gather.3.cloned.1.call-done = bf16[2048,1024]{1,0:T(8,128)(2,1)} async-done(((bf16[512,1024]{1,0:T(8,128)(2,1)}), bf16[2048,1024]{1,0:T(8,128)(2,1)}) %all-gather.3.cloned.1.call-update) | async-done | bytes 4194320 | tf_op jit(solution)/shard_map/all_gather | solution.py:62
  313.0 2.9 fusion.27
  315.9 50.5 %all-to-all-done.2 = bf16[32,48,2048]{2,1,0:T(8,128)(2,1)} async-done(((bf16[32,48,2048]{2,1,0:T(8,128)(2,1)}), bf16[32,48,2048]{2,1,0:T(8,128)(2,1)}, u32[]{:S(2)}, u32[]{:S(2)}) %all-to-all-start.2) | async-done | bytes 6291488 | tf_op jit(solution)/shard_map/all_to_all | solution.py:48
  366.4 14.4 %gather_fusion.2 = bf16[1280,2048]{1,0:T(8,128)(2,1)} fusion(bf16[1536,2048]{1,0:T(8,128)(2,1)} %bitcast.8, s32[2048]{0:T(1024)S(1)} %pad_clamp_fusion), kind=kCustom, calls=%fused_computation.2 | custom fusion | bytes 10490880 | tf_op jit(solution)/shard_map/gather | solution.py:56
  380.8 9.6 %reshape.109 = bf16[128,10,2048]{2,1,0:T(8,128)(2,1)} reshape(bf16[1280,2048]{1,0:T(8,128)(2,1)} %gather_fusion.2) | data formatting | bytes 10485760 | tf_op jit(solution)/shard_map/reshape | solution.py:56
  390.3 20.5 %fusion.26 = (bf16[128,1,2048]{2,1,0:T(2,128)(2,1)}, bf16[128,1,2048]{2,1,0:T(2,128)(2,1)}, bf16[128,1,2048]{2,1,0:T(2,128)(2,1)}, bf16[128,1,2048]{2,1,0:T(2,12...) fusion(bf16[128,10,2048]{2,1,0:T(8,128)(2,1)} %reshape.109), kind=kLoop, calls=%fused_computation.50 | loop fusion | bytes 10485760 | tf_op jit(solution)/shard_map/slice | solution.py:59
  410.8 0.0 all-gather.5.cloned.1.call-done
  410.8 0.0 copy-start.1
  410.9 8.8 %fusion.2 = bf16[128,2048]{1,0:T(8,128)(2,1)} fusion(bf16[512,2048]{1,0:T(8,128)(2,1)} %all-gather.5.cloned.1.call-done, bf16[128,1,2048]{2,1,0:T(2,128)(2,1)} %get-tuple-element.16, bf16[128,1,2048]{2,1,0:T(2,128)(2,1)} %get-tuple-element.8, bf16[128,1,2048]{2,1,0:T(2,128)(2,1)} %get-tuple-element.9, bf16[128,1,2048]{2,1,0:T(2,128)(2,1)} %get-tuple-element.10, ...), kind=kOutput, calls=%fused_computation.10 | convolution fusion | flops 274595840 | bytes 8389120 | tf_op jit(solution)/shard_map/dot_general | solution.py:67
  419.6 0.0 copy-done.1
  (11 shorter events, 0.1 us)
Async XLA Ops:
  6.5 203.3 %copy-start = (bf16[1,512,2048]{2,1,0:T(8,128)(2,1)S(1)}, bf16[1,512,2048]{2,1,0:T(8,128)(2,1)}, u32[]{:S(2)}) copy-start(bf16[1,512,2048]{2,1,0:T(8,128)(2,1)} %param.14) | copy-start | bytes 6291460
  6.5 35.8 %copy-start.2 = (bf16[128,2048]{1,0:T(8,128)(2,1)S(1)}, bf16[128,2048]{1,0:T(8,128)(2,1)}, u32[]{:S(2)}) copy-start(bf16[128,2048]{1,0:T(8,128)(2,1)} %param.9) | copy-start | bytes 1572868
  35.0 20.4 %all-to-all-start.1 = ((bf16[32,1,48]{2,1,0:T(2,128)(2,1)}), bf16[32,1,48]{2,1,0:T(2,128)(2,1)S(1)}, u32[]{:S(2)}, u32[]{:S(2)}) async-start(bf16[32,1,48]{2,1,0:T(2,128)(2,1)} %all_to_all.16), calls=%async_computation.1 | async-start | bytes 32768 | tf_op jit(solution)/shard_map/all_to_all | solution.py:45
  55.4 146.0 %all-to-all-start = ((bf16[32,48,2048]{2,1,0:T(8,128)(2,1)}), bf16[32,48,2048]{2,1,0:T(8,128)(2,1)}, u32[]{:S(2)}, u32[]{:S(2)}) async-start(bf16[32,48,2048]{2,1,0:T(8,128)(2,1)} %broadcast_select_fusion), calls=%async_computation | async-start | bytes 12582912 | tf_op jit(solution)/shard_map/all_to_all | solution.py:38
  221.6 5.3 %copy-start.3 = (bf16[2048]{0:T(1024)(128)(2,1)S(1)}, bf16[2048]{0:T(1024)(128)(2,1)}, u32[]{:S(2)}) copy-start(bf16[2048]{0:T(1024)(128)(2,1)} %param.17) | copy-start | bytes 12292
  221.6 144.7 %all-to-all-start.2 = ((bf16[32,48,2048]{2,1,0:T(8,128)(2,1)}), bf16[32,48,2048]{2,1,0:T(8,128)(2,1)}, u32[]{:S(2)}, u32[]{:S(2)}) async-start(bf16[32,48,2048]{2,1,0:T(8,128)(2,1)} %bitcast.54), calls=%async_computation.2 | async-start | bytes 12582912 | tf_op jit(solution)/shard_map/all_to_all | solution.py:48
  225.4 87.6 %all-gather.3.cloned.1.call-start = ((), (), s32[]{:S(2)}) async-start(), calls=%async_computation.3 | async-start | bytes 5242880 | tf_op jit(solution)/shard_map/all_gather | solution.py:62
  226.1 184.7 %all-gather.5.cloned.1.call-start = ((), (), s32[]{:S(2)}) async-start(), calls=%async_computation.4 | async-start | bytes 2621440 | tf_op jit(solution)/shard_map/all_gather | solution.py:69
  410.8 8.8 %copy-start.1 = (bf16[1,512,2048]{2,1,0:T(8,128)(2,1)S(1)}, bf16[1,512,2048]{2,1,0:T(8,128)(2,1)}, u32[]{:S(2)}) copy-start(bf16[1,512,2048]{2,1,0:T(8,128)(2,1)} %param.14) | copy-start | bytes 6291460
Sparse Core Ops, SparseCore 0:
  227.8 85.1 all-gather.2
  314.5 19.5 all-gather.4
where the time goes:
time: 427 us; the launch traced here: 426 us
  waiting for transfers between devices  277 us (65%)
  local copies, waits for them, and re-layouts  70 us (16%)
  matrix products  32.2 us (8%)
  starting transfers between devices  17.3 us (4%)
  other arithmetic  16.1 us (4%)
  between operations  13.6 us (3%)
    all_to_all x1, waiting for transfers between devices, shards(): lax.all_to_all(outgoing, ('expert', 'dp'), split_axis=0, concat_axis=0, t...  140 us
    all_gather x1, waiting for transfers between devices, shards(): lax.all_gather(shared_gate_up, 'dp', axis=0, tiled=True)  85.8 us
    all_to_all x1, waiting for transfers between devices, shards(): lax.all_to_all(answer.astype(jnp.bfloat16).reshape(shape), ('expert', 'dp...  50.5 us
    slice x1, local copies, waits for them, and re-layouts, shards(): routed = routed + gathered[:, column].astype(jnp.float32)  20.5 us
    gather x1, local copies, waits for them, and re-layouts, shards(): gathered = returned[slot_index].reshape(tok_count, top_count, width)  14.4 us
    dot_general x1, matrix products, shards(): answer = jnp.dot(hidden, expert_down[0], preferred_element_type=jnp.float32)  11.7 us
    reshape x1, local copies, waits for them, and re-layouts, shards(): gathered = returned[slot_index].reshape(tok_count, top_count, width)  9.56 us
    gather x1, local copies, waits for them, and re-layouts, shards(): route_weight.reshape(-1)[picked]  9.46 us
  transfers between devices with their start and end apart: 5, of which 3 were waited for; matrix products, arithmetic and copies ran while one was open for 14% of the time, Pallas kernels for 0%

commit v1 on v0

--- a/solution.py
+++ b/solution.py
@@ -2,6 +2,144 @@
 import jax.numpy as jnp
 from jax import lax
 from jax.sharding import PartitionSpec as P
+
+BOTH = ("expert", "dp")
+RING = (0, 1, 3, 2)
+
+
+def moved(array, step):
+    pairs = []
+    for device in range(32):
+        z, y, x, core = device // 8, device // 4 % 2, device // 2 % 2, device % 2
+        z, y, x, core = step(z, y, x, core)
+        pairs.append((device, ((z * 2 + y) * 2 + x) * 2 + core))
+    return lax.ppermute(array, BOTH, pairs)
+
+
+def to_core(z, y, x, core):
+    return z, y, x, 1 - core
+
+
+def to_x(z, y, x, core):
+    return z, y, 1 - x, core
+
+
+def to_y(z, y, x, core):
+    return z, 1 - y, x, core
+
+
+def ring_on(z, y, x, core):
+    return RING[(RING.index(z) + 1) % 4], y, x, core
+
+
+def ring_back(z, y, x, core):
+    return RING[(RING.index(z) + 3) % 4], y, x, core
+
+
+def blocks(
+    tokens,
+    expert_ids,
+    route_weight,
+    expert_gate,
+    expert_up,
+    expert_down,
+    shared_gate_up,
+    shared_down,
+    shared_switch,
+):
+    bf16, f32 = jnp.bfloat16, jnp.float32
+    rows, width = tokens.shape
+    half = rows // 2
+    me = lax.axis_index(BOTH)
+    z, y, x, core = me // 8, me // 4 % 2, me // 2 % 2, me % 2
+    ring_place = jnp.array(RING)[z]
+
+    dense = jnp.sum(
+        jnp.where(
+            expert_ids.T[:, None, :] == jnp.arange(32, dtype=jnp.int32)[None, :, None],
+            route_weight.T[:, None, :].astype(f32),
+            0.0,
+        ),
+        axis=0,
+    ).astype(bf16)
+    pairs = jnp.broadcast_to(dense.reshape(16, 1, 2 * rows), (16, 2, 2 * rows)).reshape(32, 1, 2 * rows)
+    got = lax.all_to_all(pairs, BOTH, split_axis=0, concat_axis=0, tiled=True).reshape(32, 2 * rows)
+    sources = []
+    for back in range(4):
+        for dy in range(2):
+            for dx in range(2):
+                from_z = jnp.array(RING)[(ring_place + 4 - back) % 4]
+                sources.append(((from_z * 2 + (y + dy) % 2) * 2 + (x + dx) % 2) * 2 + core)
+    pick = (jnp.stack(sources)[:, None] == jnp.arange(32)[None, :]).astype(bf16)
+    slot_weight = jnp.dot(pick, got, preferred_element_type=f32)
+    slot_weight = slot_weight.reshape(4, 4, 2, rows).transpose(0, 2, 1, 3).reshape(4, 2, 4 * rows, 1)
+
+    mine = (expert_gate[0], expert_up[0], expert_down[0])
+    other = tuple(moved(part, to_core) for part in mine)
+    my_weight = jnp.where(core == 0, slot_weight[:, 0], slot_weight[:, 1])
+    other_weight = jnp.where(core == 0, slot_weight[:, 1], slot_weight[:, 0])
+
+    feature = shared_gate_up.shape[1] // 8
+    group = jnp.stack([shared_gate_up[:, q * feature : (q + 1) * feature] for q in range(8)])
+
+    def plane_slice(y_to, x_to):
+        q = y_to * 2 + x_to
+        gate_part = lax.dynamic_index_in_dim(group, q, 0, keepdims=False)
+        up_part = lax.dynamic_index_in_dim(group, 4 + q, 0, keepdims=False)
+        down_part = lax.dynamic_slice_in_dim(shared_down, q * feature, feature, 0)
+        return jnp.concatenate([gate_part, up_part], axis=1), down_part
+
+    own_up, own_down = plane_slice(y, x)
+    sent_up, sent_down = plane_slice(y, 1 - x)
+    far_up, far_down = moved(sent_up, to_x), moved(sent_down, to_x)
+    near_up2, near_down2 = moved(own_up, to_core), moved(own_down, to_core)
+    far_up2, far_down2 = moved(far_up, to_core), moved(far_down, to_core)
+    def by_k(own, near, far, far_near):
+        low = jnp.where(core == 0, jnp.stack([own, near]), jnp.stack([near, own]))
+        high = jnp.where(core == 0, jnp.stack([far, far_near]), jnp.stack([far_near, far]))
+        return jnp.where(x == 0, jnp.stack([low, high]), jnp.stack([high, low]))
+
+    shared_in = by_k(own_up, near_up2, far_up, far_up2).reshape(width, 2 * feature)
+    shared_out_rows = by_k(own_down, near_down2, far_down, far_down2)
+    shared_out_rows = shared_out_rows.transpose(2, 0, 1, 3).reshape(feature, width)
+
+    columns = [tokens]
+    for back in range(3):
+        columns.append(moved(columns[-1], ring_on))
+    partial = []
+    for back in range(4):
+        block = columns[back]
+        by_x, by_y = moved(block, to_x), moved(block, to_y)
+        corner_top = moved(by_y[:half], to_x)
+        corner_low = moved(by_x[half:], to_y)
+        stacked = jnp.concatenate([block, by_x, by_y, corner_top, corner_low], axis=0)
+        total = 0.0
+        for part, weight in ((mine, my_weight[back]), (other, other_weight[back])):
+            gate = jnp.dot(stacked, part[0], preferred_element_type=f32)
+            upper = jnp.dot(stacked, part[1], preferred_element_type=f32)
+            hidden = (jax.nn.silu(gate) * upper).astype(bf16)
+            total = total + jnp.dot(hidden, part[2], preferred_element_type=f32) * weight
+        if back == 0:
+            both = jnp.dot(stacked, shared_in, preferred_element_type=f32)
+            hidden = (jax.nn.silu(both[:, :feature]) * both[:, feature:]).astype(bf16)
+            switch = jax.nn.sigmoid(jnp.dot(stacked, shared_switch, preferred_element_type=f32))
+            total = total + switch[:, None] * jnp.dot(hidden, shared_out_rows, preferred_element_type=f32)
+        partial.append(total.astype(bf16).reshape(4, rows, width))
+
+    arriving = None
+    for back in (3, 2, 1, 0):
+        here, along_x, along_y, corner = partial[back]
+        top = moved(corner[:half], to_x).astype(f32)
+        low = moved(corner[half:], to_y).astype(f32)
+        along_y = jnp.concatenate([along_y[:half].astype(f32) + top, along_y[half:].astype(f32)]).astype(bf16)
+        along_x = jnp.concatenate([along_x[:half].astype(f32), along_x[half:].astype(f32) + low]).astype(bf16)
+        total = here.astype(f32) + moved(along_x, to_x).astype(f32) + moved(along_y, to_y).astype(f32)
+        if arriving is not None:
+            total = total + arriving.astype(f32)
+        total = total.astype(bf16)
+        if back:
+            arriving = moved(total, ring_back)
+    return total
 
 
 def shards(
@@ -86,4 +224,5 @@
         P(),
     )
     out_specs = P(("groups", "expert", "dp"), None)
-    return jax.shard_map(shards, mesh=mesh, in_specs=in_specs, out_specs=out_specs, check_vma=False)
+    part = blocks if (mesh.shape["expert"], mesh.shape["dp"]) == (8, 4) else shards
+    return jax.shard_map(part, mesh=mesh, in_specs=in_specs, out_specs=out_specs, check_vma=False)

time: 427 us -> 273 us (0.64)
  waiting for transfers between devices: 277 us -> 59.1 us
  matrix products: 32.2 us -> 97.2 us
  starting transfers between devices: 17.3 us -> 51 us
  local copies, waits for them, and re-layouts: 70 us -> 47.3 us
  between operations: 13.6 us -> 5.88 us
  other arithmetic: 16.1 us -> 10.9 us
    all_to_all x3 -> x1, waiting for transfers between devices: 190 us -> 0.01 us  [blocks(): lax.all_to_all(pairs, BOTH, split_axis=0, concat_axis=0, tiled=True)]
    all_gather x2 -> x0, waiting for transfers between devices: 85.8 us -> none  [the longest x1 85.8 us: shards(): lax.all_gather(shared_gate_up, 'dp', axis=0, tiled=True)]
    dot_general x5 -> x20, matrix products: 32.2 us -> 97.2 us  [the longest x8 60.7 us: blocks(): jnp.dot(hidden, part[2], preferred_element_type=f32) * weight]
    ppermute x0 -> x47, waiting for transfers between devices: none -> 59.1 us  [moved(): return lax.ppermute(array, BOTH, pairs)]
    ppermute x0 -> x47, starting transfers between devices: none -> 48.1 us  [moved(): return lax.ppermute(array, BOTH, pairs)]
    gather x3 -> x0, local copies, waits for them, and re-layouts: 31 us -> none  [the longest x1 14.4 us: shards(): gathered = returned[slot_index].reshape(tok_count, top_count, width)]
    unnamed x11 -> x60, local copies, waits for them, and re-layouts: 1.8 us -> 28.5 us
    all_to_all x3 -> x1, starting transfers between devices: 17 us -> 2.95 us  [blocks(): lax.all_to_all(pairs, BOTH, split_axis=0, concat_axis=0, tiled=True)]
  transfers between devices with their start and end apart: 5 -> 48, of which waited for: 3 -> 15; matrix products, arithmetic and copies ran while one was open for 14% -> 56% of each run, Pallas kernels for 0% -> 0%
where the time goes in v1:
time: 273 us; the launch traced here: 271 us
  matrix products  97.2 us (36%)
  waiting for transfers between devices  59.1 us (22%)
  starting transfers between devices  51 us (19%)
  local copies, waits for them, and re-layouts  47.3 us (17%)
  other arithmetic  10.9 us (4%)
  between operations  5.88 us (2%)
    dot_general x8, matrix products, blocks(): jnp.dot(hidden, part[2], preferred_element_type=f32) * weight  60.7 us
    ppermute x47, waiting for transfers between devices, moved(): return lax.ppermute(array, BOTH, pairs)  59.1 us
    ppermute x47, starting transfers between devices, moved(): return lax.ppermute(array, BOTH, pairs)  48.1 us
    dot_general x8, matrix products, blocks(): gate = jnp.dot(stacked, part[0], preferred_element_type=f32)  30.8 us
    unnamed x60, local copies, waits for them, and re-layouts  28.5 us
  transfers between devices with their start and end apart: 48, of which 15 were waited for; matrix products, arithmetic and copies ran while one was open for 56% of the time, Pallas kernels for 0%

profile of v1, /device:TPU:0, one launch (start us, length us, event | category | flops | bytes accessed | tf_op | source)
XLA Modules:
  0.0 271.4 jit_solution(9002964502997539457)
XLA Ops:
  0.0 3.0 %collective-permute-start.17 = (bf16[128,2048]{1,0:T(8,128)(2,1)}, bf16[128,2048]{1,0:T(8,128)(2,1)}, u32[]{:S(2)}, u32[]{:S(2)}) collective-permute-start(bf16[128,2048]{1,0:T(8,128)(2,1)} %param.26), channel_id=1, source_target_pairs={{0,8},{1,9},{2,10},{3,11},{4,12},{5,13},{6,14},{7,15},{8,24},{9,25... | collective-permute-start | bytes 1572872 | tf_op jit(solution)/shard_map/ppermute | solution.py:16
  9.4 3.0 %all-to-all-start = ((bf16[32,2,128]{2,1,0:T(2,128)(2,1)}), bf16[32,2,128]{2,1,0:T(2,128)(2,1)S(1)}, u32[]{:S(2)}, u32[]{:S(2)}) async-start(bf16[32,2,128]{2,1,0:T(2,128)(2,1)} %reshape.455), calls=%async_computation | async-start | bytes 32768 | tf_op jit(solution)/shard_map/all_to_all | solution.py:66
  14.2 1.8 collective-permute-start.11
  17.2 1.6 bitcast_dynamic-update-slice_fusion.7
  18.8 1.6 bitcast_dynamic-update-slice_fusion.6
  23.5 1.6 bitcast_dynamic-update-slice_fusion.3
  28.2 1.6 bitcast_dynamic-update-slice_fusion
  50.4 7.2 %collective-permute-done.8 = bf16[512,256]{1,0:T(8,128)(2,1)S(1)} collective-permute-done((bf16[512,256]{1,0:T(8,128)(2,1)}, bf16[512,256]{1,0:T(8,128)(2,1)S(1)}, u32[]{:S(2)}, u32[]{:S(2)}) %collective-permute-start.8) | collective-permute-done | bytes 262176 | tf_op jit(solution)/shard_map/ppermute | solution.py:16
  58.5 1.8 collective-permute-start.3
  60.3 1.9 constant_dynamic-update-slice_fusion.9
  64.1 2.3 collective-permute-done.2
  66.7 1.8 collective-permute-start.19
  68.6 3.8 %fusion.54 = f32[512,512]{1,0:T(8,128)} fusion(bf16[512,2048]{1,0:T(8,128)(2,1)S(1)} %constant_dynamic-update-slice_fusion, bf16[1,2048,512]{2,1,0:T(8,128)(2,1)} %param.29), kind=kOutput, calls=%fused_computation.121 | convolution fusion | flops 1073741824 | bytes 5242880 | tf_op jit(solution)/shard_map/dot_general | solution.py:118
  73.7 2.7 %fusion.13 = f32[512,2048]{1,0:T(8,128)} fusion(bf16[128,2048]{0,1:T(8,128)(2,1)S(1)} %bitcast.170, f32[512,256]{1,0:T(8,128)S(1)} %fusion.83), kind=kOutput, calls=%fused_computation.57 | convolution fusion | flops 268828672 | bytes 5242880 | tf_op jit(solution)/shard_map/dot_general | solution.py:126
  76.5 7.0 %fusion = f32[512,2048]{1,0:T(8,128)} fusion(f32[512,512]{1,0:T(8,128)} %fusion.54, bf16[1,512,2048]{2,1,0:T(8,128)(2,1)} %param.31, bf16[512,2048]{1,0:T(8,128)(2,1)S(1)} %constant_dynamic-update-slice_fusion, bf16[1,2048,512]{2,1,0:T(8,128)(2,1)} %param.30), kind=kOutput, calls=%fused_computation.18 | convolution fusion | flops 2149056512 | bytes 11534336 | tf_op jit(solution)/shard_map/dot_general | solution.py:121
  87.2 1.9 constant_dynamic-update-slice_fusion.14
  94.2 4.5 %fusion.52 = f32[512,512]{1,0:T(8,128)} fusion(bf16[512,2048]{1,0:T(8,128)(2,1)} %constant_dynamic-update-slice_fusion.5, bf16[1,2048,512]{2,1,0:T(8,128)(2,1)} %param.29), kind=kOutput, calls=%fused_computation.119 | convolution fusion | flops 1073741824 | bytes 5242880 | tf_op jit(solution)/shard_map/dot_general | solution.py:118
  98.7 7.7 %fusion.1 = f32[512,2048]{1,0:T(8,128)} fusion(f32[512,512]{1,0:T(8,128)} %fusion.52, bf16[1,512,2048]{2,1,0:T(8,128)(2,1)} %param.31, bf16[512,2048]{1,0:T(8,128)(2,1)} %constant_dynamic-update-slice_fusion.5, bf16[1,2048,512]{2,1,0:T(8,128)(2,1)} %param.30), kind=kOutput, calls=%fused_computation.19 | convolution fusion | flops 2149056512 | bytes 11534336 | tf_op jit(solution)/shard_map/dot_general | solution.py:121
  108.6 1.9 constant_dynamic-update-slice_fusion.19
  110.6 4.6 %collective-permute-done.29 = bf16[64,2048]{1,0:T(8,128)(2,1)S(1)} collective-permute-done((bf16[64,2048]{1,0:T(8,128)(2,1)S(1)}, bf16[64,2048]{1,0:T(8,128)(2,1)S(1)}, u32[]{:S(2)}, u32[]{:S(2)}) %collective-permute-start.29) | collective-permute-done | bytes 262176 | tf_op jit(solution)/shard_map/ppermute | solution.py:16
  118.7 3.8 %fusion.50 = f32[512,512]{1,0:T(8,128)} fusion(bf16[512,2048]{1,0:T(8,128)(2,1)S(1)} %constant_dynamic-update-slice_fusion.10, bf16[1,2048,512]{2,1,0:T(8,128)(2,1)} %param.29), kind=kOutput, calls=%fused_computation.117 | convolution fusion | flops 1073741824 | bytes 5242880 | tf_op jit(solution)/shard_map/dot_general | solution.py:118
  122.6 7.5 %fusion.2 = f32[512,2048]{1,0:T(8,128)} fusion(f32[512,512]{1,0:T(8,128)} %fusion.50, bf16[1,512,2048]{2,1,0:T(8,128)(2,1)} %param.31, bf16[512,2048]{1,0:T(8,128)(2,1)} %copy-done.10, bf16[1,2048,512]{2,1,0:T(8,128)(2,1)} %param.30), kind=kOutput, calls=%fused_computation.20 | convolution fusion | flops 2149056512 | bytes 11534336 | tf_op jit(solution)/shard_map/dot_general | solution.py:121
  133.6 4.4 %fusion.85 = f32[512,512]{1,0:T(8,128)} fusion(bf16[512,2048]{1,0:T(8,128)(2,1)} %copy-done.10, bf16[2048,512]{1,0:T(8,128)(2,1)} %collective-permute-done.4), kind=kOutput, calls=%fused_computation.148 | convolution fusion | flops 1073741824 | bytes 5242880 | tf_op jit(solution)/shard_map/dot_general | solution.py:118
  138.1 8.2 %add_convert_fusion.1 = bf16[512,2048]{1,0:T(8,128)(2,1)} fusion(f32[512,2048]{1,0:T(8,128)} %fusion.2, bf16[512,2048]{1,0:T(8,128)(2,1)} %collective-permute-done.6, f32[512]{0:T(512)S(1)} %bitcast.186, f32[512]{0:T(512)S(1)} %bitcast.185, f32[512,512]{1,0:T(8,128)} %fusion.85, bf16[512,2048]{1,0:T(8,128)(2,1)} %copy-done.10, ...), kind=kOutput, calls=%fused_computation.1 | convolution fusion | flops 2153250816 | bytes 13635584 | tf_op jit(solution)/shard_map/dot_general | solution.py:121
  146.3 2.3 fusion.68
  150.7 3.8 %fusion.84 = f32[512,512]{1,0:T(8,128)} fusion(bf16[512,2048]{1,0:T(8,128)(2,1)S(1)} %copy-done.8, bf16[2048,512]{1,0:T(8,128)(2,1)} %collective-permute-done.4), kind=kOutput, calls=%fused_computation.147 | convolution fusion | flops 1073741824 | bytes 5242880 | tf_op jit(solution)/shard_map/dot_general | solution.py:118
  154.6 8.1 %add_convert_fusion.2 = bf16[512,2048]{1,0:T(8,128)(2,1)} fusion(f32[512,2048]{1,0:T(8,128)} %fusion.1, bf16[512,2048]{1,0:T(8,128)(2,1)} %collective-permute-done.6, f32[512]{0:T(512)S(1)} %bitcast.184, f32[512]{0:T(512)S(1)} %bitcast.183, f32[512,512]{1,0:T(8,128)} %fusion.84, bf16[512,2048]{1,0:T(8,128)(2,1)} %constant_dynamic-update-slice_fusion.5, ...), kind=kOutput, calls=%fused_computation.2 | convolution fusion | flops 2153250816 | bytes 13635584 | tf_op jit(solution)/shard_map/dot_general | solution.py:121
  162.7 2.1 fusion.67
  166.2 4.0 %fusion.81 = f32[512,512]{1,0:T(8,128)} fusion(bf16[512,2048]{1,0:T(8,128)(2,1)S(1)} %constant_dynamic-update-slice_fusion, bf16[2048,512]{1,0:T(8,128)(2,1)} %collective-permute-done.4), kind=kOutput, calls=%fused_computation.144 | convolution fusion | flops 1073741824 | bytes 5242880 | tf_op jit(solution)/shard_map/dot_general | solution.py:118
  170.2 9.0 %add_convert_fusion.3 = bf16[512,2048]{1,0:T(8,128)(2,1)} fusion(f32[512,2048]{1,0:T(8,128)} %fusion.13, f32[512,2048]{1,0:T(8,128)} %fusion, bf16[512,2048]{1,0:T(8,128)(2,1)} %collective-permute-done.6, f32[512]{0:T(512)S(1)} %add_divide_fusion, f32[512]{0:T(512)S(1)} %bitcast.182, f32[512]{0:T(512)S(1)} %bitcast.181, f32[512,512]{1,0:T(8,128)} %fusion.81, ...), kind=kOutput, calls=%fused_computation.3 | convolution fusion | flops 2155347968 | bytes 17831936 | tf_op jit(solution)/shard_map/dot_general | solution.py:121
  180.9 1.7 constant_dynamic-update-slice_fusion.16
  182.6 1.7 constant_dynamic-update-slice_fusion.15
  184.2 3.6 %fusion.48 = f32[512,512]{1,0:T(8,128)S(1)} fusion(bf16[512,2048]{1,0:T(8,128)(2,1)} %constant_dynamic-update-slice_fusion.15, bf16[1,2048,512]{2,1,0:T(8,128)(2,1)} %param.29), kind=kOutput, calls=%fused_computation.115 | convolution fusion | flops 1073741824 | bytes 5242880 | tf_op jit(solution)/shard_map/dot_general | solution.py:118
  187.8 6.6 %fusion.3 = f32[512,2048]{1,0:T(8,128)} fusion(f32[512,512]{1,0:T(8,128)S(1)} %fusion.48, bf16[1,512,2048]{2,1,0:T(8,128)(2,1)} %param.31, bf16[512,2048]{1,0:T(8,128)(2,1)S(1)} %copy-done.7, bf16[1,2048,512]{2,1,0:T(8,128)(2,1)} %param.30), kind=kOutput, calls=%fused_computation.21 | convolution fusion | flops 2149056512 | bytes 11534336 | tf_op jit(solution)/shard_map/dot_general | solution.py:121
  194.5 2.8 %fusion.86 = f32[512,512]{1,0:T(8,128)S(1)} fusion(bf16[512,2048]{1,0:T(8,128)(2,1)S(1)} %copy-done.7, bf16[2048,512]{1,0:T(8,128)(2,1)} %collective-permute-done.4), kind=kOutput, calls=%fused_computation.149 | convolution fusion | flops 1073741824 | bytes 5242880 | tf_op jit(solution)/shard_map/dot_general | solution.py:118
  197.3 6.5 %add_convert_fusion = bf16[512,2048]{1,0:T(8,128)(2,1)S(1)} fusion(f32[512,2048]{1,0:T(8,128)} %fusion.3, bf16[512,2048]{1,0:T(8,128)(2,1)} %collective-permute-done.6, f32[512]{0:T(512)S(1)} %bitcast.180, f32[512]{0:T(512)S(1)} %bitcast.179, f32[512,512]{1,0:T(8,128)S(1)} %fusion.86, bf16[512,2048]{1,0:T(8,128)(2,1)} %constant_dynamic-update-slice_fusion.15, ...), kind=kOutput, calls=%fused_computation | convolution fusion | flops 2153250816 | bytes 13635584 | tf_op jit(solution)/shard_map/dot_general | solution.py:121
  205.8 5.0 %collective-permute-done.40 = bf16[64,2048]{1,0:T(8,128)(2,1)S(1)} collective-permute-done((bf16[64,2048]{1,0:T(8,128)(2,1)S(1)}, bf16[64,2048]{1,0:T(8,128)(2,1)S(1)}, u32[]{:S(2)}, u32[]{:S(2)}) %collective-permute-start.40) | collective-permute-done | bytes 262176 | tf_op jit(solution)/shard_map/ppermute | solution.py:16
  212.4 2.4 collective-permute-start.13
  217.7 9.6 %collective-permute-done.43 = bf16[128,2048]{1,0:T(8,128)(2,1)S(1)} collective-permute-done((bf16[128,2048]{1,0:T(8,128)(2,1)S(1)}, bf16[128,2048]{1,0:T(8,128)(2,1)S(1)}, u32[]{:S(2)}, u32[]{:S(2)}) %collective-permute-start.43) | collective-permute-done | bytes 524320 | tf_op jit(solution)/shard_map/ppermute | solution.py:16
  228.2 3.1 %collective-permute-done.41 = bf16[128,2048]{1,0:T(8,128)(2,1)S(1)} collective-permute-done((bf16[128,2048]{1,0:T(8,128)(2,1)S(1)}, bf16[128,2048]{1,0:T(8,128)(2,1)S(1)}, u32[]{:S(2)}, u32[]{:S(2)}) %collective-permute-start.41) | collective-permute-done | bytes 524320 | tf_op jit(solution)/shard_map/ppermute | solution.py:16
  232.9 2.8 %collective-permute-start.44 = (bf16[128,2048]{1,0:T(8,128)(2,1)S(1)}, bf16[128,2048]{1,0:T(8,128)(2,1)S(1)}, u32[]{:S(2)}, u32[]{:S(2)}) collective-permute-start(bf16[128,2048]{1,0:T(8,128)(2,1)S(1)} %add_convert_fusion.7), channel_id=1, source_target_pairs={{0,16},{1,17},{2,18},{3,19},{4,20},{5,21},{6,22},{7,23},{8,0},{9,1... | collective-permute-start | bytes 1572872 | tf_op jit(solution)/shard_map/ppermute | solution.py:16
  236.9 8.2 %collective-permute-done.34 = bf16[128,2048]{1,0:T(8,128)(2,1)S(1)} collective-permute-done((bf16[128,2048]{1,0:T(8,128)(2,1)S(1)}, bf16[128,2048]{1,0:T(8,128)(2,1)S(1)}, u32[]{:S(2)}, u32[]{:S(2)}) %collective-permute-start.34) | collective-permute-done | bytes 524320 | tf_op jit(solution)/shard_map/ppermute | solution.py:16
  246.3 3.4 %collective-permute-start.45 = (bf16[128,2048]{1,0:T(8,128)(2,1)S(1)}, bf16[128,2048]{1,0:T(8,128)(2,1)S(1)}, u32[]{:S(2)}, u32[]{:S(2)}) collective-permute-start(bf16[128,2048]{1,0:T(8,128)(2,1)S(1)} %add_convert_fusion.6), channel_id=1, source_target_pairs={{0,16},{1,17},{2,18},{3,19},{4,20},{5,21},{6,22},{7,23},{8,0},{9,1... | collective-permute-start | bytes 1572872 | tf_op jit(solution)/shard_map/ppermute | solution.py:16
  250.8 8.7 %collective-permute-done.25 = bf16[128,2048]{1,0:T(8,128)(2,1)S(1)} collective-permute-done((bf16[128,2048]{1,0:T(8,128)(2,1)S(1)}, bf16[128,2048]{1,0:T(8,128)(2,1)S(1)}, u32[]{:S(2)}, u32[]{:S(2)}) %collective-permute-start.25) | collective-permute-done | bytes 524320 | tf_op jit(solution)/shard_map/ppermute | solution.py:16
  260.6 1.9 collective-permute-start.46
  262.5 2.5 collective-permute-done.16
  265.1 2.2 collective-permute-done.14
  267.2 3.1 %collective-permute-done.46 = bf16[128,2048]{1,0:T(8,128)(2,1)S(1)} collective-permute-done((bf16[128,2048]{1,0:T(8,128)(2,1)S(1)}, bf16[128,2048]{1,0:T(8,128)(2,1)S(1)}, u32[]{:S(2)}, u32[]{:S(2)}) %collective-permute-start.46) | collective-permute-done | bytes 524320 | tf_op jit(solution)/shard_map/ppermute | solution.py:16
  (186 shorter events, 73.2 us)
Async XLA Ops:
  0.0 58.5 %collective-permute-start.17 = (bf16[128,2048]{1,0:T(8,128)(2,1)}, bf16[128,2048]{1,0:T(8,128)(2,1)}, u32[]{:S(2)}, u32[]{:S(2)}) collective-permute-start(bf16[128,2048]{1,0:T(8,128)(2,1)} %param.26), channel_id=1, source_target_pairs={{0,8},{1,9},{2,10},{3,11},{4,12},{5,13},{6,14},{7,15},{8,24},{9,25... | collective-permute-start | bytes 1572872 | tf_op jit(solution)/shard_map/ppermute | solution.py:16
  3.0 55.1 %collective-permute-start = (bf16[128,2048]{1,0:T(8,128)(2,1)}, bf16[128,2048]{1,0:T(8,128)(2,1)S(1)}, u32[]{:S(2)}, u32[]{:S(2)}) collective-permute-start(bf16[128,2048]{1,0:T(8,128)(2,1)} %param.26), channel_id=1, source_target_pairs={{0,2},{1,3},{2,0},{3,1},{4,6},{5,7},{6,4},{7,5},{8,10},{9,11},{10,... | collective-permute-start | bytes 1572872 | tf_op jit(solution)/shard_map/ppermute | solution.py:16
  4.5 53.1 %collective-permute-start.1 = (bf16[128,2048]{1,0:T(8,128)(2,1)}, bf16[128,2048]{1,0:T(8,128)(2,1)S(1)}, u32[]{:S(2)}, u32[]{:S(2)}) collective-permute-start(bf16[128,2048]{1,0:T(8,128)(2,1)} %param.26), channel_id=1, source_target_pairs={{0,4},{1,5},{2,6},{3,7},{4,0},{5,1},{6,2},{7,3},{8,12},{9,13},{10,... | collective-permute-start | bytes 1572872 | tf_op jit(solution)/shard_map/ppermute | solution.py:16
  9.4 34.1 %all-to-all-start = ((bf16[32,2,128]{2,1,0:T(2,128)(2,1)}), bf16[32,2,128]{2,1,0:T(2,128)(2,1)S(1)}, u32[]{:S(2)}, u32[]{:S(2)}) async-start(bf16[32,2,128]{2,1,0:T(2,128)(2,1)} %reshape.455), calls=%async_computation | async-start | bytes 32768 | tf_op jit(solution)/shard_map/all_to_all | solution.py:66
  14.2 32.2 %collective-permute-start.11 = (bf16[128,512]{0,1:T(8,128)(2,1)}, bf16[128,512]{0,1:T(8,128)(2,1)}, u32[]{:S(2)}, u32[]{:S(2)}) collective-permute-start(bf16[128,512]{0,1:T(8,128)(2,1)} %copy.44), channel_id=1, source_target_pairs={{0,2},{1,3},{2,0},{3,1},{4,6},{5,7},{6,4},{7,5},{8,10},{9,11},{10,... | collective-permute-start | bytes 393224 | tf_op jit(solution)/shard_map/ppermute | solution.py:16
  16.1 30.9 %collective-permute-start.10 = (bf16[128,512]{0,1:T(8,128)(2,1)S(1)}, bf16[128,512]{0,1:T(8,128)(2,1)}, u32[]{:S(2)}, u32[]{:S(2)}) collective-permute-start(bf16[128,512]{0,1:T(8,128)(2,1)S(1)} %copy.43), channel_id=1, source_target_pairs={{0,1},{1,0},{2,3},{3,2},{4,5},{5,4},{6,7},{7,6},{8,9},{9,8},{10,11... | collective-permute-start | bytes 393224 | tf_op jit(solution)/shard_map/ppermute | solution.py:16
  46.4 3.6 %collective-permute-start.7 = (bf16[512,256]{1,0:T(8,128)(2,1)}, bf16[512,256]{1,0:T(8,128)(2,1)S(1)}, u32[]{:S(2)}, u32[]{:S(2)}) collective-permute-start(bf16[512,256]{1,0:T(8,128)(2,1)} %get-tuple-element.36), channel_id=1, source_target_pairs={{0,1},{1,0},{2,3},{3,2},{4,5},{5,4},{6,7},{7,6},{8,9},{9,8},{10,11... | collective-permute-start | bytes 786440 | tf_op jit(solution)/shard_map/ppermute | solution.py:16
  46.9 1.7 collective-permute-start.12
  48.7 8.9 %collective-permute-start.8 = (bf16[512,256]{1,0:T(8,128)(2,1)}, bf16[512,256]{1,0:T(8,128)(2,1)S(1)}, u32[]{:S(2)}, u32[]{:S(2)}) collective-permute-start(bf16[512,256]{1,0:T(8,128)(2,1)} %pad_maximum_fusion.9), channel_id=1, source_target_pairs={{0,2},{1,3},{2,0},{3,1},{4,6},{5,7},{6,4},{7,5},{8,10},{9,11},{10,... | collective-permute-start | bytes 786440 | tf_op jit(solution)/shard_map/ppermute | solution.py:16
  50.0 88.0 %collective-permute-start.6 = (bf16[512,2048]{1,0:T(8,128)(2,1)}, bf16[512,2048]{1,0:T(8,128)(2,1)}, u32[]{:S(2)}, u32[]{:S(2)}) collective-permute-start(bf16[512,2048]{1,0:T(8,128)(2,1)} %bitcast.187), channel_id=1, source_target_pairs={{0,1},{1,0},{2,3},{3,2},{4,5},{5,4},{6,7},{7,6},{8,9},{9,8},{10,11... | collective-permute-start | bytes 6291464 | tf_op jit(solution)/shard_map/ppermute | solution.py:16
  57.6 76.0 %collective-permute-start.4 = (bf16[2048,512]{1,0:T(8,128)(2,1)}, bf16[2048,512]{1,0:T(8,128)(2,1)}, u32[]{:S(2)}, u32[]{:S(2)}) collective-permute-start(bf16[2048,512]{1,0:T(8,128)(2,1)} %bitcast), channel_id=1, source_target_pairs={{0,1},{1,0},{2,3},{3,2},{4,5},{5,4},{6,7},{7,6},{8,9},{9,8},{10,11... | collective-permute-start | bytes 6291464 | tf_op jit(solution)/shard_map/ppermute | solution.py:16
  57.6 4.7 %collective-permute-start.9 = (bf16[512,256]{1,0:T(8,128)(2,1)S(1)}, bf16[512,256]{1,0:T(8,128)(2,1)S(1)}, u32[]{:S(2)}, u32[]{:S(2)}) collective-permute-start(bf16[512,256]{1,0:T(8,128)(2,1)S(1)} %collective-permute-done.8), channel_id=1, source_target_pairs={{0,1},{1,0},{2,3},{3,2},{4,5},{5,4},{6,7},{7,6},{8,9},{9,8},{10,11... | collective-permute-start | bytes 786440 | tf_op jit(solution)/shard_map/ppermute | solution.py:16
  58.1 8.3 %collective-permute-start.2 = (bf16[64,2048]{1,0:T(8,128)(2,1)S(1)}, bf16[64,2048]{1,0:T(8,128)(2,1)S(1)}, u32[]{:S(2)}, u32[]{:S(2)}) collective-permute-start(bf16[64,2048]{1,0:T(8,128)(2,1)S(1)} %slice.270), channel_id=1, source_target_pairs={{0,2},{1,3},{2,0},{3,1},{4,6},{5,7},{6,4},{7,5},{8,10},{9,11},{10,... | collective-permute-start | bytes 786440 | tf_op jit(solution)/shard_map/ppermute | solution.py:16
  58.5 8.2 %collective-permute-start.3 = (bf16[64,2048]{1,0:T(8,128)(2,1)S(1)}, bf16[64,2048]{1,0:T(8,128)(2,1)S(1)}, u32[]{:S(2)}, u32[]{:S(2)}) collective-permute-start(bf16[64,2048]{1,0:T(8,128)(2,1)S(1)} %slice.271), channel_id=1, source_target_pairs={{0,4},{1,5},{2,6},{3,7},{4,0},{5,1},{6,2},{7,3},{8,12},{9,13},{10,... | collective-permute-start | bytes 786440 | tf_op jit(solution)/shard_map/ppermute | solution.py:16
  62.3 23.4 %collective-permute-start.26 = (bf16[128,2048]{1,0:T(8,128)(2,1)}, bf16[128,2048]{1,0:T(8,128)(2,1)}, u32[]{:S(2)}, u32[]{:S(2)}) collective-permute-start(bf16[128,2048]{1,0:T(8,128)(2,1)} %collective-permute-done.17), channel_id=1, source_target_pairs={{0,8},{1,9},{2,10},{3,11},{4,12},{5,13},{6,14},{7,15},{8,24},{9,25... | collective-permute-start | bytes 1572872 | tf_op jit(solution)/shard_map/ppermute | solution.py:16
  66.4 18.6 %collective-permute-start.18 = (bf16[128,2048]{1,0:T(8,128)(2,1)}, bf16[128,2048]{1,0:T(8,128)(2,1)S(1)}, u32[]{:S(2)}, u32[]{:S(2)}) collective-permute-start(bf16[128,2048]{1,0:T(8,128)(2,1)} %collective-permute-done.17), channel_id=1, source_target_pairs={{0,2},{1,3},{2,0},{3,1},{4,6},{5,7},{6,4},{7,5},{8,10},{9,11},{10,... | collective-permute-start | bytes 1572872 | tf_op jit(solution)/shard_map/ppermute | solution.py:16
  66.7 16.8 %collective-permute-start.19 = (bf16[128,2048]{1,0:T(8,128)(2,1)}, bf16[128,2048]{1,0:T(8,128)(2,1)S(1)}, u32[]{:S(2)}, u32[]{:S(2)}) collective-permute-start(bf16[128,2048]{1,0:T(8,128)(2,1)} %collective-permute-done.17), channel_id=1, source_target_pairs={{0,4},{1,5},{2,6},{3,7},{4,0},{5,1},{6,2},{7,3},{8,12},{9,13},{10,... | collective-permute-start | bytes 1572872 | tf_op jit(solution)/shard_map/ppermute | solution.py:16
  83.5 7.2 %collective-permute-start.20 = (bf16[64,2048]{1,0:T(8,128)(2,1)S(1)}, bf16[64,2048]{1,0:T(8,128)(2,1)S(1)}, u32[]{:S(2)}, u32[]{:S(2)}) collective-permute-start(bf16[64,2048]{1,0:T(8,128)(2,1)S(1)} %slice.284), channel_id=1, source_target_pairs={{0,2},{1,3},{2,0},{3,1},{4,6},{5,7},{6,4},{7,5},{8,10},{9,11},{10,... | collective-permute-start | bytes 786440 | tf_op jit(solution)/shard_map/ppermute | solution.py:16
  85.1 7.5 %collective-permute-start.21 = (bf16[64,2048]{1,0:T(8,128)(2,1)S(1)}, bf16[64,2048]{1,0:T(8,128)(2,1)S(1)}, u32[]{:S(2)}, u32[]{:S(2)}) collective-permute-start(bf16[64,2048]{1,0:T(8,128)(2,1)S(1)} %slice.285), channel_id=1, source_target_pairs={{0,4},{1,5},{2,6},{3,7},{4,0},{5,1},{6,2},{7,3},{8,12},{9,13},{10,... | collective-permute-start | bytes 786440 | tf_op jit(solution)/shard_map/ppermute | solution.py:16
  85.7 22.3 %collective-permute-start.35 = (bf16[128,2048]{1,0:T(8,128)(2,1)}, bf16[128,2048]{1,0:T(8,128)(2,1)}, u32[]{:S(2)}, u32[]{:S(2)}) collective-permute-start(bf16[128,2048]{1,0:T(8,128)(2,1)} %collective-permute-done.26), channel_id=1, source_target_pairs={{0,8},{1,9},{2,10},{3,11},{4,12},{5,13},{6,14},{7,15},{8,24},{9,25... | collective-permute-start | bytes 1572872 | tf_op jit(solution)/shard_map/ppermute | solution.py:16
  90.7 15.7 %collective-permute-start.27 = (bf16[128,2048]{1,0:T(8,128)(2,1)}, bf16[128,2048]{1,0:T(8,128)(2,1)S(1)}, u32[]{:S(2)}, u32[]{:S(2)}) collective-permute-start(bf16[128,2048]{1,0:T(8,128)(2,1)} %collective-permute-done.26), channel_id=1, source_target_pairs={{0,2},{1,3},{2,0},{3,1},{4,6},{5,7},{6,4},{7,5},{8,10},{9,11},{10,... | collective-permute-start | bytes 1572872 | tf_op jit(solution)/shard_map/ppermute | solution.py:16
  92.6 13.8 %collective-permute-start.28 = (bf16[128,2048]{1,0:T(8,128)(2,1)}, bf16[128,2048]{1,0:T(8,128)(2,1)S(1)}, u32[]{:S(2)}, u32[]{:S(2)}) collective-permute-start(bf16[128,2048]{1,0:T(8,128)(2,1)} %collective-permute-done.26), channel_id=1, source_target_pairs={{0,4},{1,5},{2,6},{3,7},{4,0},{5,1},{6,2},{7,3},{8,12},{9,13},{10,... | collective-permute-start | bytes 1572872 | tf_op jit(solution)/shard_map/ppermute | solution.py:16
  106.3 31.7 %collective-permute-start.5 = (bf16[2048,512]{1,0:T(8,128)(2,1)}, bf16[2048,512]{1,0:T(8,128)(2,1)}, u32[]{:S(2)}, u32[]{:S(2)}) collective-permute-start(bf16[2048,512]{1,0:T(8,128)(2,1)} %bitcast.188), channel_id=1, source_target_pairs={{0,1},{1,0},{2,3},{3,2},{4,5},{5,4},{6,7},{7,6},{8,9},{9,8},{10,11... | collective-permute-start | bytes 6291464 | tf_op jit(solution)/shard_map/ppermute | solution.py:16
  106.4 8.8 %collective-permute-start.29 = (bf16[64,2048]{1,0:T(8,128)(2,1)S(1)}, bf16[64,2048]{1,0:T(8,128)(2,1)S(1)}, u32[]{:S(2)}, u32[]{:S(2)}) collective-permute-start(bf16[64,2048]{1,0:T(8,128)(2,1)S(1)} %slice.294), channel_id=1, source_target_pairs={{0,2},{1,3},{2,0},{3,1},{4,6},{5,7},{6,4},{7,5},{8,10},{9,11},{10,... | collective-permute-start | bytes 786440 | tf_op jit(solution)/shard_map/ppermute | solution.py:16
  108.0 8.7 %collective-permute-start.30 = (bf16[64,2048]{1,0:T(8,128)(2,1)S(1)}, bf16[64,2048]{1,0:T(8,128)(2,1)S(1)}, u32[]{:S(2)}, u32[]{:S(2)}) collective-permute-start(bf16[64,2048]{1,0:T(8,128)(2,1)S(1)} %slice.295), channel_id=1, source_target_pairs={{0,4},{1,5},{2,6},{3,7},{4,0},{5,1},{6,2},{7,3},{8,12},{9,13},{10,... | collective-permute-start | bytes 786440 | tf_op jit(solution)/shard_map/ppermute | solution.py:16
  115.2 16.8 %collective-permute-start.36 = (bf16[128,2048]{1,0:T(8,128)(2,1)}, bf16[128,2048]{1,0:T(8,128)(2,1)S(1)}, u32[]{:S(2)}, u32[]{:S(2)}) collective-permute-start(bf16[128,2048]{1,0:T(8,128)(2,1)} %collective-permute-done.35), channel_id=1, source_target_pairs={{0,2},{1,3},{2,0},{3,1},{4,6},{5,7},{6,4},{7,5},{8,10},{9,11},{10,... | collective-permute-start | bytes 1572872 | tf_op jit(solution)/shard_map/ppermute | solution.py:16
  116.7 13.5 %collective-permute-start.37 = (bf16[128,2048]{1,0:T(8,128)(2,1)}, bf16[128,2048]{1,0:T(8,128)(2,1)S(1)}, u32[]{:S(2)}, u32[]{:S(2)}) collective-permute-start(bf16[128,2048]{1,0:T(8,128)(2,1)} %collective-permute-done.35), channel_id=1, source_target_pairs={{0,4},{1,5},{2,6},{3,7},{4,0},{5,1},{6,2},{7,3},{8,12},{9,13},{10,... | collective-permute-start | bytes 1572872 | tf_op jit(solution)/shard_map/ppermute | solution.py:16
  130.9 50.0 %collective-permute-start.38 = (bf16[64,2048]{1,0:T(8,128)(2,1)}, bf16[64,2048]{1,0:T(8,128)(2,1)}, u32[]{:S(2)}, u32[]{:S(2)}) collective-permute-start(bf16[64,2048]{1,0:T(8,128)(2,1)} %slice.304), channel_id=1, source_target_pairs={{0,2},{1,3},{2,0},{3,1},{4,6},{5,7},{6,4},{7,5},{8,10},{9,11},{10,... | collective-permute-start | bytes 786440 | tf_op jit(solution)/shard_map/ppermute | solution.py:16
  132.7 49.9 %collective-permute-start.39 = (bf16[64,2048]{1,0:T(8,128)(2,1)}, bf16[64,2048]{1,0:T(8,128)(2,1)}, u32[]{:S(2)}, u32[]{:S(2)}) collective-permute-start(bf16[64,2048]{1,0:T(8,128)(2,1)} %slice.305), channel_id=1, source_target_pairs={{0,4},{1,5},{2,6},{3,7},{4,0},{5,1},{6,2},{7,3},{8,12},{9,13},{10,... | collective-permute-start | bytes 786440 | tf_op jit(solution)/shard_map/ppermute | solution.py:16
  148.6 66.4 %collective-permute-start.31 = (bf16[64,2048]{1,0:T(8,128)(2,1)}, bf16[64,2048]{1,0:T(8,128)(2,1)}, u32[]{:S(2)}, u32[]{:S(2)}) collective-permute-start(bf16[64,2048]{1,0:T(8,128)(2,1)} %get-tuple-element.20), channel_id=1, source_target_pairs={{0,4},{1,5},{2,6},{3,7},{4,0},{5,1},{6,2},{7,3},{8,12},{9,13},{10,... | collective-permute-start | bytes 786440 | tf_op jit(solution)/shard_map/ppermute | solution.py:16
  149.8 65.4 %collective-permute-start.33 = (bf16[64,2048]{1,0:T(8,128)(2,1)}, bf16[64,2048]{1,0:T(8,128)(2,1)}, u32[]{:S(2)}, u32[]{:S(2)}) collective-permute-start(bf16[64,2048]{1,0:T(8,128)(2,1)} %get-tuple-element.19), channel_id=1, source_target_pairs={{0,2},{1,3},{2,0},{3,1},{4,6},{5,7},{6,4},{7,5},{8,10},{9,11},{10,... | collective-permute-start | bytes 786440 | tf_op jit(solution)/shard_map/ppermute | solution.py:16
  164.8 67.5 %collective-permute-start.22 = (bf16[64,2048]{1,0:T(8,128)(2,1)}, bf16[64,2048]{1,0:T(8,128)(2,1)}, u32[]{:S(2)}, u32[]{:S(2)}) collective-permute-start(bf16[64,2048]{1,0:T(8,128)(2,1)} %get-tuple-element.14), channel_id=1, source_target_pairs={{0,4},{1,5},{2,6},{3,7},{4,0},{5,1},{6,2},{7,3},{8,12},{9,13},{10,... | collective-permute-start | bytes 786440 | tf_op jit(solution)/shard_map/ppermute | solution.py:16
  204.0 6.9 %collective-permute-start.40 = (bf16[64,2048]{1,0:T(8,128)(2,1)S(1)}, bf16[64,2048]{1,0:T(8,128)(2,1)S(1)}, u32[]{:S(2)}, u32[]{:S(2)}) collective-permute-start(bf16[64,2048]{1,0:T(8,128)(2,1)S(1)} %get-tuple-element.26), channel_id=1, source_target_pairs={{0,4},{1,5},{2,6},{3,7},{4,0},{5,1},{6,2},{7,3},{8,12},{9,13},{10,... | collective-permute-start | bytes 786440 | tf_op jit(solution)/shard_map/ppermute | solution.py:16
  204.7 7.7 %collective-permute-start.42 = (bf16[64,2048]{1,0:T(8,128)(2,1)S(1)}, bf16[64,2048]{1,0:T(8,128)(2,1)S(1)}, u32[]{:S(2)}, u32[]{:S(2)}) collective-permute-start(bf16[64,2048]{1,0:T(8,128)(2,1)S(1)} %get-tuple-element.25), channel_id=1, source_target_pairs={{0,2},{1,3},{2,0},{3,1},{4,6},{5,7},{6,4},{7,5},{8,10},{9,11},{10,... | collective-permute-start | bytes 786440 | tf_op jit(solution)/shard_map/ppermute | solution.py:16
  210.9 22.1 %collective-permute-start.24 = (bf16[64,2048]{1,0:T(8,128)(2,1)S(1)}, bf16[64,2048]{1,0:T(8,128)(2,1)S(1)}, u32[]{:S(2)}, u32[]{:S(2)}) collective-permute-start(bf16[64,2048]{1,0:T(8,128)(2,1)S(1)} %copy-done.6), channel_id=1, source_target_pairs={{0,2},{1,3},{2,0},{3,1},{4,6},{5,7},{6,4},{7,5},{8,10},{9,11},{10,... | collective-permute-start | bytes 786440 | tf_op jit(solution)/shard_map/ppermute | solution.py:16
  212.4 37.3 %collective-permute-start.13 = (bf16[64,2048]{1,0:T(8,128)(2,1)S(1)}, bf16[64,2048]{1,0:T(8,128)(2,1)S(1)}, u32[]{:S(2)}, u32[]{:S(2)}) collective-permute-start(bf16[64,2048]{1,0:T(8,128)(2,1)S(1)} %get-tuple-element.8), channel_id=1, source_target_pairs={{0,4},{1,5},{2,6},{3,7},{4,0},{5,1},{6,2},{7,3},{8,12},{9,13},{10,... | collective-permute-start | bytes 786440 | tf_op jit(solution)/shard_map/ppermute | solution.py:16
  215.1 12.2 %collective-permute-start.43 = (bf16[128,2048]{1,0:T(8,128)(2,1)S(1)}, bf16[128,2048]{1,0:T(8,128)(2,1)S(1)}, u32[]{:S(2)}, u32[]{:S(2)}) collective-permute-start(bf16[128,2048]{1,0:T(8,128)(2,1)S(1)} %pad_maximum_fusion.7), channel_id=1, source_target_pairs={{0,4},{1,5},{2,6},{3,7},{4,0},{5,1},{6,2},{7,3},{8,12},{9,13},{10,... | collective-permute-start | bytes 1572872 | tf_op jit(solution)/shard_map/ppermute | solution.py:16
  215.2 16.2 %collective-permute-start.41 = (bf16[128,2048]{1,0:T(8,128)(2,1)S(1)}, bf16[128,2048]{1,0:T(8,128)(2,1)S(1)}, u32[]{:S(2)}, u32[]{:S(2)}) collective-permute-start(bf16[128,2048]{1,0:T(8,128)(2,1)S(1)} %pad_maximum_fusion.6), channel_id=1, source_target_pairs={{0,2},{1,3},{2,0},{3,1},{4,6},{5,7},{6,4},{7,5},{8,10},{9,11},{10,... | collective-permute-start | bytes 1572872 | tf_op jit(solution)/shard_map/ppermute | solution.py:16
  227.3 22.4 %collective-permute-start.15 = (bf16[64,2048]{1,0:T(8,128)(2,1)S(1)}, bf16[64,2048]{1,0:T(8,128)(2,1)S(1)}, u32[]{:S(2)}, u32[]{:S(2)}) collective-permute-start(bf16[64,2048]{1,0:T(8,128)(2,1)S(1)} %get-tuple-element.7), channel_id=1, source_target_pairs={{0,2},{1,3},{2,0},{3,1},{4,6},{5,7},{6,4},{7,5},{8,10},{9,11},{10,... | collective-permute-start | bytes 786440 | tf_op jit(solution)/shard_map/ppermute | solution.py:16
  231.3 13.8 %collective-permute-start.34 = (bf16[128,2048]{1,0:T(8,128)(2,1)S(1)}, bf16[128,2048]{1,0:T(8,128)(2,1)S(1)}, u32[]{:S(2)}, u32[]{:S(2)}) collective-permute-start(bf16[128,2048]{1,0:T(8,128)(2,1)S(1)} %pad_maximum_fusion.5), channel_id=1, source_target_pairs={{0,4},{1,5},{2,6},{3,7},{4,0},{5,1},{6,2},{7,3},{8,12},{9,13},{10,... | collective-permute-start | bytes 1572872 | tf_op jit(solution)/shard_map/ppermute | solution.py:16
  232.3 13.1 %collective-permute-start.32 = (bf16[128,2048]{1,0:T(8,128)(2,1)S(1)}, bf16[128,2048]{1,0:T(8,128)(2,1)S(1)}, u32[]{:S(2)}, u32[]{:S(2)}) collective-permute-start(bf16[128,2048]{1,0:T(8,128)(2,1)S(1)} %pad_maximum_fusion.4), channel_id=1, source_target_pairs={{0,2},{1,3},{2,0},{3,1},{4,6},{5,7},{6,4},{7,5},{8,10},{9,11},{10,... | collective-permute-start | bytes 1572872 | tf_op jit(solution)/shard_map/ppermute | solution.py:16
  232.9 13.0 %collective-permute-start.44 = (bf16[128,2048]{1,0:T(8,128)(2,1)S(1)}, bf16[128,2048]{1,0:T(8,128)(2,1)S(1)}, u32[]{:S(2)}, u32[]{:S(2)}) collective-permute-start(bf16[128,2048]{1,0:T(8,128)(2,1)S(1)} %add_convert_fusion.7), channel_id=1, source_target_pairs={{0,16},{1,17},{2,18},{3,19},{4,20},{5,21},{6,22},{7,23},{8,0},{9,1... | collective-permute-start | bytes 1572872 | tf_op jit(solution)/shard_map/ppermute | solution.py:16
  245.2 14.3 %collective-permute-start.25 = (bf16[128,2048]{1,0:T(8,128)(2,1)S(1)}, bf16[128,2048]{1,0:T(8,128)(2,1)S(1)}, u32[]{:S(2)}, u32[]{:S(2)}) collective-permute-start(bf16[128,2048]{1,0:T(8,128)(2,1)S(1)} %pad_maximum_fusion.3), channel_id=1, source_target_pairs={{0,4},{1,5},{2,6},{3,7},{4,0},{5,1},{6,2},{7,3},{8,12},{9,13},{10,... | collective-permute-start | bytes 1572872 | tf_op jit(solution)/shard_map/ppermute | solution.py:16
  245.4 14.9 %collective-permute-start.23 = (bf16[128,2048]{1,0:T(8,128)(2,1)S(1)}, bf16[128,2048]{1,0:T(8,128)(2,1)S(1)}, u32[]{:S(2)}, u32[]{:S(2)}) collective-permute-start(bf16[128,2048]{1,0:T(8,128)(2,1)S(1)} %pad_maximum_fusion.2), channel_id=1, source_target_pairs={{0,2},{1,3},{2,0},{3,1},{4,6},{5,7},{6,4},{7,5},{8,10},{9,11},{10,... | collective-permute-start | bytes 1572872 | tf_op jit(solution)/shard_map/ppermute | solution.py:16
  246.3 14.0 %collective-permute-start.45 = (bf16[128,2048]{1,0:T(8,128)(2,1)S(1)}, bf16[128,2048]{1,0:T(8,128)(2,1)S(1)}, u32[]{:S(2)}, u32[]{:S(2)}) collective-permute-start(bf16[128,2048]{1,0:T(8,128)(2,1)S(1)} %add_convert_fusion.6), channel_id=1, source_target_pairs={{0,16},{1,17},{2,18},{3,19},{4,20},{5,21},{6,22},{7,23},{8,0},{9,1... | collective-permute-start | bytes 1572872 | tf_op jit(solution)/shard_map/ppermute | solution.py:16
  249.9 15.2 %collective-permute-start.16 = (bf16[128,2048]{1,0:T(8,128)(2,1)S(1)}, bf16[128,2048]{1,0:T(8,128)(2,1)S(1)}, u32[]{:S(2)}, u32[]{:S(2)}) collective-permute-start(bf16[128,2048]{1,0:T(8,128)(2,1)S(1)} %pad_maximum_fusion.1), channel_id=1, source_target_pairs={{0,4},{1,5},{2,6},{3,7},{4,0},{5,1},{6,2},{7,3},{8,12},{9,13},{10,... | collective-permute-start | bytes 1572872 | tf_op jit(solution)/shard_map/ppermute | solution.py:16
  250.2 17.0 %collective-permute-start.14 = (bf16[128,2048]{1,0:T(8,128)(2,1)S(1)}, bf16[128,2048]{1,0:T(8,128)(2,1)S(1)}, u32[]{:S(2)}, u32[]{:S(2)}) collective-permute-start(bf16[128,2048]{1,0:T(8,128)(2,1)S(1)} %pad_maximum_fusion), channel_id=1, source_target_pairs={{0,2},{1,3},{2,0},{3,1},{4,6},{5,7},{6,4},{7,5},{8,10},{9,11},{10,... | collective-permute-start | bytes 1572872 | tf_op jit(solution)/shard_map/ppermute | solution.py:16
  260.6 9.7 %collective-permute-start.46 = (bf16[128,2048]{1,0:T(8,128)(2,1)S(1)}, bf16[128,2048]{1,0:T(8,128)(2,1)S(1)}, u32[]{:S(2)}, u32[]{:S(2)}) collective-permute-start(bf16[128,2048]{1,0:T(8,128)(2,1)S(1)} %add_convert_fusion.5), channel_id=1, source_target_pairs={{0,16},{1,17},{2,18},{3,19},{4,20},{5,21},{6,22},{7,23},{8,0},{9,1... | collective-permute-start | bytes 1572872 | tf_op jit(solution)/shard_map/ppermute | solution.py:16
  (16 other events, 96.7 us)

commit v2 on v0

--- a/solution.py
+++ b/solution.py
@@ -1,7 +1,252 @@
+import functools
+
 import jax
 import jax.numpy as jnp
 from jax import lax
+from jax.experimental import pallas as pl
+from jax.experimental.pallas import tpu as pltpu
 from jax.sharding import PartitionSpec as P
+
+BOTH = ("expert", "dp")
+bf16, f32 = jnp.bfloat16, jnp.float32
+
+
+def moved(array, step):
+    pairs = []
+    for device in range(32):
+        z, y, x, core = device // 8, device // 4 % 2, device // 2 % 2, device % 2
+        z, y, x, core = step(z, y, x, core)
+        pairs.append((device, ((z * 2 + y) * 2 + x) * 2 + core))
+    return lax.ppermute(array, BOTH, pairs)
+
+
+def to_core(z, y, x, core):
+    return z, y, x, 1 - core
+
+
+def to_x(z, y, x, core):
+    return z, y, 1 - x, core
+
+
+def to_y(z, y, x, core):
+    return z, 1 - y, x, core
+
+
+def ring_on(z, y, x, core):
+    return (1, 3, 0, 2)[z], y, x, core
+
+
+def ring_back(z, y, x, core):
+    return (2, 0, 3, 1)[z], y, x, core
+
+
+def silu(v):
+    return v / (1.0 + jnp.exp(-v))
+
+
+def prepare(ids_ref, weight_ref, up_ref, down_ref, pairs_ref, own_ref, sent_ref):
+    experts = pairs_ref.shape[0]
+    rows = ids_ref.shape[1]
+    expert = lax.broadcasted_iota(jnp.int32, (experts, rows), 0)
+    near = jnp.zeros((experts, rows), f32)
+    far = jnp.zeros((experts, rows), f32)
+    weights = weight_ref[...].astype(f32)
+    for k in range(ids_ref.shape[0]):
+        named = ids_ref[k : k + 1, :]
+        weight = weights[k : k + 1, :]
+        near = jnp.where(named == expert, weight, near)
+        far = jnp.where((named ^ 1) == expert, weight, far)
+    pairs_ref[:, :rows] = near.astype(bf16)
+    pairs_ref[:, rows:] = far.astype(bf16)
+    depth, both = up_ref.shape
+    feature = both // 8
+    half_out = down_ref.shape[1] // 2
+    plane = lax.axis_index("expert") % 2 * 2
+    x = lax.axis_index("dp") // 2
+    for ref, place in ((own_ref, plane + x), (sent_ref, plane + 1 - x)):
+        start = pl.multiple_of(place * feature, feature)
+        ref[:depth, :feature] = up_ref[:, pl.ds(start, feature)]
+        up_start = pl.multiple_of(both // 2 + start, feature)
+        ref[:depth, feature:] = up_ref[:, pl.ds(up_start, feature)]
+        for side in range(2):
+            ref[depth + side * feature : depth + (side + 1) * feature, :] = down_ref[
+                pl.ds(start, feature), side * half_out : (side + 1) * half_out
+            ]
+
+
+def feed(shared, slot, *refs):
+    here, by_x, by_y, top, low = refs[:5]
+    weights = refs[5:11]
+    got, pick = refs[11:13]
+    rest = refs[13:]
+    if shared:
+        pieces, switch_ref, rest = rest[:4], rest[4], rest[5:]
+    out_here, out_x, out_y, out_top, out_low, rows_ref, total = rest
+    step = pl.program_id(0)
+    tile = here.shape[0]
+    half = tile // 2
+
+    @pl.when(step == 0)
+    def _():
+        rows_ref[:tile] = here[...]
+        rows_ref[tile : 2 * tile] = by_x[...]
+        rows_ref[2 * tile : 3 * tile] = by_y[...]
+        rows_ref[3 * tile : 3 * tile + half] = top[...]
+        rows_ref[3 * tile + half :] = low[...]
+        if shared:
+            place = lax.axis_index("dp")
+            depth = rows_ref.shape[1] // 4
+            feature = pieces[0].shape[1] // 2
+            both = jnp.zeros((4 * tile, 2 * feature), f32)
+            turn = jnp.zeros((4 * tile, 1), f32)
+            for j, piece in enumerate(pieces):
+                start = pl.multiple_of((place ^ j) * depth, depth)
+                both += jnp.dot(rows_ref[:, pl.ds(start, depth)], piece[:depth], preferred_element_type=f32)
+                fixed = slice(j * depth, (j + 1) * depth)
+                turn += jnp.sum(
+                    rows_ref[:, fixed].astype(f32) * switch_ref[:, fixed].astype(f32), axis=1, keepdims=True
+                )
+            hidden = (silu(both[:, :feature]) * both[:, feature:]).astype(bf16)
+            turn = 1.0 / (1.0 + jnp.exp(-turn))
+            for j, piece in enumerate(pieces):
+                for side in range(2):
+                    start = pl.multiple_of((place ^ j) * depth + side * (depth // 2), depth // 2)
+                    part = piece[depth + side * feature : depth + (side + 1) * feature]
+                    total[:, pl.ds(start, depth // 2)] = turn * jnp.dot(hidden, part, preferred_element_type=f32)
+        else:
+            total[...] = jnp.zeros_like(total)
+
+    def add(gate_ref, up_ref, down_ref, which):
+        columns = lax.dot_general(
+            got[:, which * tile : (which + 1) * tile],
+            pick[...],
+            (((0,), (0,)), ((), ())),
+            preferred_element_type=f32,
+        )
+        scale = jnp.concatenate([columns[:, slot * 4 + s : slot * 4 + s + 1] for s in range(4)], axis=0)
+        gate = jnp.dot(rows_ref[...], gate_ref[0], preferred_element_type=f32)
+        upper = jnp.dot(rows_ref[...], up_ref[0], preferred_element_type=f32)
+        hidden = (silu(gate) * upper).astype(bf16)
+        span = 512
+        for start in range(0, total.shape[1], span):
+            cut = slice(start, start + span)
+            total[:, cut] += scale * jnp.dot(hidden, down_ref[0, :, cut], preferred_element_type=f32)
+
+    @pl.when(step < 2)
+    def _():
+        add(*weights[:3], 0)
+
+    @pl.when(step >= 2)
+    def _():
+        add(*weights[3:], 1)
+
+    @pl.when(step == 3)
+    def _():
+        out_here[...] = total[:tile].astype(bf16)
+        out_x[...] = total[tile : 2 * tile].astype(bf16)
+        out_y[...] = total[2 * tile : 3 * tile].astype(bf16)
+        out_top[...] = total[3 * tile : 3 * tile + half].astype(bf16)
+        out_low[...] = total[3 * tile + half :].astype(bf16)
+
+
+def whole(array):
+    return pl.BlockSpec(array.shape, lambda i: (0,) * array.ndim)
+
+
+def run_feed(slot, parts, mine, other, got, pick, extra):
+    tile, width = parts[0].shape
+    hidden = mine[0].shape[2]
+    cut = hidden // 2
+
+    def tiles(first):
+        def at(i):
+            return jnp.clip(i - first, 0, 1)
+
+        return [
+            pl.BlockSpec((1, width, cut), lambda i: (0, 0, at(i))),
+            pl.BlockSpec((1, width, cut), lambda i: (0, 0, at(i))),
+            pl.BlockSpec((1, cut, width), lambda i: (0, at(i), 0)),
+        ]
+
+    outs = [jax.ShapeDtypeStruct((n, width), bf16) for n in (tile, tile, tile, tile // 2, tile // 2)]
+    return pl.pallas_call(
+        functools.partial(feed, bool(extra), slot),
+        grid=(4,),
+        in_specs=[whole(p) for p in parts]
+        + tiles(0)
+        + tiles(2)
+        + [whole(got), whole(pick)]
+        + [whole(e) for e in extra],
+        out_specs=[whole(o) for o in outs],
+        out_shape=outs,
+        scratch_shapes=[pltpu.VMEM((4 * tile, width), bf16), pltpu.VMEM((4 * tile, width), f32)],
+        compiler_params=pltpu.CompilerParams(vmem_limit_bytes=40 * 1024 * 1024),
+        cost_estimate=pl.CostEstimate(
+            flops=2 * 4 * tile * width * hidden * 6, bytes_accessed=16 * 2**20, transcendentals=4 * tile * hidden * 2
+        ),
+    )(*parts, *mine, *other, got, pick, *extra)
+
+
+def blocks(
+    tokens,
+    expert_ids,
+    route_weight,
+    expert_gate,
+    expert_up,
+    expert_down,
+    shared_gate_up,
+    shared_down,
+    shared_switch,
+):
+    rows, width = tokens.shape
+    half = rows // 2
+    place, plane = lax.axis_index("dp"), lax.axis_index("expert")
+    z, y = plane // 2, plane % 2
+    ring_place = z ^ (z // 2)
+    depth, both = shared_gate_up.shape
+    feature = both // 8
+    piece_shape = jax.ShapeDtypeStruct((depth + 2 * feature, 2 * feature), bf16)
+    pairs, own, sent = pl.pallas_call(
+        prepare,
+        out_shape=[jax.ShapeDtypeStruct((32, 2 * rows), bf16), piece_shape, piece_shape],
+    )(expert_ids.T, route_weight.T, shared_gate_up, shared_down)
+    got = lax.all_to_all(pairs.reshape(32, 1, 2 * rows), BOTH, split_axis=0, concat_axis=0, tiled=True)
+    got = got.reshape(32, 2 * rows)
+    slot = lax.broadcasted_iota(jnp.int32, (32, 128), 1)
+    from_place = (ring_place + 4 - slot // 4) % 4
+    from_z = from_place ^ (from_place // 2)
+    source = (from_z * 2 + (y ^ (slot // 2 % 2))) * 4 + (place ^ (slot % 2 * 2))
+    pick = (source == lax.broadcasted_iota(jnp.int32, (32, 128), 0)).astype(bf16)
+
+    mine = (expert_gate, expert_up, expert_down)
+    other = tuple(moved(part, to_core) for part in mine)
+    far = moved(sent, to_x)
+    extra = (own, moved(own, to_core), far, moved(far, to_core), shared_switch.reshape(1, width))
+
+    columns = [tokens]
+    for back in range(3):
+        columns.append(moved(columns[-1], ring_on))
+    partial = []
+    for back in range(4):
+        block = columns[back]
+        by_x, by_y = moved(block, to_x), moved(block, to_y)
+        top, low = moved(by_y[:half], to_x), moved(by_x[half:], to_y)
+        parts = (block, by_x, by_y, top, low)
+        partial.append(run_feed(back, parts, mine, other, got, pick, () if back else extra))
+
+    arriving = None
+    for back in (3, 2, 1, 0):
+        here, along_x, along_y, top, low = partial[back]
+        top, low = moved(top, to_x).astype(f32), moved(low, to_y).astype(f32)
+        along_y = jnp.concatenate([along_y[:half].astype(f32) + top, along_y[half:].astype(f32)]).astype(bf16)
+        along_x = jnp.concatenate([along_x[:half].astype(f32), along_x[half:].astype(f32) + low]).astype(bf16)
+        total = here.astype(f32) + moved(along_x, to_x).astype(f32) + moved(along_y, to_y).astype(f32)
+        if arriving is not None:
+            total = total + arriving.astype(f32)
+        total = total.astype(bf16)
+        if back:
+            arriving = moved(total, ring_back)
+    return total
 
 
 def shards(
@@ -86,4 +331,5 @@
         P(),
     )
     out_specs = P(("groups", "expert", "dp"), None)
-    return jax.shard_map(shards, mesh=mesh, in_specs=in_specs, out_specs=out_specs, check_vma=False)
+    part = blocks if (mesh.shape["expert"], mesh.shape["dp"]) == (8, 4) else shards
+    return jax.shard_map(part, mesh=mesh, in_specs=in_specs, out_specs=out_specs, check_vma=False)

time: 427 us -> 213 us (0.50)
  waiting for transfers between devices: 277 us -> 87.6 us
  local copies, waits for them, and re-layouts: 70 us -> 9.04 us
  Pallas kernels: 0 us -> 46.1 us
  starting transfers between devices: 17.3 us -> 60.8 us
  matrix products: 32.2 us -> 0 us
  between operations: 13.6 us -> 0.41 us
  other arithmetic: 16.1 us -> 7.17 us
    all_to_all x3 -> x1, waiting for transfers between devices: 190 us -> 0.01 us  [blocks(): lax.all_to_all(pairs.reshape(32, 1, 2 * rows), BOTH, split_axis=0, concat...]
    ppermute x0 -> x44, waiting for transfers between devices: none -> 87.5 us  [moved(): return lax.ppermute(array, BOTH, pairs)]
    all_gather x2 -> x0, waiting for transfers between devices: 85.8 us -> none  [the longest x1 85.8 us: shards(): lax.all_gather(shared_gate_up, 'dp', axis=0, tiled=True)]
    ppermute x0 -> x44, starting transfers between devices: none -> 57.6 us  [moved(): return lax.ppermute(array, BOTH, pairs)]
    pallas_call x0 -> x5, Pallas kernels: none -> 46.1 us  [the longest x4 43.7 us: run_feed(): pl.pallas_call(functools.partial(feed, bool(extra), slot), grid=(4,), in_...]
    dot_general x5 -> x0, matrix products: 32.2 us -> none  [the longest x1 11.7 us: shards(): answer = jnp.dot(hidden, expert_down[0], preferred_element_type=jnp.float32)]
    gather x3 -> x0, local copies, waits for them, and re-layouts: 31 us -> none  [the longest x1 14.4 us: shards(): gathered = returned[slot_index].reshape(tok_count, top_count, width)]
    slice x3 -> x16, local copies, waits for them, and re-layouts: 20.8 us -> 1.73 us  [the longest x8 1.58 us: blocks(): top, low = (moved(by_y[:half], to_x), moved(by_x[half:], to_y))]
  transfers between devices with their start and end apart: 5 -> 45, of which waited for: 3 -> 20; matrix products, arithmetic and copies ran while one was open for 14% -> 6% of each run, Pallas kernels for 0% -> 22%
where the time goes in v2:
time: 213 us; the launch traced here: 211 us
  waiting for transfers between devices  87.6 us (41%)
  starting transfers between devices  60.8 us (29%)
  Pallas kernels  46.1 us (22%)
  local copies, waits for them, and re-layouts  9.04 us (4%)
  other arithmetic  7.17 us (3%)
    ppermute x44, waiting for transfers between devices, moved(): return lax.ppermute(array, BOTH, pairs)  87.5 us
    ppermute x44, starting transfers between devices, moved(): return lax.ppermute(array, BOTH, pairs)  57.6 us
    pallas_call x4, Pallas kernels, run_feed(): pl.pallas_call(functools.partial(feed, bool(extra), slot), grid=(4,), in_...  43.7 us
    unnamed x25, local copies, waits for them, and re-layouts  6.07 us
  transfers between devices with their start and end apart: 45, of which 20 were waited for; matrix products, arithmetic and copies ran while one was open for 6% of the time, Pallas kernels for 22%

profile of v2, /device:TPU:0, one launch (start us, length us, event | category | flops | bytes accessed | tf_op | source)
XLA Modules:
  0.0 211.1 jit_solution(11031147649958730493)
XLA Ops:
  0.0 3.0 %collective-permute-start.14 = (bf16[128,2048]{1,0:T(8,128)(2,1)}, bf16[128,2048]{1,0:T(8,128)(2,1)S(1)}, u32[]{:S(2)}, u32[]{:S(2)}) collective-permute-start(bf16[128,2048]{1,0:T(8,128)(2,1)} %refs_0_.1), channel_id=1, source_target_pairs={{0,8},{1,9},{2,10},{3,11},{4,12},{5,13},{6,14},{7,15},{8,24},{9,25... | collective-permute-start | bytes 1572872 | tf_op jit(solution)/shard_map/ppermute | solution.py:20
  3.0 2.4 %shard_map.91 = (bf16[32,256]{1,0:T(8,128)(2,1)}, bf16[768,256]{1,0:T(8,128)(2,1)}, bf16[768,256]{1,0:T(8,128)(2,1)}) custom-call(s32[10,128]{1,0:T(8,128)} %bitcast.11, bf16[10,128]{1,0:T(8,128)(2,1)} %bitcast.12, bf16[512,1024]{1,0:T(8,128)(2,1)} %up_ref.1, bf16[512,512]{1,0:T(8,128)(2,1)} %down_ref.1), custom_call_target="tpu_custom_call" | custom-call | tf_op jit(solution)/shard_map/pallas_call | solution.py:209
  5.5 1.5 collective-permute-start.8
  7.5 1.5 collective-permute-start.1
  9.0 8.7 %collective-permute-done.8.refs_15_ = bf16[768,256]{1,0:T(8,128)(2,1)S(1)} collective-permute-done((bf16[768,256]{1,0:T(8,128)(2,1)}, bf16[768,256]{1,0:T(8,128)(2,1)S(1)}, u32[]{:S(2)}, u32[]{:S(2)}) %collective-permute-start.8) | collective-permute-done | bytes 393248 | tf_op jit(solution)/shard_map/ppermute | solution.py:20
  18.2 9.3 %collective-permute-done.refs_1_ = bf16[128,2048]{1,0:T(8,128)(2,1)S(1)} collective-permute-done((bf16[128,2048]{1,0:T(8,128)(2,1)}, bf16[128,2048]{1,0:T(8,128)(2,1)S(1)}, u32[]{:S(2)}, u32[]{:S(2)}) %collective-permute-start) | collective-permute-done | bytes 524320 | tf_op jit(solution)/shard_map/ppermute | solution.py:20
  27.5 2.6 %collective-permute-start.23 = (bf16[128,2048]{1,0:T(8,128)(2,1)S(1)}, bf16[128,2048]{1,0:T(8,128)(2,1)}, u32[]{:S(2)}, u32[]{:S(2)}) collective-permute-start(bf16[128,2048]{1,0:T(8,128)(2,1)S(1)} %collective-permute-done.14.refs_0_), channel_id=1, source_target_pairs={{0,8},{1,9},{2,10},{3,11},{4,12},{5,13},{6,14},{7,15},{8,24},{9,25... | collective-permute-start | bytes 1572872 | tf_op jit(solution)/shard_map/ppermute | solution.py:20
  30.1 1.5 collective-permute-start.15
  31.6 9.4 %collective-permute-done.23.refs_0_ = bf16[128,2048]{1,0:T(8,128)(2,1)} collective-permute-done((bf16[128,2048]{1,0:T(8,128)(2,1)S(1)}, bf16[128,2048]{1,0:T(8,128)(2,1)}, u32[]{:S(2)}, u32[]{:S(2)}) %collective-permute-start.23) | collective-permute-done | bytes 524320 | tf_op jit(solution)/shard_map/ppermute | solution.py:20
  41.0 1.5 collective-permute-start.24
  43.0 1.5 collective-permute-start.25
  44.5 9.0 %collective-permute-done.24.refs_1_ = bf16[128,2048]{1,0:T(8,128)(2,1)S(1)} collective-permute-done((bf16[128,2048]{1,0:T(8,128)(2,1)}, bf16[128,2048]{1,0:T(8,128)(2,1)S(1)}, u32[]{:S(2)}, u32[]{:S(2)}) %collective-permute-start.24) | collective-permute-done | bytes 524320 | tf_op jit(solution)/shard_map/ppermute | solution.py:20
  53.5 1.5 collective-permute-start.16
  55.0 2.1 %collective-permute-start.32 = (bf16[128,2048]{1,0:T(8,128)(2,1)}, bf16[128,2048]{1,0:T(8,128)(2,1)}, u32[]{:S(2)}, u32[]{:S(2)}) collective-permute-start(bf16[128,2048]{1,0:T(8,128)(2,1)} %collective-permute-done.23.refs_0_), channel_id=1, source_target_pairs={{0,8},{1,9},{2,10},{3,11},{4,12},{5,13},{6,14},{7,15},{8,24},{9,25... | collective-permute-start | bytes 1572872 | tf_op jit(solution)/shard_map/ppermute | solution.py:20
  59.7 3.2 %all-to-all-start = ((bf16[32,2,128]{2,1,0:T(2,128)(2,1)}), bf16[32,2,128]{2,1,0:T(2,128)(2,1)}, u32[]{:S(2)}, u32[]{:S(2)}) async-start(bf16[32,2,128]{2,1,0:T(2,128)(2,1)} %reshape.12), calls=%async_computation | async-start | bytes 32768 | tf_op jit(solution)/shard_map/all_to_all | solution.py:213
  66.0 1.6 collective-permute-start.26
  67.6 1.5 collective-permute-start.27
  76.8 1.5 collective-permute-start.18
  78.8 1.6 copy-done.1
  80.4 1.6 copy-done.4
  82.0 10.7 %shard_map.94 = (bf16[128,2048]{1,0:T(8,128)(2,1)S(1)}, bf16[128,2048]{1,0:T(8,128)(2,1)S(1)}, bf16[128,2048]{1,0:T(8,128)(2,1)S(1)}, bf16[64,2048]{1,0:T(8,128)(2,1)S(1)}, bf16[64,2048]{1,0:T(8,128)(2,1)S(1)}) custom-call(bf16[128,2048]{1,0:T(8,128)(2,1)} %collective-permute-done.23.refs_0_, bf16[128,2048]{1,0:T(8,128)(2,1)S(1)} %collective-permute-done.24.refs_1_, ...), custom_call_target="tpu_custom_call" | custom-call | flops 6442450944 | bytes 16777216 | tf_op jit(solution)/shard_map/pallas_call | solution.py:172
  94.0 1.5 collective-permute-start.3
  96.0 2.4 %collective-permute-start.33 = (bf16[128,2048]{1,0:T(8,128)(2,1)}, bf16[128,2048]{1,0:T(8,128)(2,1)S(1)}, u32[]{:S(2)}, u32[]{:S(2)}) collective-permute-start(bf16[128,2048]{1,0:T(8,128)(2,1)} %collective-permute-done.32.refs_0_), channel_id=1, source_target_pairs={{0,2},{1,3},{2,0},{3,1},{4,6},{5,7},{6,4},{7,5},{8,10},{9,11},{10,... | collective-permute-start | bytes 1572872 | tf_op jit(solution)/shard_map/ppermute | solution.py:20
  98.4 10.2 %shard_map.93 = (bf16[128,2048]{1,0:T(8,128)(2,1)S(1)}, bf16[128,2048]{1,0:T(8,128)(2,1)S(1)}, bf16[128,2048]{1,0:T(8,128)(2,1)S(1)}, bf16[64,2048]{1,0:T(8,128)(2,1)S(1)}, bf16[64,2048]{1,0:T(8,128)(2,1)S(1)}) custom-call(bf16[128,2048]{1,0:T(8,128)(2,1)S(1)} %copy-done.7, bf16[128,2048]{1,0:T(8,128)(2,1)S(1)} %collective-permute-done.15.refs_1_, ...), custom_call_target="tpu_custom_call" | custom-call | flops 6442450944 | bytes 16777216 | tf_op jit(solution)/shard_map/pallas_call | solution.py:172
  108.8 2.7 %collective-permute-done.33.refs_1_ = bf16[128,2048]{1,0:T(8,128)(2,1)S(1)} collective-permute-done((bf16[128,2048]{1,0:T(8,128)(2,1)}, bf16[128,2048]{1,0:T(8,128)(2,1)S(1)}, u32[]{:S(2)}, u32[]{:S(2)}) %collective-permute-start.33) | collective-permute-done | bytes 524320 | tf_op jit(solution)/shard_map/ppermute | solution.py:20
  111.5 1.7 collective-permute-start.35
  113.2 1.6 collective-permute-start.36
  115.6 1.7 collective-permute-start.21
  117.3 12.4 %shard_map.92 = (bf16[128,2048]{1,0:T(8,128)(2,1)S(1)}, bf16[128,2048]{1,0:T(8,128)(2,1)S(1)}, bf16[128,2048]{1,0:T(8,128)(2,1)S(1)}, bf16[64,2048]{1,0:T(8,128)(2,1)S(1)}, bf16[64,2048]{1,0:T(8,128)(2,1)S(1)}) custom-call(bf16[128,2048]{1,0:T(8,128)(2,1)S(1)} %copy-done.5, bf16[128,2048]{1,0:T(8,128)(2,1)S(1)} %collective-permute-done.refs_1_, ...), custom_call_target="tpu_custom_call" | custom-call | flops 6442450944 | bytes 16777216 | tf_op jit(solution)/shard_map/pallas_call | solution.py:172
  129.8 1.6 collective-permute-start.19
  131.9 10.4 %shard_map.95 = (bf16[128,2048]{1,0:T(8,128)(2,1)S(1)}, bf16[128,2048]{1,0:T(8,128)(2,1)S(1)}, bf16[128,2048]{1,0:T(8,128)(2,1)S(1)}, bf16[64,2048]{1,0:T(8,128)(2,1)S(1)}, bf16[64,2048]{1,0:T(8,128)(2,1)S(1)}) custom-call(bf16[128,2048]{1,0:T(8,128)(2,1)} %collective-permute-done.32.refs_0_, bf16[128,2048]{1,0:T(8,128)(2,1)S(1)} %collective-permute-done.33.refs_1_, ...), custom_call_target="tpu_custom_call" | custom-call | flops 6442450944 | bytes 16777216 | tf_op jit(solution)/shard_map/pallas_call | solution.py:172
  144.6 1.6 collective-permute-start.37
  146.4 3.4 %collective-permute-done.39 = bf16[64,2048]{1,0:T(8,128)(2,1)S(1)} collective-permute-done((bf16[64,2048]{1,0:T(8,128)(2,1)S(1)}, bf16[64,2048]{1,0:T(8,128)(2,1)S(1)}, u32[]{:S(2)}, u32[]{:S(2)}) %collective-permute-start.39) | collective-permute-done | bytes 262176 | tf_op jit(solution)/shard_map/ppermute | solution.py:20
  151.1 6.1 %collective-permute-done.37 = bf16[64,2048]{1,0:T(8,128)(2,1)S(1)} collective-permute-done((bf16[64,2048]{1,0:T(8,128)(2,1)S(1)}, bf16[64,2048]{1,0:T(8,128)(2,1)S(1)}, u32[]{:S(2)}, u32[]{:S(2)}) %collective-permute-start.37) | collective-permute-done | bytes 262176 | tf_op jit(solution)/shard_map/ppermute | solution.py:20
  157.4 1.5 collective-permute-start.38
  159.6 8.9 %collective-permute-done.40 = bf16[128,2048]{1,0:T(8,128)(2,1)S(1)} collective-permute-done((bf16[128,2048]{1,0:T(8,128)(2,1)S(1)}, bf16[128,2048]{1,0:T(8,128)(2,1)S(1)}, u32[]{:S(2)}, u32[]{:S(2)}) %collective-permute-start.40) | collective-permute-done | bytes 524320 | tf_op jit(solution)/shard_map/ppermute | solution.py:20
  168.5 1.4 collective-permute-start.29
  170.8 2.5 %collective-permute-start.41 = (bf16[128,2048]{1,0:T(8,128)(2,1)S(1)}, bf16[128,2048]{1,0:T(8,128)(2,1)S(1)}, u32[]{:S(2)}, u32[]{:S(2)}) collective-permute-start(bf16[128,2048]{1,0:T(8,128)(2,1)S(1)} %add_convert_fusion.3), channel_id=1, source_target_pairs={{0,16},{1,17},{2,18},{3,19},{4,20},{5,21},{6,22},{7,23},{8,0},{9,1... | collective-permute-start | bytes 1572872 | tf_op jit(solution)/shard_map/ppermute | solution.py:20
  173.5 6.3 %collective-permute-done.31 = bf16[128,2048]{1,0:T(8,128)(2,1)S(1)} collective-permute-done((bf16[128,2048]{1,0:T(8,128)(2,1)S(1)}, bf16[128,2048]{1,0:T(8,128)(2,1)S(1)}, u32[]{:S(2)}, u32[]{:S(2)}) %collective-permute-start.31) | collective-permute-done | bytes 524320 | tf_op jit(solution)/shard_map/ppermute | solution.py:20
  179.7 1.4 collective-permute-start.20
  181.8 2.2 %collective-permute-done.41 = bf16[128,2048]{1,0:T(8,128)(2,1)S(1)} collective-permute-done((bf16[128,2048]{1,0:T(8,128)(2,1)S(1)}, bf16[128,2048]{1,0:T(8,128)(2,1)S(1)}, u32[]{:S(2)}, u32[]{:S(2)}) %collective-permute-start.41) | collective-permute-done | bytes 524320 | tf_op jit(solution)/shard_map/ppermute | solution.py:20
  184.4 3.3 %collective-permute-start.42 = (bf16[128,2048]{1,0:T(8,128)(2,1)S(1)}, bf16[128,2048]{1,0:T(8,128)(2,1)S(1)}, u32[]{:S(2)}, u32[]{:S(2)}) collective-permute-start(bf16[128,2048]{1,0:T(8,128)(2,1)S(1)} %add_convert_fusion.2), channel_id=1, source_target_pairs={{0,16},{1,17},{2,18},{3,19},{4,20},{5,21},{6,22},{7,23},{8,0},{9,1... | collective-permute-start | bytes 1572872 | tf_op jit(solution)/shard_map/ppermute | solution.py:20
  187.8 1.7 collective-permute-start.11
  189.5 1.5 collective-permute-done.22
  191.0 3.6 %collective-permute-done.20 = bf16[128,2048]{1,0:T(8,128)(2,1)S(1)} collective-permute-done((bf16[128,2048]{1,0:T(8,128)(2,1)S(1)}, bf16[128,2048]{1,0:T(8,128)(2,1)S(1)}, u32[]{:S(2)}, u32[]{:S(2)}) %collective-permute-start.20) | collective-permute-done | bytes 524320 | tf_op jit(solution)/shard_map/ppermute | solution.py:20
  194.6 4.9 %collective-permute-done.42 = bf16[128,2048]{1,0:T(8,128)(2,1)S(1)} collective-permute-done((bf16[128,2048]{1,0:T(8,128)(2,1)S(1)}, bf16[128,2048]{1,0:T(8,128)(2,1)S(1)}, u32[]{:S(2)}, u32[]{:S(2)}) %collective-permute-start.42) | collective-permute-done | bytes 524320 | tf_op jit(solution)/shard_map/ppermute | solution.py:20
  199.8 3.4 %collective-permute-start.43 = (bf16[128,2048]{1,0:T(8,128)(2,1)S(1)}, bf16[128,2048]{1,0:T(8,128)(2,1)S(1)}, u32[]{:S(2)}, u32[]{:S(2)}) collective-permute-start(bf16[128,2048]{1,0:T(8,128)(2,1)S(1)} %add_convert_fusion.1), channel_id=1, source_target_pairs={{0,16},{1,17},{2,18},{3,19},{4,20},{5,21},{6,22},{7,23},{8,0},{9,1... | collective-permute-start | bytes 1572872 | tf_op jit(solution)/shard_map/ppermute | solution.py:20
  203.3 6.7 %collective-permute-done.43 = bf16[128,2048]{1,0:T(8,128)(2,1)S(1)} collective-permute-done((bf16[128,2048]{1,0:T(8,128)(2,1)S(1)}, bf16[128,2048]{1,0:T(8,128)(2,1)S(1)}, u32[]{:S(2)}, u32[]{:S(2)}) %collective-permute-start.43) | collective-permute-done | bytes 524320 | tf_op jit(solution)/shard_map/ppermute | solution.py:20
  (117 shorter events, 27.1 us)
Async XLA Ops:
  0.0 17.7 %collective-permute-start.14 = (bf16[128,2048]{1,0:T(8,128)(2,1)}, bf16[128,2048]{1,0:T(8,128)(2,1)S(1)}, u32[]{:S(2)}, u32[]{:S(2)}) collective-permute-start(bf16[128,2048]{1,0:T(8,128)(2,1)} %refs_0_.1), channel_id=1, source_target_pairs={{0,8},{1,9},{2,10},{3,11},{4,12},{5,13},{6,14},{7,15},{8,24},{9,25... | collective-permute-start | bytes 1572872 | tf_op jit(solution)/shard_map/ppermute | solution.py:20
  5.5 69.2 %copy-start.8 = (bf16[768,256]{1,0:T(8,128)(2,1)S(1)}, bf16[768,256]{1,0:T(8,128)(2,1)}, u32[]{:S(2)}) copy-start(bf16[768,256]{1,0:T(8,128)(2,1)} %get-tuple-element.29.refs_13_) | copy-start | bytes 1179652
  5.5 12.2 %collective-permute-start.8 = (bf16[768,256]{1,0:T(8,128)(2,1)}, bf16[768,256]{1,0:T(8,128)(2,1)S(1)}, u32[]{:S(2)}, u32[]{:S(2)}) collective-permute-start(bf16[768,256]{1,0:T(8,128)(2,1)} %get-tuple-element.30), channel_id=1, source_target_pairs={{0,2},{1,3},{2,0},{3,1},{4,6},{5,7},{6,4},{7,5},{8,10},{9,11},{10,... | collective-permute-start | bytes 1179656 | tf_op jit(solution)/shard_map/ppermute | solution.py:20
  7.0 20.5 %collective-permute-start = (bf16[128,2048]{1,0:T(8,128)(2,1)}, bf16[128,2048]{1,0:T(8,128)(2,1)S(1)}, u32[]{:S(2)}, u32[]{:S(2)}) collective-permute-start(bf16[128,2048]{1,0:T(8,128)(2,1)} %refs_0_.1), channel_id=1, source_target_pairs={{0,2},{1,3},{2,0},{3,1},{4,6},{5,7},{6,4},{7,5},{8,10},{9,11},{10,... | collective-permute-start | bytes 1572872 | tf_op jit(solution)/shard_map/ppermute | solution.py:20
  7.5 22.6 %collective-permute-start.1 = (bf16[128,2048]{1,0:T(8,128)(2,1)}, bf16[128,2048]{1,0:T(8,128)(2,1)S(1)}, u32[]{:S(2)}, u32[]{:S(2)}) collective-permute-start(bf16[128,2048]{1,0:T(8,128)(2,1)} %refs_0_.1), channel_id=1, source_target_pairs={{0,4},{1,5},{2,6},{3,7},{4,0},{5,1},{6,2},{7,3},{8,12},{9,13},{10,... | collective-permute-start | bytes 1572872 | tf_op jit(solution)/shard_map/ppermute | solution.py:20
  9.0 67.0 %collective-permute-start.4 = (bf16[1,2048,512]{2,1,0:T(8,128)(2,1)}, bf16[1,2048,512]{2,1,0:T(8,128)(2,1)}, u32[]{:S(2)}, u32[]{:S(2)}) collective-permute-start(bf16[1,2048,512]{2,1,0:T(8,128)(2,1)} %refs_5_.7), channel_id=1, source_target_pairs={{0,1},{1,0},{2,3},{3,2},{4,5},{5,4},{6,7},{7,6},{8,9},{9,8},{10,11... | collective-permute-start | bytes 6291464 | tf_op jit(solution)/shard_map/ppermute | solution.py:20
  17.7 37.3 %copy-start.9 = (bf16[768,256]{1,0:T(8,128)(2,1)}, bf16[768,256]{1,0:T(8,128)(2,1)S(1)}, u32[]{:S(2)}) copy-start(bf16[768,256]{1,0:T(8,128)(2,1)S(1)} %collective-permute-done.8.refs_15_) | copy-start | bytes 1179652
  17.7 59.1 %collective-permute-start.5 = (bf16[1,2048,512]{2,1,0:T(8,128)(2,1)}, bf16[1,2048,512]{2,1,0:T(8,128)(2,1)}, u32[]{:S(2)}, u32[]{:S(2)}) collective-permute-start(bf16[1,2048,512]{2,1,0:T(8,128)(2,1)} %refs_6_.7), channel_id=1, source_target_pairs={{0,1},{1,0},{2,3},{3,2},{4,5},{5,4},{6,7},{7,6},{8,9},{9,8},{10,11... | collective-permute-start | bytes 6291464 | tf_op jit(solution)/shard_map/ppermute | solution.py:20
  17.7 26.8 %copy-start.6 = (bf16[128,2048]{1,0:T(8,128)(2,1)}, bf16[128,2048]{1,0:T(8,128)(2,1)S(1)}, u32[]{:S(2)}) copy-start(bf16[128,2048]{1,0:T(8,128)(2,1)S(1)} %collective-permute-done.14.refs_0_) | copy-start | bytes 1572868
  17.7 60.6 %collective-permute-start.6 = (bf16[1,512,2048]{2,1,0:T(8,128)(2,1)}, bf16[1,512,2048]{2,1,0:T(8,128)(2,1)}, u32[]{:S(2)}, u32[]{:S(2)}) collective-permute-start(bf16[1,512,2048]{2,1,0:T(8,128)(2,1)} %refs_7_.7), channel_id=1, source_target_pairs={{0,1},{1,0},{2,3},{3,2},{4,5},{5,4},{6,7},{7,6},{8,9},{9,8},{10,11... | collective-permute-start | bytes 6291464 | tf_op jit(solution)/shard_map/ppermute | solution.py:20
  27.5 13.5 %collective-permute-start.23 = (bf16[128,2048]{1,0:T(8,128)(2,1)S(1)}, bf16[128,2048]{1,0:T(8,128)(2,1)}, u32[]{:S(2)}, u32[]{:S(2)}) collective-permute-start(bf16[128,2048]{1,0:T(8,128)(2,1)S(1)} %collective-permute-done.14.refs_0_), channel_id=1, source_target_pairs={{0,8},{1,9},{2,10},{3,11},{4,12},{5,13},{6,14},{7,15},{8,24},{9,25... | collective-permute-start | bytes 1572872 | tf_op jit(solution)/shard_map/ppermute | solution.py:20
  30.1 12.9 %collective-permute-start.15 = (bf16[128,2048]{1,0:T(8,128)(2,1)S(1)}, bf16[128,2048]{1,0:T(8,128)(2,1)S(1)}, u32[]{:S(2)}, u32[]{:S(2)}) collective-permute-start(bf16[128,2048]{1,0:T(8,128)(2,1)S(1)} %collective-permute-done.14.refs_0_), channel_id=1, source_target_pairs={{0,2},{1,3},{2,0},{3,1},{4,6},{5,7},{6,4},{7,5},{8,10},{9,11},{10,... | collective-permute-start | bytes 1572872 | tf_op jit(solution)/shard_map/ppermute | solution.py:20
  41.0 12.5 %collective-permute-start.24 = (bf16[128,2048]{1,0:T(8,128)(2,1)}, bf16[128,2048]{1,0:T(8,128)(2,1)S(1)}, u32[]{:S(2)}, u32[]{:S(2)}) collective-permute-start(bf16[128,2048]{1,0:T(8,128)(2,1)} %collective-permute-done.23.refs_0_), channel_id=1, source_target_pairs={{0,2},{1,3},{2,0},{3,1},{4,6},{5,7},{6,4},{7,5},{8,10},{9,11},{10,... | collective-permute-start | bytes 1572872 | tf_op jit(solution)/shard_map/ppermute | solution.py:20
  43.0 12.0 %collective-permute-start.25 = (bf16[128,2048]{1,0:T(8,128)(2,1)}, bf16[128,2048]{1,0:T(8,128)(2,1)S(1)}, u32[]{:S(2)}, u32[]{:S(2)}) collective-permute-start(bf16[128,2048]{1,0:T(8,128)(2,1)} %collective-permute-done.23.refs_0_), channel_id=1, source_target_pairs={{0,4},{1,5},{2,6},{3,7},{4,0},{5,1},{6,2},{7,3},{8,12},{9,13},{10,... | collective-permute-start | bytes 1572872 | tf_op jit(solution)/shard_map/ppermute | solution.py:20
  53.5 12.5 %collective-permute-start.16 = (bf16[128,2048]{1,0:T(8,128)(2,1)}, bf16[128,2048]{1,0:T(8,128)(2,1)S(1)}, u32[]{:S(2)}, u32[]{:S(2)}) collective-permute-start(bf16[128,2048]{1,0:T(8,128)(2,1)} %copy-done.6), channel_id=1, source_target_pairs={{0,4},{1,5},{2,6},{3,7},{4,0},{5,1},{6,2},{7,3},{8,12},{9,13},{10,... | collective-permute-start | bytes 1572872 | tf_op jit(solution)/shard_map/ppermute | solution.py:20
  55.0 12.6 %collective-permute-start.32 = (bf16[128,2048]{1,0:T(8,128)(2,1)}, bf16[128,2048]{1,0:T(8,128)(2,1)}, u32[]{:S(2)}, u32[]{:S(2)}) collective-permute-start(bf16[128,2048]{1,0:T(8,128)(2,1)} %collective-permute-done.23.refs_0_), channel_id=1, source_target_pairs={{0,8},{1,9},{2,10},{3,11},{4,12},{5,13},{6,14},{7,15},{8,24},{9,25... | collective-permute-start | bytes 1572872 | tf_op jit(solution)/shard_map/ppermute | solution.py:20
  59.7 11.4 %all-to-all-start = ((bf16[32,2,128]{2,1,0:T(2,128)(2,1)}), bf16[32,2,128]{2,1,0:T(2,128)(2,1)}, u32[]{:S(2)}, u32[]{:S(2)}) async-start(bf16[32,2,128]{2,1,0:T(2,128)(2,1)} %reshape.12), calls=%async_computation | async-start | bytes 32768 | tf_op jit(solution)/shard_map/all_to_all | solution.py:213
  66.0 8.6 %collective-permute-start.26 = (bf16[64,2048]{1,0:T(8,128)(2,1)}, bf16[64,2048]{1,0:T(8,128)(2,1)}, u32[]{:S(2)}, u32[]{:S(2)}) collective-permute-start(bf16[64,2048]{1,0:T(8,128)(2,1)} %slice.100), channel_id=1, source_target_pairs={{0,2},{1,3},{2,0},{3,1},{4,6},{5,7},{6,4},{7,5},{8,10},{9,11},{10,... | collective-permute-start | bytes 786440 | tf_op jit(solution)/shard_map/ppermute | solution.py:20
  67.6 8.4 %collective-permute-start.27 = (bf16[64,2048]{1,0:T(8,128)(2,1)}, bf16[64,2048]{1,0:T(8,128)(2,1)}, u32[]{:S(2)}, u32[]{:S(2)}) collective-permute-start(bf16[64,2048]{1,0:T(8,128)(2,1)} %slice.101), channel_id=1, source_target_pairs={{0,4},{1,5},{2,6},{3,7},{4,0},{5,1},{6,2},{7,3},{8,12},{9,13},{10,... | collective-permute-start | bytes 786440 | tf_op jit(solution)/shard_map/ppermute | solution.py:20
  74.6 38.5 %collective-permute-start.7 = (bf16[768,256]{1,0:T(8,128)(2,1)S(1)}, bf16[768,256]{1,0:T(8,128)(2,1)S(1)}, u32[]{:S(2)}, u32[]{:S(2)}) collective-permute-start(bf16[768,256]{1,0:T(8,128)(2,1)S(1)} %copy-done.8), channel_id=1, source_target_pairs={{0,1},{1,0},{2,3},{3,2},{4,5},{5,4},{6,7},{7,6},{8,9},{9,8},{10,11... | collective-permute-start | bytes 1179656 | tf_op jit(solution)/shard_map/ppermute | solution.py:20
  76.0 39.6 %collective-permute-start.9 = (bf16[768,256]{1,0:T(8,128)(2,1)}, bf16[768,256]{1,0:T(8,128)(2,1)S(1)}, u32[]{:S(2)}, u32[]{:S(2)}) collective-permute-start(bf16[768,256]{1,0:T(8,128)(2,1)} %copy-done.9), channel_id=1, source_target_pairs={{0,1},{1,0},{2,3},{3,2},{4,5},{5,4},{6,7},{7,6},{8,9},{9,8},{10,11... | collective-permute-start | bytes 1179656 | tf_op jit(solution)/shard_map/ppermute | solution.py:20
  76.0 16.7 %collective-permute-start.17 = (bf16[64,2048]{1,0:T(8,128)(2,1)S(1)}, bf16[64,2048]{1,0:T(8,128)(2,1)S(1)}, u32[]{:S(2)}, u32[]{:S(2)}) collective-permute-start(bf16[64,2048]{1,0:T(8,128)(2,1)S(1)} %slice.98), channel_id=1, source_target_pairs={{0,2},{1,3},{2,0},{3,1},{4,6},{5,7},{6,4},{7,5},{8,10},{9,11},{10,... | collective-permute-start | bytes 786440 | tf_op jit(solution)/shard_map/ppermute | solution.py:20
  76.8 17.2 %collective-permute-start.18 = (bf16[64,2048]{1,0:T(8,128)(2,1)S(1)}, bf16[64,2048]{1,0:T(8,128)(2,1)S(1)}, u32[]{:S(2)}, u32[]{:S(2)}) collective-permute-start(bf16[64,2048]{1,0:T(8,128)(2,1)S(1)} %slice.99), channel_id=1, source_target_pairs={{0,4},{1,5},{2,6},{3,7},{4,0},{5,1},{6,2},{7,3},{8,12},{9,13},{10,... | collective-permute-start | bytes 786440 | tf_op jit(solution)/shard_map/ppermute | solution.py:20
  78.3 17.7 %collective-permute-start.34 = (bf16[128,2048]{1,0:T(8,128)(2,1)}, bf16[128,2048]{1,0:T(8,128)(2,1)S(1)}, u32[]{:S(2)}, u32[]{:S(2)}) collective-permute-start(bf16[128,2048]{1,0:T(8,128)(2,1)} %collective-permute-done.32.refs_0_), channel_id=1, source_target_pairs={{0,4},{1,5},{2,6},{3,7},{4,0},{5,1},{6,2},{7,3},{8,12},{9,13},{10,... | collective-permute-start | bytes 1572872 | tf_op jit(solution)/shard_map/ppermute | solution.py:20
  92.7 22.0 %collective-permute-start.2 = (bf16[64,2048]{1,0:T(8,128)(2,1)S(1)}, bf16[64,2048]{1,0:T(8,128)(2,1)S(1)}, u32[]{:S(2)}, u32[]{:S(2)}) collective-permute-start(bf16[64,2048]{1,0:T(8,128)(2,1)S(1)} %slice.96), channel_id=1, source_target_pairs={{0,2},{1,3},{2,0},{3,1},{4,6},{5,7},{6,4},{7,5},{8,10},{9,11},{10,... | collective-permute-start | bytes 786440 | tf_op jit(solution)/shard_map/ppermute | solution.py:20
  94.0 21.3 %collective-permute-start.3 = (bf16[64,2048]{1,0:T(8,128)(2,1)S(1)}, bf16[64,2048]{1,0:T(8,128)(2,1)S(1)}, u32[]{:S(2)}, u32[]{:S(2)}) collective-permute-start(bf16[64,2048]{1,0:T(8,128)(2,1)S(1)} %slice.97), channel_id=1, source_target_pairs={{0,4},{1,5},{2,6},{3,7},{4,0},{5,1},{6,2},{7,3},{8,12},{9,13},{10,... | collective-permute-start | bytes 786440 | tf_op jit(solution)/shard_map/ppermute | solution.py:20
  96.0 15.4 %collective-permute-start.33 = (bf16[128,2048]{1,0:T(8,128)(2,1)}, bf16[128,2048]{1,0:T(8,128)(2,1)S(1)}, u32[]{:S(2)}, u32[]{:S(2)}) collective-permute-start(bf16[128,2048]{1,0:T(8,128)(2,1)} %collective-permute-done.32.refs_0_), channel_id=1, source_target_pairs={{0,2},{1,3},{2,0},{3,1},{4,6},{5,7},{6,4},{7,5},{8,10},{9,11},{10,... | collective-permute-start | bytes 1572872 | tf_op jit(solution)/shard_map/ppermute | solution.py:20
  111.5 18.3 %collective-permute-start.35 = (bf16[64,2048]{1,0:T(8,128)(2,1)S(1)}, bf16[64,2048]{1,0:T(8,128)(2,1)S(1)}, u32[]{:S(2)}, u32[]{:S(2)}) collective-permute-start(bf16[64,2048]{1,0:T(8,128)(2,1)S(1)} %slice.102), channel_id=1, source_target_pairs={{0,2},{1,3},{2,0},{3,1},{4,6},{5,7},{6,4},{7,5},{8,10},{9,11},{10,... | collective-permute-start | bytes 786440 | tf_op jit(solution)/shard_map/ppermute | solution.py:20
  113.2 18.2 %collective-permute-start.36 = (bf16[64,2048]{1,0:T(8,128)(2,1)S(1)}, bf16[64,2048]{1,0:T(8,128)(2,1)S(1)}, u32[]{:S(2)}, u32[]{:S(2)}) collective-permute-start(bf16[64,2048]{1,0:T(8,128)(2,1)S(1)} %slice.103), channel_id=1, source_target_pairs={{0,4},{1,5},{2,6},{3,7},{4,0},{5,1},{6,2},{7,3},{8,12},{9,13},{10,... | collective-permute-start | bytes 786440 | tf_op jit(solution)/shard_map/ppermute | solution.py:20
  114.7 27.6 %collective-permute-start.30 = (bf16[64,2048]{1,0:T(8,128)(2,1)S(1)}, bf16[64,2048]{1,0:T(8,128)(2,1)S(1)}, u32[]{:S(2)}, u32[]{:S(2)}) collective-permute-start(bf16[64,2048]{1,0:T(8,128)(2,1)S(1)} %get-tuple-element.45), channel_id=1, source_target_pairs={{0,2},{1,3},{2,0},{3,1},{4,6},{5,7},{6,4},{7,5},{8,10},{9,11},{10,... | collective-permute-start | bytes 786440 | tf_op jit(solution)/shard_map/ppermute | solution.py:20
  115.3 28.0 %collective-permute-start.28 = (bf16[64,2048]{1,0:T(8,128)(2,1)S(1)}, bf16[64,2048]{1,0:T(8,128)(2,1)S(1)}, u32[]{:S(2)}, u32[]{:S(2)}) collective-permute-start(bf16[64,2048]{1,0:T(8,128)(2,1)S(1)} %get-tuple-element.43), channel_id=1, source_target_pairs={{0,4},{1,5},{2,6},{3,7},{4,0},{5,1},{6,2},{7,3},{8,12},{9,13},{10,... | collective-permute-start | bytes 786440 | tf_op jit(solution)/shard_map/ppermute | solution.py:20
  115.6 29.0 %collective-permute-start.21 = (bf16[64,2048]{1,0:T(8,128)(2,1)S(1)}, bf16[64,2048]{1,0:T(8,128)(2,1)S(1)}, u32[]{:S(2)}, u32[]{:S(2)}) collective-permute-start(bf16[64,2048]{1,0:T(8,128)(2,1)S(1)} %get-tuple-element.40), channel_id=1, source_target_pairs={{0,2},{1,3},{2,0},{3,1},{4,6},{5,7},{6,4},{7,5},{8,10},{9,11},{10,... | collective-permute-start | bytes 786440 | tf_op jit(solution)/shard_map/ppermute | solution.py:20
  129.8 29.1 %collective-permute-start.19 = (bf16[64,2048]{1,0:T(8,128)(2,1)S(1)}, bf16[64,2048]{1,0:T(8,128)(2,1)S(1)}, u32[]{:S(2)}, u32[]{:S(2)}) collective-permute-start(bf16[64,2048]{1,0:T(8,128)(2,1)S(1)} %get-tuple-element.38), channel_id=1, source_target_pairs={{0,4},{1,5},{2,6},{3,7},{4,0},{5,1},{6,2},{7,3},{8,12},{9,13},{10,... | collective-permute-start | bytes 786440 | tf_op jit(solution)/shard_map/ppermute | solution.py:20
  131.3 39.5 %collective-permute-start.12 = (bf16[64,2048]{1,0:T(8,128)(2,1)S(1)}, bf16[64,2048]{1,0:T(8,128)(2,1)S(1)}, u32[]{:S(2)}, u32[]{:S(2)}) collective-permute-start(bf16[64,2048]{1,0:T(8,128)(2,1)S(1)} %get-tuple-element.35), channel_id=1, source_target_pairs={{0,2},{1,3},{2,0},{3,1},{4,6},{5,7},{6,4},{7,5},{8,10},{9,11},{10,... | collective-permute-start | bytes 786440 | tf_op jit(solution)/shard_map/ppermute | solution.py:20
  142.3 45.4 %collective-permute-start.10 = (bf16[64,2048]{1,0:T(8,128)(2,1)S(1)}, bf16[64,2048]{1,0:T(8,128)(2,1)S(1)}, u32[]{:S(2)}, u32[]{:S(2)}) collective-permute-start(bf16[64,2048]{1,0:T(8,128)(2,1)S(1)} %get-tuple-element.33), channel_id=1, source_target_pairs={{0,4},{1,5},{2,6},{3,7},{4,0},{5,1},{6,2},{7,3},{8,12},{9,13},{10,... | collective-permute-start | bytes 786440 | tf_op jit(solution)/shard_map/ppermute | solution.py:20
  143.3 6.4 %collective-permute-start.39 = (bf16[64,2048]{1,0:T(8,128)(2,1)S(1)}, bf16[64,2048]{1,0:T(8,128)(2,1)S(1)}, u32[]{:S(2)}, u32[]{:S(2)}) collective-permute-start(bf16[64,2048]{1,0:T(8,128)(2,1)S(1)} %get-tuple-element.50), channel_id=1, source_target_pairs={{0,2},{1,3},{2,0},{3,1},{4,6},{5,7},{6,4},{7,5},{8,10},{9,11},{10,... | collective-permute-start | bytes 786440 | tf_op jit(solution)/shard_map/ppermute | solution.py:20
  144.6 12.7 %collective-permute-start.37 = (bf16[64,2048]{1,0:T(8,128)(2,1)S(1)}, bf16[64,2048]{1,0:T(8,128)(2,1)S(1)}, u32[]{:S(2)}, u32[]{:S(2)}) collective-permute-start(bf16[64,2048]{1,0:T(8,128)(2,1)S(1)} %get-tuple-element.48), channel_id=1, source_target_pairs={{0,4},{1,5},{2,6},{3,7},{4,0},{5,1},{6,2},{7,3},{8,12},{9,13},{10,... | collective-permute-start | bytes 786440 | tf_op jit(solution)/shard_map/ppermute | solution.py:20
  149.8 18.7 %collective-permute-start.40 = (bf16[128,2048]{1,0:T(8,128)(2,1)S(1)}, bf16[128,2048]{1,0:T(8,128)(2,1)S(1)}, u32[]{:S(2)}, u32[]{:S(2)}) collective-permute-start(bf16[128,2048]{1,0:T(8,128)(2,1)S(1)} %pad_maximum_fusion.7), channel_id=1, source_target_pairs={{0,4},{1,5},{2,6},{3,7},{4,0},{5,1},{6,2},{7,3},{8,12},{9,13},{10,... | collective-permute-start | bytes 1572872 | tf_op jit(solution)/shard_map/ppermute | solution.py:20
  157.4 13.2 %collective-permute-start.38 = (bf16[128,2048]{1,0:T(8,128)(2,1)S(1)}, bf16[128,2048]{1,0:T(8,128)(2,1)S(1)}, u32[]{:S(2)}, u32[]{:S(2)}) collective-permute-start(bf16[128,2048]{1,0:T(8,128)(2,1)S(1)} %pad_maximum_fusion.6), channel_id=1, source_target_pairs={{0,2},{1,3},{2,0},{3,1},{4,6},{5,7},{6,4},{7,5},{8,10},{9,11},{10,... | collective-permute-start | bytes 1572872 | tf_op jit(solution)/shard_map/ppermute | solution.py:20
  158.9 20.8 %collective-permute-start.31 = (bf16[128,2048]{1,0:T(8,128)(2,1)S(1)}, bf16[128,2048]{1,0:T(8,128)(2,1)S(1)}, u32[]{:S(2)}, u32[]{:S(2)}) collective-permute-start(bf16[128,2048]{1,0:T(8,128)(2,1)S(1)} %pad_maximum_fusion.5), channel_id=1, source_target_pairs={{0,4},{1,5},{2,6},{3,7},{4,0},{5,1},{6,2},{7,3},{8,12},{9,13},{10,... | collective-permute-start | bytes 1572872 | tf_op jit(solution)/shard_map/ppermute | solution.py:20
  168.5 13.3 %collective-permute-start.29 = (bf16[128,2048]{1,0:T(8,128)(2,1)S(1)}, bf16[128,2048]{1,0:T(8,128)(2,1)S(1)}, u32[]{:S(2)}, u32[]{:S(2)}) collective-permute-start(bf16[128,2048]{1,0:T(8,128)(2,1)S(1)} %pad_maximum_fusion.4), channel_id=1, source_target_pairs={{0,2},{1,3},{2,0},{3,1},{4,6},{5,7},{6,4},{7,5},{8,10},{9,11},{10,... | collective-permute-start | bytes 1572872 | tf_op jit(solution)/shard_map/ppermute | solution.py:20
  170.6 20.4 %collective-permute-start.22 = (bf16[128,2048]{1,0:T(8,128)(2,1)S(1)}, bf16[128,2048]{1,0:T(8,128)(2,1)S(1)}, u32[]{:S(2)}, u32[]{:S(2)}) collective-permute-start(bf16[128,2048]{1,0:T(8,128)(2,1)S(1)} %pad_maximum_fusion.3), channel_id=1, source_target_pairs={{0,4},{1,5},{2,6},{3,7},{4,0},{5,1},{6,2},{7,3},{8,12},{9,13},{10,... | collective-permute-start | bytes 1572872 | tf_op jit(solution)/shard_map/ppermute | solution.py:20
  170.8 13.2 %collective-permute-start.41 = (bf16[128,2048]{1,0:T(8,128)(2,1)S(1)}, bf16[128,2048]{1,0:T(8,128)(2,1)S(1)}, u32[]{:S(2)}, u32[]{:S(2)}) collective-permute-start(bf16[128,2048]{1,0:T(8,128)(2,1)S(1)} %add_convert_fusion.3), channel_id=1, source_target_pairs={{0,16},{1,17},{2,18},{3,19},{4,20},{5,21},{6,22},{7,23},{8,0},{9,1... | collective-permute-start | bytes 1572872 | tf_op jit(solution)/shard_map/ppermute | solution.py:20
  179.7 14.9 %collective-permute-start.20 = (bf16[128,2048]{1,0:T(8,128)(2,1)S(1)}, bf16[128,2048]{1,0:T(8,128)(2,1)S(1)}, u32[]{:S(2)}, u32[]{:S(2)}) collective-permute-start(bf16[128,2048]{1,0:T(8,128)(2,1)S(1)} %pad_maximum_fusion.2), channel_id=1, source_target_pairs={{0,2},{1,3},{2,0},{3,1},{4,6},{5,7},{6,4},{7,5},{8,10},{9,11},{10,... | collective-permute-start | bytes 1572872 | tf_op jit(solution)/shard_map/ppermute | solution.py:20
  181.8 21.5 %collective-permute-start.13 = (bf16[128,2048]{1,0:T(8,128)(2,1)S(1)}, bf16[128,2048]{1,0:T(8,128)(2,1)S(1)}, u32[]{:S(2)}, u32[]{:S(2)}) collective-permute-start(bf16[128,2048]{1,0:T(8,128)(2,1)S(1)} %pad_maximum_fusion.1), channel_id=1, source_target_pairs={{0,4},{1,5},{2,6},{3,7},{4,0},{5,1},{6,2},{7,3},{8,12},{9,13},{10,... | collective-permute-start | bytes 1572872 | tf_op jit(solution)/shard_map/ppermute | solution.py:20
  184.4 15.1 %collective-permute-start.42 = (bf16[128,2048]{1,0:T(8,128)(2,1)S(1)}, bf16[128,2048]{1,0:T(8,128)(2,1)S(1)}, u32[]{:S(2)}, u32[]{:S(2)}) collective-permute-start(bf16[128,2048]{1,0:T(8,128)(2,1)S(1)} %add_convert_fusion.2), channel_id=1, source_target_pairs={{0,16},{1,17},{2,18},{3,19},{4,20},{5,21},{6,22},{7,23},{8,0},{9,1... | collective-permute-start | bytes 1572872 | tf_op jit(solution)/shard_map/ppermute | solution.py:20
  187.8 15.5 %collective-permute-start.11 = (bf16[128,2048]{1,0:T(8,128)(2,1)S(1)}, bf16[128,2048]{1,0:T(8,128)(2,1)S(1)}, u32[]{:S(2)}, u32[]{:S(2)}) collective-permute-start(bf16[128,2048]{1,0:T(8,128)(2,1)S(1)} %pad_maximum_fusion), channel_id=1, source_target_pairs={{0,2},{1,3},{2,0},{3,1},{4,6},{5,7},{6,4},{7,5},{8,10},{9,11},{10,... | collective-permute-start | bytes 1572872 | tf_op jit(solution)/shard_map/ppermute | solution.py:20
  199.8 10.1 %collective-permute-start.43 = (bf16[128,2048]{1,0:T(8,128)(2,1)S(1)}, bf16[128,2048]{1,0:T(8,128)(2,1)S(1)}, u32[]{:S(2)}, u32[]{:S(2)}) collective-permute-start(bf16[128,2048]{1,0:T(8,128)(2,1)S(1)} %add_convert_fusion.1), channel_id=1, source_target_pairs={{0,16},{1,17},{2,18},{3,19},{4,20},{5,21},{6,22},{7,23},{8,0},{9,1... | collective-permute-start | bytes 1572872 | tf_op jit(solution)/shard_map/ppermute | solution.py:20
  (8 other events, 61.9 us)

commit v3 on v0

--- a/solution.py
+++ b/solution.py
@@ -1,7 +1,274 @@
+import functools
+
 import jax
 import jax.numpy as jnp
 from jax import lax
+from jax.experimental import pallas as pl
+from jax.experimental.pallas import tpu as pltpu
 from jax.sharding import PartitionSpec as P
+
+BOTH = ("expert", "dp")
+bf16, f32 = jnp.bfloat16, jnp.float32
+
+
+def moved(array, step):
+    pairs = []
+    for device in range(32):
+        z, y, x, core = device // 8, device // 4 % 2, device // 2 % 2, device % 2
+        z, y, x, core = step(z, y, x, core)
+        pairs.append((device, ((z * 2 + y) * 2 + x) * 2 + core))
+    return lax.ppermute(array, BOTH, pairs)
+
+
+def to_x(z, y, x, core):
+    return z, y, 1 - x, core
+
+
+def to_y(z, y, x, core):
+    return z, 1 - y, x, core
+
+
+def ring_on(z, y, x, core):
+    return (1, 3, 0, 2)[z], y, x, core
+
+
+def ring_back(z, y, x, core):
+    return (2, 0, 3, 1)[z], y, x, core
+
+
+def silu(v):
+    return v / (1.0 + jnp.exp(-v))
+
+
+def widen(tokens_ref, ids_ref, weight_ref, wide_ref):
+    rows, width = tokens_ref.shape
+    wide_ref[:, :width] = tokens_ref[...]
+    lanes = wide_ref.shape[1] - width
+    expert = lax.broadcasted_iota(jnp.int32, (lanes, rows), 0)
+    dense = jnp.zeros((lanes, rows), f32)
+    weights = weight_ref[...].astype(f32)
+    for k in range(ids_ref.shape[0]):
+        dense = jnp.where(ids_ref[k : k + 1, :] == expert, weights[k : k + 1, :], dense)
+    wide_ref[:, width:] = dense.T.astype(bf16)
+
+
+def share(up_ref, down_ref, own_ref, sent_ref):
+    depth, both = up_ref.shape
+    feature = both // 8
+    half_out = down_ref.shape[1] // 2
+    plane = lax.axis_index("expert") % 2 * 2
+    x = lax.axis_index("dp") // 2
+    for ref, place in ((own_ref, plane + x), (sent_ref, plane + 1 - x)):
+        start = pl.multiple_of(place * feature, feature)
+        ref[:depth, :feature] = up_ref[:, pl.ds(start, feature)]
+        up_start = pl.multiple_of(both // 2 + start, feature)
+        ref[:depth, feature:] = up_ref[:, pl.ds(up_start, feature)]
+        for side in range(2):
+            ref[depth + side * feature : depth + (side + 1) * feature, :] = down_ref[
+                pl.ds(start, feature), side * half_out : (side + 1) * half_out
+            ]
+
+
+def feed(shared, count, *refs):
+    parts, rest = refs[:count], refs[count:]
+    (gate_hbm, up_hbm, down_hbm), rest = rest[:3], rest[3:]
+    if shared:
+        (own, far, switch_ref), rest = rest[:3], rest[3:]
+    outs, (rows_ref, scale_ref, hidden_ref, base, gate_ref, up_ref, down_ref, sems) = rest[:-8], rest[-8:]
+    rows, width = rows_ref.shape
+    step = pl.program_id(0)
+    cut = gate_ref.shape[2]
+
+    def tile_copies(index, which, side):
+        columns = pl.ds(pl.multiple_of(side * cut, cut), cut)
+        return (
+            pltpu.make_async_copy(gate_hbm.at[which, 0, :, columns], gate_ref.at[index], sems.at[0, index]),
+            pltpu.make_async_copy(up_hbm.at[which, 0, :, columns], up_ref.at[index], sems.at[1, index]),
+        )
+
+    def down_copies():
+        return [
+            pltpu.make_async_copy(down_hbm.at[which, 0], down_ref.at[which], sems.at[2, which]) for which in range(2)
+        ]
+
+    @pl.when(step == 0)
+    def _():
+        for index in range(4):
+            for copy in tile_copies(index, index // 2, index % 2):
+                copy.start()
+        for copy in down_copies():
+            copy.start()
+        chip = lax.axis_index("expert") * 2 + lax.axis_index("dp") // 2
+        start = 0
+        for ref in parts:
+            span = slice(start, start + ref.shape[0])
+            start += ref.shape[0]
+            rows_ref[span] = ref[:, :width]
+            weight = ref[:, width:].astype(f32)
+            expert = lax.broadcasted_iota(jnp.int32, weight.shape, 1)
+            for which in range(2):
+                chosen = jnp.where(expert == chip * 2 + which, weight, 0.0)
+                scale_ref[which, span] = jnp.sum(chosen, axis=1, keepdims=True)
+        if shared:
+            x = lax.axis_index("dp") // 2
+            depth = width // 4
+            feature = own.shape[2] // 2
+            both = jnp.zeros((rows, 2 * feature), f32)
+            turn = jnp.zeros((rows, 1), f32)
+            pieces = [(ref.at[core], (x ^ across) * 2 + core) for across, ref in enumerate((own, far)) for core in range(2)]
+            for j, (piece, place) in enumerate(pieces):
+                start = pl.multiple_of(place * depth, depth)
+                both += jnp.dot(rows_ref[:, pl.ds(start, depth)], piece[:depth], preferred_element_type=f32)
+                fixed = slice(j * depth, (j + 1) * depth)
+                turn += jnp.sum(
+                    rows_ref[:, fixed].astype(f32) * switch_ref[:, fixed].astype(f32), axis=1, keepdims=True
+                )
+            hidden = (silu(both[:, :feature]) * both[:, feature:]).astype(bf16)
+            turn = 1.0 / (1.0 + jnp.exp(-turn))
+            for piece, place in pieces:
+                for side in range(2):
+                    start = pl.multiple_of(place * depth + side * (depth // 2), depth // 2)
+                    part = piece[depth + side * feature : depth + (side + 1) * feature]
+                    base[:, pl.ds(start, depth // 2)] = turn * jnp.dot(hidden, part, preferred_element_type=f32)
+
+    for copy in tile_copies(step, step // 2, step % 2):
+        copy.wait()
+    gate = jnp.dot(rows_ref[...], gate_ref[step], preferred_element_type=f32)
+    upper = jnp.dot(rows_ref[...], up_ref[step], preferred_element_type=f32)
+    hidden_ref[step] = (silu(gate) * upper).astype(bf16)
+
+    @pl.when(step == 3)
+    def _():
+        for copy in down_copies():
+            copy.wait()
+        span = 512
+        for start in range(0, width, span):
+            columns = slice(start, start + span)
+            total = base[:, columns] if shared else 0.0
+            for which in range(2):
+                answer = jnp.dot(hidden_ref[2 * which], down_ref[which, :cut, columns], preferred_element_type=f32)
+                answer += jnp.dot(hidden_ref[2 * which + 1], down_ref[which, cut:, columns], preferred_element_type=f32)
+                total = total + scale_ref[which] * answer
+            total = total.astype(bf16)
+            first = 0
+            for ref in outs:
+                ref[:, columns] = total[first : first + ref.shape[0]]
+                first += ref.shape[0]
+
+
+def whole(array):
+    return pl.BlockSpec(array.shape, lambda i: (0,) * array.ndim)
+
+
+def run_feed(parts, cuts, experts, extra):
+    hidden, width = experts[2].shape[2:]
+    rows, cut = sum(cuts), hidden // 2
+    outs = [jax.ShapeDtypeStruct((n, width), bf16) for n in cuts]
+    return pl.pallas_call(
+        functools.partial(feed, bool(extra), len(parts)),
+        grid=(4,),
+        in_specs=[whole(p) for p in parts]
+        + [pl.BlockSpec(memory_space=pltpu.HBM)] * 3
+        + [whole(e) for e in extra],
+        out_specs=[whole(o) for o in outs],
+        out_shape=outs,
+        scratch_shapes=[
+            pltpu.VMEM((rows, width), bf16),
+            pltpu.VMEM((2, rows, 1), f32),
+            pltpu.VMEM((4, rows, cut), bf16),
+            pltpu.VMEM((rows, width) if extra else (8, 128), f32),
+            pltpu.VMEM((4, width, cut), bf16),
+            pltpu.VMEM((4, width, cut), bf16),
+            pltpu.VMEM((2, hidden, width), bf16),
+            pltpu.SemaphoreType.DMA((3, 4)),
+        ],
+        compiler_params=pltpu.CompilerParams(vmem_limit_bytes=28 * 1024 * 1024),
+        cost_estimate=pl.CostEstimate(
+            flops=2 * rows * width * hidden * 6, bytes_accessed=16 * 2**20, transcendentals=rows * hidden * 2
+        ),
+    )(*parts, *experts, *extra)
+
+
+def summed(*terms):
+    return sum(term.astype(f32) for term in terms).astype(bf16)
+
+
+def top_added(array, top):
+    half = top.shape[0]
+    return jnp.concatenate([array[:half].astype(f32) + top.astype(f32), array[half:].astype(f32)]).astype(bf16)
+
+
+def low_added(array, low):
+    half = low.shape[0]
+    return jnp.concatenate([array[:half].astype(f32), array[half:].astype(f32) + low.astype(f32)]).astype(bf16)
+
+
+def blocks(
+    tokens,
+    expert_ids,
+    route_weight,
+    expert_gate,
+    expert_up,
+    expert_down,
+    shared_gate_up,
+    shared_down,
+    shared_switch,
+):
+    rows, width = tokens.shape
+    half = rows // 2
+    depth, both = shared_gate_up.shape
+    feature = both // 8
+    wide = pl.pallas_call(
+        widen,
+        out_shape=jax.ShapeDtypeStruct((rows, width + 128), bf16),
+    )(tokens, expert_ids.T, route_weight.T)
+    piece_shape = jax.ShapeDtypeStruct((depth + 2 * feature, 2 * feature), bf16)
+    own, sent = pl.pallas_call(share, out_shape=[piece_shape, piece_shape])(shared_gate_up, shared_down)
+    cores = [[0, 1], [2, 3]]
+
+    def paired(part):
+        return lax.all_gather(part, "dp", axis_index_groups=cores)
+
+    experts = [paired(part) for part in (expert_gate, expert_up, expert_down)]
+    on_x = on_y = on_z = moved
+
+    first = on_z(wide, ring_on)
+    x0, y0 = on_x(wide, to_x), on_y(wide, to_y)
+    second = on_z(first, ring_on)
+    top, low = on_x(y0[:half], to_x), on_y(x0[half:], to_y)
+    corner0 = jnp.concatenate([top, low])
+    x1, y1 = on_x(first, to_x), on_y(first, to_y)
+    corner1 = on_z(corner0, ring_on)
+    third = on_z(wide, ring_back)
+    x2, y2 = on_x(second, to_x), on_y(second, to_y)
+    corner2 = on_z(corner1, ring_on)
+    far = on_x(sent, to_x)
+    x3, y3 = on_x(third, to_x), on_y(third, to_y)
+    top, low = on_x(y3[:half], to_x), on_y(x3[half:], to_y)
+    full, halves = (rows,) * 4, (rows,) * 3 + (half,) * 2
+    partial1 = run_feed((first, x1, y1, corner1), full, experts, ())
+    partial2 = run_feed((second, x2, y2, corner2), halves, experts, ())
+    partial3 = run_feed((third, x3, y3, top, low), halves, experts, ())
+    extra = (paired(own), paired(far), shared_switch.reshape(1, width))
+    partial0 = run_feed((wide, x0, y0, corner0), full, experts, extra)
+
+    def straight(here, along_x, along_y):
+        return here, on_x(along_x, to_x), on_y(along_y, to_y)
+
+    def in_plane(here, along_x, along_y, top, low):
+        top, low = on_x(top, to_x), on_y(low, to_y)
+        return straight(here, low_added(along_x, low), top_added(along_y, top))
+
+    plane1 = straight(*partial1[:3])
+    corner = on_z(partial1[3], ring_back)
+    plane2 = in_plane(*partial2)
+    second = on_z(summed(*plane2), ring_back)
+    plane3 = in_plane(*partial3)
+    first = on_z(summed(*plane1, second), ring_back)
+    third = on_z(summed(*plane3), ring_on)
+    corner = summed(partial0[3], corner)
+    plane0 = in_plane(*partial0[:3], corner[:half], corner[half:])
+    return summed(*plane0, first, third)
 
 
 def shards(
@@ -86,4 +353,5 @@
         P(),
     )
     out_specs = P(("groups", "expert", "dp"), None)
-    return jax.shard_map(shards, mesh=mesh, in_specs=in_specs, out_specs=out_specs, check_vma=False)
+    part = blocks if (mesh.shape["expert"], mesh.shape["dp"]) == (8, 4) else shards
+    return jax.shard_map(part, mesh=mesh, in_specs=in_specs, out_specs=out_specs, check_vma=False)

time: 427 us -> 201 us (0.47)
  waiting for transfers between devices: 277 us -> 79.3 us
  local copies, waits for them, and re-layouts: 70 us -> 10.6 us
  Pallas kernels: 0 us -> 44.8 us
  matrix products: 32.2 us -> 0 us
  starting transfers between devices: 17.3 us -> 44.8 us
  other arithmetic: 16.1 us -> 2.78 us
  blocking collectives: 0 us -> 4.94 us
    all_to_all x3 -> x0, waiting for transfers between devices: 190 us -> none  [the longest x1 140 us: shards(): lax.all_to_all(outgoing, ('expert', 'dp'), split_axis=0, concat_axis=0, t...]
    all_gather x2 -> x3, waiting for transfers between devices: 85.8 us -> 0.02 us  [paired(): return lax.all_gather(part, 'dp', axis_index_groups=cores)]
    ppermute x0 -> x36, waiting for transfers between devices: none -> 77.2 us  [moved(): return lax.ppermute(array, BOTH, pairs)]
    pallas_call x0 -> x6, Pallas kernels: none -> 44.8 us  [the longest x4 40.4 us: run_feed(): pl.pallas_call(functools.partial(feed, bool(extra), len(parts)), grid=(4,...]
    ppermute x0 -> x36, starting transfers between devices: none -> 44.7 us  [moved(): return lax.ppermute(array, BOTH, pairs)]
    dot_general x5 -> x0, matrix products: 32.2 us -> none  [the longest x1 11.7 us: shards(): answer = jnp.dot(hidden, expert_down[0], preferred_element_type=jnp.float32)]
    gather x3 -> x0, local copies, waits for them, and re-layouts: 31 us -> none  [the longest x1 14.4 us: shards(): gathered = returned[slot_index].reshape(tok_count, top_count, width)]
    slice x3 -> x11, local copies, waits for them, and re-layouts: 20.8 us -> 0.23 us  [the longest x3 0.06 us: top_added(): array[half:].astype(f32)]
  transfers between devices with their start and end apart: 5 -> 39, of which waited for: 3 -> 12; matrix products, arithmetic and copies ran while one was open for 14% -> 1% of each run, Pallas kernels for 0% -> 22%
where the time goes in v3:
time: 201 us
  waiting for transfers between devices  79.3 us (39%)
  starting transfers between devices  44.8 us (22%)
  Pallas kernels  44.8 us (22%)
  between operations  13.5 us (7%)
  local copies, waits for them, and re-layouts  10.6 us (5%)
  blocking collectives  4.94 us (2%)
  other arithmetic  2.78 us (1%)
    ppermute x36, waiting for transfers between devices, moved(): return lax.ppermute(array, BOTH, pairs)  77.2 us
    ppermute x36, starting transfers between devices, moved(): return lax.ppermute(array, BOTH, pairs)  44.7 us
    pallas_call x4, Pallas kernels, run_feed(): pl.pallas_call(functools.partial(feed, bool(extra), len(parts)), grid=(4,...  40.4 us
    unnamed x27, local copies, waits for them, and re-layouts  10.4 us
    all_gather x2, blocking collectives, paired(): return lax.all_gather(part, 'dp', axis_index_groups=cores)  4.94 us
  transfers between devices with their start and end apart: 39, of which 12 were waited for; matrix products, arithmetic and copies ran while one was open for 1% of the time, Pallas kernels for 22%

profile of v3, /device:TPU:0, one launch (start us, length us, event | category | flops | bytes accessed | tf_op | source)
XLA Modules:
  0.0 200.7 jit_solution(11920086131488246238)
XLA Ops:
  8.8 2.0 shard_map.91.refs_0_
  10.7 3.0 %collective-permute-start.1 = (bf16[128,2176]{1,0:T(8,128)(2,1)}, bf16[128,2176]{1,0:T(8,128)(2,1)S(1)}, u32[]{:S(2)}, u32[]{:S(2)}) collective-permute-start(bf16[128,2176]{1,0:T(8,128)(2,1)} %shard_map.91.refs_0_), channel_id=1, source_target_pairs={{0,4},{1,5},{2,6},{3,7},{4,0},{5,1},{6,2},{7,3},{8,12},{9,13},{10,... | collective-permute-start | bytes 1671176 | tf_op jit(solution)/shard_map/ppermute | solution.py:20
  13.7 1.5 collective-permute-start
  15.2 2.6 %collective-permute-start.26 = (bf16[128,2176]{1,0:T(8,128)(2,1)}, bf16[128,2176]{1,0:T(8,128)(2,1)S(1)}, u32[]{:S(2)}, u32[]{:S(2)}) collective-permute-start(bf16[128,2176]{1,0:T(8,128)(2,1)} %shard_map.91.refs_0_), channel_id=1, source_target_pairs={{0,16},{1,17},{2,18},{3,19},{4,20},{5,21},{6,22},{7,23},{8,0},{9,1... | collective-permute-start | bytes 1671176 | tf_op jit(solution)/shard_map/ppermute | solution.py:20
  17.8 8.7 %collective-permute-done.1.refs_2_ = bf16[128,2176]{1,0:T(8,128)(2,1)S(1)} collective-permute-done((bf16[128,2176]{1,0:T(8,128)(2,1)}, bf16[128,2176]{1,0:T(8,128)(2,1)S(1)}, u32[]{:S(2)}, u32[]{:S(2)}) %collective-permute-start.1) | collective-permute-done | bytes 557088 | tf_op jit(solution)/shard_map/ppermute | solution.py:20
  26.6 1.8 collective-permute-start.2
  28.3 2.4 %shard_map.92 = (bf16[768,256]{1,0:T(8,128)(2,1)}, bf16[768,256]{1,0:T(8,128)(2,1)}) custom-call(bf16[512,1024]{1,0:T(8,128)(2,1)} %up_ref.1, bf16[512,512]{1,0:T(8,128)(2,1)} %down_ref.1), custom_call_target="tpu_custom_call" | custom-call | tf_op jit(solution)/shard_map/pallas_call | solution.py:226
  31.1 1.8 collective-permute-start.3
  32.9 1.5 collective-permute-start.27
  34.4 8.8 %collective-permute-done.5.refs_0_ = bf16[128,2176]{1,0:T(8,128)(2,1)} collective-permute-done((bf16[128,2176]{1,0:T(8,128)(2,1)}, bf16[128,2176]{1,0:T(8,128)(2,1)}, u32[]{:S(2)}, u32[]{:S(2)}) %collective-permute-start.5) | collective-permute-done | bytes 557088 | tf_op jit(solution)/shard_map/ppermute | solution.py:20
  44.5 2.4 %collective-permute-start.8 = (bf16[128,2176]{1,0:T(8,128)(2,1)S(1)}, bf16[128,2176]{1,0:T(8,128)(2,1)}, u32[]{:S(2)}, u32[]{:S(2)}) collective-permute-start(bf16[128,2176]{1,0:T(8,128)(2,1)S(1)} %constant_dynamic-update-slice_fusion.refs_3_), channel_id=1, source_target_pairs={{0,8},{1,9},{2,10},{3,11},{4,12},{5,13},{6,14},{7,15},{8,24},{9,25... | collective-permute-start | bytes 1671176 | tf_op jit(solution)/shard_map/ppermute | solution.py:20
  46.8 10.9 %collective-permute-done.28.refs_2_ = bf16[128,2176]{1,0:T(8,128)(2,1)S(1)} collective-permute-done((bf16[128,2176]{1,0:T(8,128)(2,1)S(1)}, bf16[128,2176]{1,0:T(8,128)(2,1)S(1)}, u32[]{:S(2)}, u32[]{:S(2)}) %collective-permute-start.28) | collective-permute-done | bytes 557088 | tf_op jit(solution)/shard_map/ppermute | solution.py:20
  59.0 2.6 %all-gather.3 = bf16[1536,256]{1,0:T(8,128)(2,1)S(1)} all-gather(bf16[768,256]{1,0:T(8,128)(2,1)} %get-tuple-element.25), channel_id=5, replica_groups={{0,1},{2,3},{4,5},{6,7},{8,9},{10,11},{12,13},{14,15},{16,17},{18,19},{..., dimensions={0}, use_global_device_ids=true | all-gather | bytes 1179648 | tf_op jit(solution)/shard_map/all_gather | solution.py:230
  61.6 2.4 %all-gather.4 = bf16[1536,256]{1,0:T(8,128)(2,1)S(1)} all-gather(bf16[768,256]{1,0:T(8,128)(2,1)S(1)} %collective-permute-done.4), channel_id=6, replica_groups={{0,1},{2,3},{4,5},{6,7},{8,9},{10,11},{12,13},{14,15},{16,17},{18,19},{..., dimensions={0}, use_global_device_ids=true | all-gather | bytes 1179648 | tf_op jit(solution)/shard_map/all_gather | solution.py:230
  63.9 1.5 collective-permute-start.6
  65.4 1.5 collective-permute-start.7
  68.7 2.4 %collective-permute-done.8.refs_3_ = bf16[128,2176]{1,0:T(8,128)(2,1)} collective-permute-done((bf16[128,2176]{1,0:T(8,128)(2,1)S(1)}, bf16[128,2176]{1,0:T(8,128)(2,1)}, u32[]{:S(2)}, u32[]{:S(2)}) %collective-permute-start.8) | collective-permute-done | bytes 557088 | tf_op jit(solution)/shard_map/ppermute | solution.py:20
  71.2 1.0 copy-done.2
  72.2 2.2 %copy-done.5 = bf16[2,2048,512]{2,1,0:T(8,128)(2,1)S(1)} copy-done((bf16[2,2048,512]{2,1,0:T(8,128)(2,1)S(1)}, bf16[2,2048,512]{2,1,0:T(8,128)(2,1)}, u32[]{:S(2)}) %copy-start.5) | copy-done | bytes 4194328
  74.4 2.2 %copy-done.6 = bf16[2,2048,512]{2,1,0:T(8,128)(2,1)S(1)} copy-done((bf16[2,2048,512]{2,1,0:T(8,128)(2,1)S(1)}, bf16[2,2048,512]{2,1,0:T(8,128)(2,1)}, u32[]{:S(2)}) %copy-start.6) | copy-done | bytes 4194328
  76.6 2.2 %copy-done.7 = bf16[2,512,2048]{2,1,0:T(8,128)(2,1)S(1)} copy-done((bf16[2,512,2048]{2,1,0:T(8,128)(2,1)S(1)}, bf16[2,512,2048]{2,1,0:T(8,128)(2,1)}, u32[]{:S(2)}) %copy-start.7) | copy-done | bytes 4194328
  78.8 1.1 copy-done.9
  79.8 1.0 copy-done.11
  80.8 8.7 %shard_map.96 = (bf16[128,2048]{1,0:T(8,128)(2,1)S(1)}, bf16[128,2048]{1,0:T(8,128)(2,1)S(1)}, bf16[128,2048]{1,0:T(8,128)(2,1)S(1)}, bf16[64,2048]{1,0:T(8,128)(2,1)S(1)}, bf16[64,2048]{1,0:T(8,128)(2,1)S(1)}) custom-call(bf16[128,2176]{1,0:T(8,128)(2,1)S(1)} %copy-done.9, bf16[128,2176]{1,0:T(8,128)(2,1)S(1)} %collective-permute-done.27.refs_1_, ...), custom_call_target="tpu_custom_call" | custom-call | flops 6442450944 | bytes 16777216 | tf_op jit(solution)/shard_map/pallas_call | solution.py:167
  89.6 1.3 collective-permute-done.17.refs_1_
  90.9 1.5 collective-permute-start.33
  92.4 1.5 collective-permute-start.31
  93.9 10.3 %shard_map.95 = (bf16[128,2048]{1,0:T(8,128)(2,1)S(1)}, bf16[128,2048]{1,0:T(8,128)(2,1)S(1)}, bf16[128,2048]{1,0:T(8,128)(2,1)S(1)}, bf16[64,2048]{1,0:T(8,128)(2,1)S(1)}, bf16[64,2048]{1,0:T(8,128)(2,1)S(1)}) custom-call(bf16[128,2176]{1,0:T(8,128)(2,1)} %collective-permute-done.16.refs_0_, bf16[128,2176]{1,0:T(8,128)(2,1)} %collective-permute-done.17.refs_1_, ...), custom_call_target="tpu_custom_call" | custom-call | flops 6442450944 | bytes 16777216 | tf_op jit(solution)/shard_map/pallas_call | solution.py:167
  105.4 10.3 %shard_map.94 = (bf16[128,2048]{1,0:T(8,128)(2,1)S(1)}, bf16[128,2048]{1,0:T(8,128)(2,1)S(1)}, bf16[128,2048]{1,0:T(8,128)(2,1)S(1)}, bf16[128,2048]{1,0:T(8,128)(2,1)S(1)}) custom-call(bf16[128,2176]{1,0:T(8,128)(2,1)} %collective-permute-done.5.refs_0_, bf16[128,2176]{1,0:T(8,128)(2,1)} %collective-permute-done.6.refs_1_, ...), custom_call_target="tpu_custom_call" | custom-call | flops 6442450944 | bytes 16777216 | tf_op jit(solution)/shard_map/pallas_call | solution.py:167
  115.8 1.6 collective-permute-start.15
  117.4 11.0 %shard_map.93 = (bf16[128,2048]{1,0:T(8,128)(2,1)S(1)}, bf16[128,2048]{1,0:T(8,128)(2,1)S(1)}, bf16[128,2048]{1,0:T(8,128)(2,1)S(1)}, bf16[128,2048]{1,0:T(8,128)(2,1)S(1)}) custom-call(bf16[128,2176]{1,0:T(8,128)(2,1)S(1)} %copy-done, bf16[128,2176]{1,0:T(8,128)(2,1)S(1)} %collective-permute-done.refs_1_, ...), custom_call_target="tpu_custom_call" | custom-call | flops 6442450944 | bytes 16777216 | tf_op jit(solution)/shard_map/pallas_call | solution.py:167
  128.5 1.7 collective-permute-start.9
  131.0 1.0 collective-permute-start.32
  132.1 1.2 collective-permute-start.23
  133.5 6.8 %collective-permute-done.9 = bf16[128,2048]{1,0:T(8,128)(2,1)S(1)} collective-permute-done((bf16[128,2048]{1,0:T(8,128)(2,1)S(1)}, bf16[128,2048]{1,0:T(8,128)(2,1)S(1)}, u32[]{:S(2)}, u32[]{:S(2)}) %collective-permute-start.9) | collective-permute-done | bytes 524320 | tf_op jit(solution)/shard_map/ppermute | solution.py:20
  140.3 1.5 collective-permute-start.21
  141.9 3.3 %collective-permute-done.34 = bf16[128,2048]{1,0:T(8,128)(2,1)S(1)} collective-permute-done((bf16[128,2048]{1,0:T(8,128)(2,1)S(1)}, bf16[128,2048]{1,0:T(8,128)(2,1)S(1)}, u32[]{:S(2)}, u32[]{:S(2)}) %collective-permute-start.34) | collective-permute-done | bytes 524320 | tf_op jit(solution)/shard_map/ppermute | solution.py:20
  145.8 1.5 collective-permute-start.12
  147.5 6.2 %collective-permute-done.23 = bf16[128,2048]{1,0:T(8,128)(2,1)S(1)} collective-permute-done((bf16[128,2048]{1,0:T(8,128)(2,1)S(1)}, bf16[128,2048]{1,0:T(8,128)(2,1)S(1)}, u32[]{:S(2)}, u32[]{:S(2)}) %collective-permute-start.23) | collective-permute-done | bytes 524320 | tf_op jit(solution)/shard_map/ppermute | solution.py:20
  155.1 1.9 collective-permute-start.35
  157.3 12.6 %collective-permute-done.12 = bf16[64,2048]{1,0:T(8,128)(2,1)S(1)} collective-permute-done((bf16[64,2048]{1,0:T(8,128)(2,1)S(1)}, bf16[64,2048]{1,0:T(8,128)(2,1)S(1)}, u32[]{:S(2)}, u32[]{:S(2)}) %collective-permute-start.12) | collective-permute-done | bytes 262176 | tf_op jit(solution)/shard_map/ppermute | solution.py:20
  169.9 1.9 collective-permute-start.24
  171.9 1.5 collective-permute-start.13
  173.6 1.5 collective-permute-start.11
  175.1 6.6 %collective-permute-done.24 = bf16[128,2048]{1,0:T(8,128)(2,1)S(1)} collective-permute-done((bf16[128,2048]{1,0:T(8,128)(2,1)S(1)}, bf16[128,2048]{1,0:T(8,128)(2,1)S(1)}, u32[]{:S(2)}, u32[]{:S(2)}) %collective-permute-start.24) | collective-permute-done | bytes 524320 | tf_op jit(solution)/shard_map/ppermute | solution.py:20
  182.0 2.3 %collective-permute-start.25 = (bf16[128,2048]{1,0:T(8,128)(2,1)S(1)}, bf16[128,2048]{1,0:T(8,128)(2,1)S(1)}, u32[]{:S(2)}, u32[]{:S(2)}) collective-permute-start(bf16[128,2048]{1,0:T(8,128)(2,1)S(1)} %add_convert_fusion.2), channel_id=1, source_target_pairs={{0,16},{1,17},{2,18},{3,19},{4,20},{5,21},{6,22},{7,23},{8,0},{9,1... | collective-permute-start | bytes 1572872 | tf_op jit(solution)/shard_map/ppermute | solution.py:20
  184.3 8.6 %collective-permute-done.25 = bf16[128,2048]{1,0:T(8,128)(2,1)S(1)} collective-permute-done((bf16[128,2048]{1,0:T(8,128)(2,1)S(1)}, bf16[128,2048]{1,0:T(8,128)(2,1)S(1)}, u32[]{:S(2)}, u32[]{:S(2)}) %collective-permute-start.25) | collective-permute-done | bytes 524320 | tf_op jit(solution)/shard_map/ppermute | solution.py:20
  193.0 1.2 add_convert_fusion
  (98 shorter events, 12.3 us)
Async XLA Ops:
  6.5 64.6 %all-gather.9.cloned.1.call-start = ((), (), s32[]{:S(2)}) async-start(), calls=%async_computation | async-start | bytes 6291456 | tf_op jit(solution)/shard_map/all_gather | solution.py:230
  7.3 63.9 %all-gather.11.cloned.1.call-start = ((), (), s32[]{:S(2)}) async-start(), calls=%async_computation.1 | async-start | bytes 6291456 | tf_op jit(solution)/shard_map/all_gather | solution.py:230
  8.0 53.5 %copy-start.12 = (bf16[2048]{0:T(1024)(128)(2,1)S(1)}, bf16[2048]{0:T(1024)(128)(2,1)}, u32[]{:S(2)}) copy-start(bf16[2048]{0:T(1024)(128)(2,1)} %param.17) | copy-start | bytes 12292
  8.0 63.1 %all-gather.13.cloned.1.call-start = ((), (), s32[]{:S(2)}) async-start(), calls=%async_computation.2 | async-start | bytes 6291456 | tf_op jit(solution)/shard_map/all_gather | solution.py:230
  10.7 15.8 %collective-permute-start.1 = (bf16[128,2176]{1,0:T(8,128)(2,1)}, bf16[128,2176]{1,0:T(8,128)(2,1)S(1)}, u32[]{:S(2)}, u32[]{:S(2)}) collective-permute-start(bf16[128,2176]{1,0:T(8,128)(2,1)} %shard_map.91.refs_0_), channel_id=1, source_target_pairs={{0,4},{1,5},{2,6},{3,7},{4,0},{5,1},{6,2},{7,3},{8,12},{9,13},{10,... | collective-permute-start | bytes 1671176 | tf_op jit(solution)/shard_map/ppermute | solution.py:20
  13.7 17.3 %collective-permute-start = (bf16[128,2176]{1,0:T(8,128)(2,1)}, bf16[128,2176]{1,0:T(8,128)(2,1)S(1)}, u32[]{:S(2)}, u32[]{:S(2)}) collective-permute-start(bf16[128,2176]{1,0:T(8,128)(2,1)} %shard_map.91.refs_0_), channel_id=1, source_target_pairs={{0,2},{1,3},{2,0},{3,1},{4,6},{5,7},{6,4},{7,5},{8,10},{9,11},{10,... | collective-permute-start | bytes 1671176 | tf_op jit(solution)/shard_map/ppermute | solution.py:20
  15.2 17.7 %collective-permute-start.26 = (bf16[128,2176]{1,0:T(8,128)(2,1)}, bf16[128,2176]{1,0:T(8,128)(2,1)S(1)}, u32[]{:S(2)}, u32[]{:S(2)}) collective-permute-start(bf16[128,2176]{1,0:T(8,128)(2,1)} %shard_map.91.refs_0_), channel_id=1, source_target_pairs={{0,16},{1,17},{2,18},{3,19},{4,20},{5,21},{6,22},{7,23},{8,0},{9,1... | collective-permute-start | bytes 1671176 | tf_op jit(solution)/shard_map/ppermute | solution.py:20
  17.8 25.4 %collective-permute-start.5 = (bf16[128,2176]{1,0:T(8,128)(2,1)}, bf16[128,2176]{1,0:T(8,128)(2,1)}, u32[]{:S(2)}, u32[]{:S(2)}) collective-permute-start(bf16[128,2176]{1,0:T(8,128)(2,1)} %shard_map.91.refs_0_), channel_id=1, source_target_pairs={{0,8},{1,9},{2,10},{3,11},{4,12},{5,13},{6,14},{7,15},{8,24},{9,25... | collective-permute-start | bytes 1671176 | tf_op jit(solution)/shard_map/ppermute | solution.py:20
  26.6 17.1 %collective-permute-start.2 = (bf16[64,2176]{1,0:T(8,128)(2,1)S(1)}, bf16[64,2176]{1,0:T(8,128)(2,1)S(1)}, u32[]{:S(2)}, u32[]{:S(2)}) collective-permute-start(bf16[64,2176]{1,0:T(8,128)(2,1)S(1)} %slice.72), channel_id=1, source_target_pairs={{0,2},{1,3},{2,0},{3,1},{4,6},{5,7},{6,4},{7,5},{8,10},{9,11},{10,... | collective-permute-start | bytes 835592 | tf_op jit(solution)/shard_map/ppermute | solution.py:20
  30.7 30.8 %collective-permute-start.4 = (bf16[768,256]{1,0:T(8,128)(2,1)}, bf16[768,256]{1,0:T(8,128)(2,1)S(1)}, u32[]{:S(2)}, u32[]{:S(2)}) collective-permute-start(bf16[768,256]{1,0:T(8,128)(2,1)} %get-tuple-element.26), channel_id=1, source_target_pairs={{0,2},{1,3},{2,0},{3,1},{4,6},{5,7},{6,4},{7,5},{8,10},{9,11},{10,... | collective-permute-start | bytes 1179656 | tf_op jit(solution)/shard_map/ppermute | solution.py:20
  31.1 13.4 %collective-permute-start.3 = (bf16[64,2176]{1,0:T(8,128)(2,1)S(1)}, bf16[64,2176]{1,0:T(8,128)(2,1)S(1)}, u32[]{:S(2)}, u32[]{:S(2)}) collective-permute-start(bf16[64,2176]{1,0:T(8,128)(2,1)S(1)} %slice.73), channel_id=1, source_target_pairs={{0,4},{1,5},{2,6},{3,7},{4,0},{5,1},{6,2},{7,3},{8,12},{9,13},{10,... | collective-permute-start | bytes 835592 | tf_op jit(solution)/shard_map/ppermute | solution.py:20
  32.9 26.1 %copy-start.8 = (bf16[128,2176]{1,0:T(8,128)(2,1)}, bf16[128,2176]{1,0:T(8,128)(2,1)S(1)}, u32[]{:S(2)}) copy-start(bf16[128,2176]{1,0:T(8,128)(2,1)S(1)} %collective-permute-done.26.refs_0_) | copy-start | bytes 1671172
  32.9 25.5 %collective-permute-start.27 = (bf16[128,2176]{1,0:T(8,128)(2,1)S(1)}, bf16[128,2176]{1,0:T(8,128)(2,1)S(1)}, u32[]{:S(2)}, u32[]{:S(2)}) collective-permute-start(bf16[128,2176]{1,0:T(8,128)(2,1)S(1)} %collective-permute-done.26.refs_0_), channel_id=1, source_target_pairs={{0,2},{1,3},{2,0},{3,1},{4,6},{5,7},{6,4},{7,5},{8,10},{9,11},{10,... | collective-permute-start | bytes 1671176 | tf_op jit(solution)/shard_map/ppermute | solution.py:20
  43.2 14.5 %collective-permute-start.28 = (bf16[128,2176]{1,0:T(8,128)(2,1)S(1)}, bf16[128,2176]{1,0:T(8,128)(2,1)S(1)}, u32[]{:S(2)}, u32[]{:S(2)}) collective-permute-start(bf16[128,2176]{1,0:T(8,128)(2,1)S(1)} %collective-permute-done.26.refs_0_), channel_id=1, source_target_pairs={{0,4},{1,5},{2,6},{3,7},{4,0},{5,1},{6,2},{7,3},{8,12},{9,13},{10,... | collective-permute-start | bytes 1671176 | tf_op jit(solution)/shard_map/ppermute | solution.py:20
  43.7 21.7 %collective-permute-start.16 = (bf16[128,2176]{1,0:T(8,128)(2,1)}, bf16[128,2176]{1,0:T(8,128)(2,1)}, u32[]{:S(2)}, u32[]{:S(2)}) collective-permute-start(bf16[128,2176]{1,0:T(8,128)(2,1)} %collective-permute-done.5.refs_0_), channel_id=1, source_target_pairs={{0,8},{1,9},{2,10},{3,11},{4,12},{5,13},{6,14},{7,15},{8,24},{9,25... | collective-permute-start | bytes 1671176 | tf_op jit(solution)/shard_map/ppermute | solution.py:20
  44.5 17.1 %copy-start.3 = (bf16[128,2176]{1,0:T(8,128)(2,1)}, bf16[128,2176]{1,0:T(8,128)(2,1)S(1)}, u32[]{:S(2)}) copy-start(bf16[128,2176]{1,0:T(8,128)(2,1)S(1)} %constant_dynamic-update-slice_fusion.refs_3_) | copy-start | bytes 1671172
  44.5 26.6 %collective-permute-start.8 = (bf16[128,2176]{1,0:T(8,128)(2,1)S(1)}, bf16[128,2176]{1,0:T(8,128)(2,1)}, u32[]{:S(2)}, u32[]{:S(2)}) collective-permute-start(bf16[128,2176]{1,0:T(8,128)(2,1)S(1)} %constant_dynamic-update-slice_fusion.refs_3_), channel_id=1, source_target_pairs={{0,8},{1,9},{2,10},{3,11},{4,12},{5,13},{6,14},{7,15},{8,24},{9,25... | collective-permute-start | bytes 1671176 | tf_op jit(solution)/shard_map/ppermute | solution.py:20
  57.7 3.8 %copy-start.1 = (bf16[128,2176]{1,0:T(8,128)(2,1)}, bf16[128,2176]{1,0:T(8,128)(2,1)S(1)}, u32[]{:S(2)}) copy-start(bf16[128,2176]{1,0:T(8,128)(2,1)S(1)} %collective-permute-done.28.refs_2_) | copy-start | bytes 1671172
  57.8 9.2 %collective-permute-start.29 = (bf16[64,2176]{1,0:T(8,128)(2,1)S(1)}, bf16[64,2176]{1,0:T(8,128)(2,1)S(1)}, u32[]{:S(2)}, u32[]{:S(2)}) collective-permute-start(bf16[64,2176]{1,0:T(8,128)(2,1)S(1)} %slice.76), channel_id=1, source_target_pairs={{0,2},{1,3},{2,0},{3,1},{4,6},{5,7},{6,4},{7,5},{8,10},{9,11},{10,... | collective-permute-start | bytes 835592 | tf_op jit(solution)/shard_map/ppermute | solution.py:20
  58.4 9.1 %collective-permute-start.30 = (bf16[64,2176]{1,0:T(8,128)(2,1)S(1)}, bf16[64,2176]{1,0:T(8,128)(2,1)S(1)}, u32[]{:S(2)}, u32[]{:S(2)}) collective-permute-start(bf16[64,2176]{1,0:T(8,128)(2,1)S(1)} %slice.77), channel_id=1, source_target_pairs={{0,4},{1,5},{2,6},{3,7},{4,0},{5,1},{6,2},{7,3},{8,12},{9,13},{10,... | collective-permute-start | bytes 835592 | tf_op jit(solution)/shard_map/ppermute | solution.py:20
  63.9 40.9 %collective-permute-start.6 = (bf16[128,2176]{1,0:T(8,128)(2,1)}, bf16[128,2176]{1,0:T(8,128)(2,1)}, u32[]{:S(2)}, u32[]{:S(2)}) collective-permute-start(bf16[128,2176]{1,0:T(8,128)(2,1)} %collective-permute-done.5.refs_0_), channel_id=1, source_target_pairs={{0,2},{1,3},{2,0},{3,1},{4,6},{5,7},{6,4},{7,5},{8,10},{9,11},{10,... | collective-permute-start | bytes 1671176 | tf_op jit(solution)/shard_map/ppermute | solution.py:20
  65.4 40.0 %collective-permute-start.7 = (bf16[128,2176]{1,0:T(8,128)(2,1)}, bf16[128,2176]{1,0:T(8,128)(2,1)}, u32[]{:S(2)}, u32[]{:S(2)}) collective-permute-start(bf16[128,2176]{1,0:T(8,128)(2,1)} %collective-permute-done.5.refs_0_), channel_id=1, source_target_pairs={{0,4},{1,5},{2,6},{3,7},{4,0},{5,1},{6,2},{7,3},{8,12},{9,13},{10,... | collective-permute-start | bytes 1671176 | tf_op jit(solution)/shard_map/ppermute | solution.py:20
  67.0 23.9 %collective-permute-start.17 = (bf16[128,2176]{1,0:T(8,128)(2,1)}, bf16[128,2176]{1,0:T(8,128)(2,1)}, u32[]{:S(2)}, u32[]{:S(2)}) collective-permute-start(bf16[128,2176]{1,0:T(8,128)(2,1)} %collective-permute-done.16.refs_0_), channel_id=1, source_target_pairs={{0,2},{1,3},{2,0},{3,1},{4,6},{5,7},{6,4},{7,5},{8,10},{9,11},{10,... | collective-permute-start | bytes 1671176 | tf_op jit(solution)/shard_map/ppermute | solution.py:20
  68.2 24.1 %collective-permute-start.18 = (bf16[128,2176]{1,0:T(8,128)(2,1)}, bf16[128,2176]{1,0:T(8,128)(2,1)}, u32[]{:S(2)}, u32[]{:S(2)}) collective-permute-start(bf16[128,2176]{1,0:T(8,128)(2,1)} %collective-permute-done.16.refs_0_), channel_id=1, source_target_pairs={{0,4},{1,5},{2,6},{3,7},{4,0},{5,1},{6,2},{7,3},{8,12},{9,13},{10,... | collective-permute-start | bytes 1671176 | tf_op jit(solution)/shard_map/ppermute | solution.py:20
  71.1 22.8 %collective-permute-start.19 = (bf16[128,2176]{1,0:T(8,128)(2,1)}, bf16[128,2176]{1,0:T(8,128)(2,1)}, u32[]{:S(2)}, u32[]{:S(2)}) collective-permute-start(bf16[128,2176]{1,0:T(8,128)(2,1)} %collective-permute-done.8.refs_3_), channel_id=1, source_target_pairs={{0,8},{1,9},{2,10},{3,11},{4,12},{5,13},{6,14},{7,15},{8,24},{9,25... | collective-permute-start | bytes 1671176 | tf_op jit(solution)/shard_map/ppermute | solution.py:20
  72.2 2.2 %copy-start.5 = (bf16[2,2048,512]{2,1,0:T(8,128)(2,1)S(1)}, bf16[2,2048,512]{2,1,0:T(8,128)(2,1)}, u32[]{:S(2)}) copy-start(bf16[2,2048,512]{2,1,0:T(8,128)(2,1)} %all-gather.9.cloned.1.call-done) | copy-start | bytes 12582916
  74.4 2.2 %copy-start.6 = (bf16[2,2048,512]{2,1,0:T(8,128)(2,1)S(1)}, bf16[2,2048,512]{2,1,0:T(8,128)(2,1)}, u32[]{:S(2)}) copy-start(bf16[2,2048,512]{2,1,0:T(8,128)(2,1)} %all-gather.11.cloned.1.call-done) | copy-start | bytes 12582916
  76.6 2.2 %copy-start.7 = (bf16[2,512,2048]{2,1,0:T(8,128)(2,1)S(1)}, bf16[2,512,2048]{2,1,0:T(8,128)(2,1)}, u32[]{:S(2)}) copy-start(bf16[2,512,2048]{2,1,0:T(8,128)(2,1)} %all-gather.13.cloned.1.call-done) | copy-start | bytes 12582916
  90.9 37.6 %collective-permute-start.33 = (bf16[64,2048]{1,0:T(8,128)(2,1)S(1)}, bf16[64,2048]{1,0:T(8,128)(2,1)S(1)}, u32[]{:S(2)}, u32[]{:S(2)}) collective-permute-start(bf16[64,2048]{1,0:T(8,128)(2,1)S(1)} %get-tuple-element.44), channel_id=1, source_target_pairs={{0,2},{1,3},{2,0},{3,1},{4,6},{5,7},{6,4},{7,5},{8,10},{9,11},{10,... | collective-permute-start | bytes 786440 | tf_op jit(solution)/shard_map/ppermute | solution.py:20
  92.4 38.0 %collective-permute-start.31 = (bf16[64,2048]{1,0:T(8,128)(2,1)S(1)}, bf16[64,2048]{1,0:T(8,128)(2,1)S(1)}, u32[]{:S(2)}, u32[]{:S(2)}) collective-permute-start(bf16[64,2048]{1,0:T(8,128)(2,1)S(1)} %get-tuple-element.42), channel_id=1, source_target_pairs={{0,4},{1,5},{2,6},{3,7},{4,0},{5,1},{6,2},{7,3},{8,12},{9,13},{10,... | collective-permute-start | bytes 786440 | tf_op jit(solution)/shard_map/ppermute | solution.py:20
  104.2 26.8 %collective-permute-start.22 = (bf16[64,2048]{1,0:T(8,128)(2,1)S(1)}, bf16[64,2048]{1,0:T(8,128)(2,1)S(1)}, u32[]{:S(2)}, u32[]{:S(2)}) collective-permute-start(bf16[64,2048]{1,0:T(8,128)(2,1)S(1)} %get-tuple-element.39), channel_id=1, source_target_pairs={{0,2},{1,3},{2,0},{3,1},{4,6},{5,7},{6,4},{7,5},{8,10},{9,11},{10,... | collective-permute-start | bytes 786440 | tf_op jit(solution)/shard_map/ppermute | solution.py:20
  104.9 12.5 %copy-start = (bf16[128,2176]{1,0:T(8,128)(2,1)S(1)}, bf16[128,2176]{1,0:T(8,128)(2,1)}, u32[]{:S(2)}) copy-start(bf16[128,2176]{1,0:T(8,128)(2,1)} %shard_map.91.refs_0_) | copy-start | bytes 1671172
  104.9 12.5 %copy-start.4 = (bf16[128,2176]{1,0:T(8,128)(2,1)S(1)}, bf16[128,2176]{1,0:T(8,128)(2,1)}, u32[]{:S(2)}) copy-start(bf16[128,2176]{1,0:T(8,128)(2,1)} %copy-done.3) | copy-start | bytes 1671172
  104.9 27.3 %collective-permute-start.20 = (bf16[64,2048]{1,0:T(8,128)(2,1)S(1)}, bf16[64,2048]{1,0:T(8,128)(2,1)S(1)}, u32[]{:S(2)}, u32[]{:S(2)}) collective-permute-start(bf16[64,2048]{1,0:T(8,128)(2,1)S(1)} %get-tuple-element.37), channel_id=1, source_target_pairs={{0,4},{1,5},{2,6},{3,7},{4,0},{5,1},{6,2},{7,3},{8,12},{9,13},{10,... | collective-permute-start | bytes 786440 | tf_op jit(solution)/shard_map/ppermute | solution.py:20
  115.8 57.8 %collective-permute-start.15 = (bf16[128,2048]{1,0:T(8,128)(2,1)S(1)}, bf16[128,2048]{1,0:T(8,128)(2,1)S(1)}, u32[]{:S(2)}, u32[]{:S(2)}) collective-permute-start(bf16[128,2048]{1,0:T(8,128)(2,1)S(1)} %get-tuple-element.34), channel_id=1, source_target_pairs={{0,4},{1,5},{2,6},{3,7},{4,0},{5,1},{6,2},{7,3},{8,12},{9,13},{10,... | collective-permute-start | bytes 1572872 | tf_op jit(solution)/shard_map/ppermute | solution.py:20
  128.5 11.8 %collective-permute-start.9 = (bf16[128,2048]{1,0:T(8,128)(2,1)S(1)}, bf16[128,2048]{1,0:T(8,128)(2,1)S(1)}, u32[]{:S(2)}, u32[]{:S(2)}) collective-permute-start(bf16[128,2048]{1,0:T(8,128)(2,1)S(1)} %get-tuple-element.30), channel_id=1, source_target_pairs={{0,16},{1,17},{2,18},{3,19},{4,20},{5,21},{6,22},{7,23},{8,0},{9,1... | collective-permute-start | bytes 1572872 | tf_op jit(solution)/shard_map/ppermute | solution.py:20
  130.3 14.9 %collective-permute-start.34 = (bf16[128,2048]{1,0:T(8,128)(2,1)S(1)}, bf16[128,2048]{1,0:T(8,128)(2,1)S(1)}, u32[]{:S(2)}, u32[]{:S(2)}) collective-permute-start(bf16[128,2048]{1,0:T(8,128)(2,1)S(1)} %pad_maximum_fusion.5), channel_id=1, source_target_pairs={{0,4},{1,5},{2,6},{3,7},{4,0},{5,1},{6,2},{7,3},{8,12},{9,13},{10,... | collective-permute-start | bytes 1572872 | tf_op jit(solution)/shard_map/ppermute | solution.py:20
  131.0 14.8 %collective-permute-start.32 = (bf16[128,2048]{1,0:T(8,128)(2,1)S(1)}, bf16[128,2048]{1,0:T(8,128)(2,1)S(1)}, u32[]{:S(2)}, u32[]{:S(2)}) collective-permute-start(bf16[128,2048]{1,0:T(8,128)(2,1)S(1)} %pad_maximum_fusion.4), channel_id=1, source_target_pairs={{0,2},{1,3},{2,0},{3,1},{4,6},{5,7},{6,4},{7,5},{8,10},{9,11},{10,... | collective-permute-start | bytes 1572872 | tf_op jit(solution)/shard_map/ppermute | solution.py:20
  132.1 21.6 %collective-permute-start.23 = (bf16[128,2048]{1,0:T(8,128)(2,1)S(1)}, bf16[128,2048]{1,0:T(8,128)(2,1)S(1)}, u32[]{:S(2)}, u32[]{:S(2)}) collective-permute-start(bf16[128,2048]{1,0:T(8,128)(2,1)S(1)} %pad_maximum_fusion.3), channel_id=1, source_target_pairs={{0,4},{1,5},{2,6},{3,7},{4,0},{5,1},{6,2},{7,3},{8,12},{9,13},{10,... | collective-permute-start | bytes 1572872 | tf_op jit(solution)/shard_map/ppermute | solution.py:20
  140.3 14.9 %collective-permute-start.21 = (bf16[128,2048]{1,0:T(8,128)(2,1)S(1)}, bf16[128,2048]{1,0:T(8,128)(2,1)S(1)}, u32[]{:S(2)}, u32[]{:S(2)}) collective-permute-start(bf16[128,2048]{1,0:T(8,128)(2,1)S(1)} %pad_maximum_fusion.2), channel_id=1, source_target_pairs={{0,2},{1,3},{2,0},{3,1},{4,6},{5,7},{6,4},{7,5},{8,10},{9,11},{10,... | collective-permute-start | bytes 1572872 | tf_op jit(solution)/shard_map/ppermute | solution.py:20
  145.3 29.8 %collective-permute-start.14 = (bf16[128,2048]{1,0:T(8,128)(2,1)S(1)}, bf16[128,2048]{1,0:T(8,128)(2,1)S(1)}, u32[]{:S(2)}, u32[]{:S(2)}) collective-permute-start(bf16[128,2048]{1,0:T(8,128)(2,1)S(1)} %get-tuple-element.33), channel_id=1, source_target_pairs={{0,2},{1,3},{2,0},{3,1},{4,6},{5,7},{6,4},{7,5},{8,10},{9,11},{10,... | collective-permute-start | bytes 1572872 | tf_op jit(solution)/shard_map/ppermute | solution.py:20
  145.8 24.1 %collective-permute-start.12 = (bf16[64,2048]{1,0:T(8,128)(2,1)S(1)}, bf16[64,2048]{1,0:T(8,128)(2,1)S(1)}, u32[]{:S(2)}, u32[]{:S(2)}) collective-permute-start(bf16[64,2048]{1,0:T(8,128)(2,1)S(1)} %get-tuple-element.46), channel_id=1, source_target_pairs={{0,2},{1,3},{2,0},{3,1},{4,6},{5,7},{6,4},{7,5},{8,10},{9,11},{10,... | collective-permute-start | bytes 786440 | tf_op jit(solution)/shard_map/ppermute | solution.py:20
  153.7 18.2 %collective-permute-start.10 = (bf16[64,2048]{1,0:T(8,128)(2,1)S(1)}, bf16[64,2048]{1,0:T(8,128)(2,1)S(1)}, u32[]{:S(2)}, u32[]{:S(2)}) collective-permute-start(bf16[64,2048]{1,0:T(8,128)(2,1)S(1)} %get-tuple-element.45), channel_id=1, source_target_pairs={{0,4},{1,5},{2,6},{3,7},{4,0},{5,1},{6,2},{7,3},{8,12},{9,13},{10,... | collective-permute-start | bytes 786440 | tf_op jit(solution)/shard_map/ppermute | solution.py:20
  155.1 29.2 %collective-permute-start.35 = (bf16[128,2048]{1,0:T(8,128)(2,1)S(1)}, bf16[128,2048]{1,0:T(8,128)(2,1)S(1)}, u32[]{:S(2)}, u32[]{:S(2)}) collective-permute-start(bf16[128,2048]{1,0:T(8,128)(2,1)S(1)} %add_convert_fusion.1), channel_id=1, source_target_pairs={{0,8},{1,9},{2,10},{3,11},{4,12},{5,13},{6,14},{7,15},{8,24},{9,25... | collective-permute-start | bytes 1572872 | tf_op jit(solution)/shard_map/ppermute | solution.py:20
  169.9 11.8 %collective-permute-start.24 = (bf16[128,2048]{1,0:T(8,128)(2,1)S(1)}, bf16[128,2048]{1,0:T(8,128)(2,1)S(1)}, u32[]{:S(2)}, u32[]{:S(2)}) collective-permute-start(bf16[128,2048]{1,0:T(8,128)(2,1)S(1)} %add_convert_fusion.3), channel_id=1, source_target_pairs={{0,16},{1,17},{2,18},{3,19},{4,20},{5,21},{6,22},{7,23},{8,0},{9,1... | collective-permute-start | bytes 1572872 | tf_op jit(solution)/shard_map/ppermute | solution.py:20
  171.9 12.4 %collective-permute-start.13 = (bf16[128,2048]{1,0:T(8,128)(2,1)S(1)}, bf16[128,2048]{1,0:T(8,128)(2,1)S(1)}, u32[]{:S(2)}, u32[]{:S(2)}) collective-permute-start(bf16[128,2048]{1,0:T(8,128)(2,1)S(1)} %pad_maximum_fusion.1), channel_id=1, source_target_pairs={{0,4},{1,5},{2,6},{3,7},{4,0},{5,1},{6,2},{7,3},{8,12},{9,13},{10,... | collective-permute-start | bytes 1572872 | tf_op jit(solution)/shard_map/ppermute | solution.py:20
  173.6 10.8 %collective-permute-start.11 = (bf16[128,2048]{1,0:T(8,128)(2,1)S(1)}, bf16[128,2048]{1,0:T(8,128)(2,1)S(1)}, u32[]{:S(2)}, u32[]{:S(2)}) collective-permute-start(bf16[128,2048]{1,0:T(8,128)(2,1)S(1)} %pad_maximum_fusion), channel_id=1, source_target_pairs={{0,2},{1,3},{2,0},{3,1},{4,6},{5,7},{6,4},{7,5},{8,10},{9,11},{10,... | collective-permute-start | bytes 1572872 | tf_op jit(solution)/shard_map/ppermute | solution.py:20
  182.0 10.9 %collective-permute-start.25 = (bf16[128,2048]{1,0:T(8,128)(2,1)S(1)}, bf16[128,2048]{1,0:T(8,128)(2,1)S(1)}, u32[]{:S(2)}, u32[]{:S(2)}) collective-permute-start(bf16[128,2048]{1,0:T(8,128)(2,1)S(1)} %add_convert_fusion.2), channel_id=1, source_target_pairs={{0,16},{1,17},{2,18},{3,19},{4,20},{5,21},{6,22},{7,23},{8,0},{9,1... | collective-permute-start | bytes 1572872 | tf_op jit(solution)/shard_map/ppermute | solution.py:20
  (4 other events, 3.8 us)
Sparse Core Ops, SparseCore 0:
  8.9 16.3 all-gather.8
  26.8 14.8 all-gather.10
  43.3 14.8 all-gather.12

commit v4 on v3

--- a/solution.py
+++ b/solution.py
@@ -18,6 +18,10 @@
         z, y, x, core = step(z, y, x, core)
         pairs.append((device, ((z * 2 + y) * 2 + x) * 2 + core))
     return lax.ppermute(array, BOTH, pairs)
+
+
+def ordered(array, *done):
+    return lax.optimization_barrier((array, *done))[0] if done else array
 
 
 def to_x(z, y, x, core):
@@ -182,7 +186,7 @@
             pltpu.VMEM((2, hidden, width), bf16),
             pltpu.SemaphoreType.DMA((3, 4)),
         ],
-        compiler_params=pltpu.CompilerParams(vmem_limit_bytes=28 * 1024 * 1024),
+        compiler_params=pltpu.CompilerParams(vmem_limit_bytes=40 * 1024 * 1024),
         cost_estimate=pl.CostEstimate(
             flops=2 * rows * width * hidden * 6, bytes_accessed=16 * 2**20, transcendentals=rows * hidden * 2
         ),
@@ -240,34 +244,39 @@
     x1, y1 = on_x(first, to_x), on_y(first, to_y)
     corner1 = on_z(corner0, ring_on)
     third = on_z(wide, ring_back)
-    x2, y2 = on_x(second, to_x), on_y(second, to_y)
+    x2, y2 = on_x(ordered(second, *experts), to_x), on_y(second, to_y)
     corner2 = on_z(corner1, ring_on)
     far = on_x(sent, to_x)
     x3, y3 = on_x(third, to_x), on_y(third, to_y)
     top, low = on_x(y3[:half], to_x), on_y(x3[half:], to_y)
     full, halves = (rows,) * 4, (rows,) * 3 + (half,) * 2
-    partial1 = run_feed((first, x1, y1, corner1), full, experts, ())
-    partial2 = run_feed((second, x2, y2, corner2), halves, experts, ())
-    partial3 = run_feed((third, x3, y3, top, low), halves, experts, ())
-    extra = (paired(own), paired(far), shared_switch.reshape(1, width))
-    partial0 = run_feed((wide, x0, y0, corner0), full, experts, extra)
 
     def straight(here, along_x, along_y):
         return here, on_x(along_x, to_x), on_y(along_y, to_y)
 
+    def corners(top, low):
+        return on_x(top, to_x), on_y(low, to_y)
+
     def in_plane(here, along_x, along_y, top, low):
-        top, low = on_x(top, to_x), on_y(low, to_y)
         return straight(here, low_added(along_x, low), top_added(along_y, top))
 
-    plane1 = straight(*partial1[:3])
+    partial1 = run_feed((first, x1, y1, corner1), full, experts, ())
+    plane1 = straight(*ordered(partial1[:3], x2, y2))
     corner = on_z(partial1[3], ring_back)
-    plane2 = in_plane(*partial2)
+    partial2 = run_feed((second, x2, y2, corner2), halves, experts, ())
+    ends2 = corners(*partial2[3:])
+    partial3 = run_feed((ordered(third, *plane1[1:]), x3, y3, top, low), halves, experts, ())
+    plane2 = in_plane(*partial2[:3], *ends2)
     second = on_z(summed(*plane2), ring_back)
-    plane3 = in_plane(*partial3)
+    ends3 = corners(*partial3[3:])
+    extra = (paired(own), paired(far), shared_switch.reshape(1, width))
+    partial0 = run_feed((ordered(wide, *ends2), x0, y0, corner0), full, experts, extra)
+    plane3 = in_plane(*partial3[:3], *ends3)
     first = on_z(summed(*plane1, second), ring_back)
     third = on_z(summed(*plane3), ring_on)
     corner = summed(partial0[3], corner)
-    plane0 = in_plane(*partial0[:3], corner[:half], corner[half:])
+    ends0 = corners(corner[:half], corner[half:])
+    plane0 = in_plane(*partial0[:3], *ends0)
     return summed(*plane0, first, third)
 
 

time: 201 us -> 191 us (0.950)
  waiting for transfers between devices: 79.3 us -> 75.3 us
  local copies, waits for them, and re-layouts: 10.6 us -> 6.87 us
    ppermute x36, waiting for transfers between devices: 77.2 us -> 73.2 us  [moved(): return lax.ppermute(array, BOTH, pairs)]
    unnamed x27 -> x13, local copies, waits for them, and re-layouts: 10.4 us -> 6.6 us
  transfers between devices with their start and end apart: 39 -> 39, of which waited for: 12 -> 12; matrix products, arithmetic and copies ran while one was open for 1% -> 1% of each run, Pallas kernels for 22% -> 23%
where the time goes in v4:
time: 191 us
  waiting for transfers between devices  75.3 us (39%)
  starting transfers between devices  43.9 us (23%)
  Pallas kernels  43.5 us (23%)
  between operations  13.4 us (7%)
  local copies, waits for them, and re-layouts  6.87 us (4%)
  blocking collectives  5.15 us (3%)
  other arithmetic  2.8 us (1%)
    ppermute x36, waiting for transfers between devices, moved(): return lax.ppermute(array, BOTH, pairs)  73.2 us
    ppermute x36, starting transfers between devices, moved(): return lax.ppermute(array, BOTH, pairs)  43.8 us
    pallas_call x4, Pallas kernels, run_feed(): pl.pallas_call(functools.partial(feed, bool(extra), len(parts)), grid=(4,...  38.7 us
    unnamed x13, local copies, waits for them, and re-layouts  6.6 us
    all_gather x2, blocking collectives, paired(): return lax.all_gather(part, 'dp', axis_index_groups=cores)  5.15 us
  transfers between devices with their start and end apart: 39, of which 12 were waited for; matrix products, arithmetic and copies ran while one was open for 1% of the time, Pallas kernels for 23%

profile of v4, /device:TPU:0, one launch (start us, length us, event | category | flops | bytes accessed | tf_op | source)
XLA Modules:
  0.0 191.0 jit_solution(14341757938978712938)
XLA Ops:
  8.8 2.0 %shard_map.91.refs_0_ = bf16[128,2176]{1,0:T(8,128)(2,1)} custom-call(bf16[128,2048]{1,0:T(8,128)(2,1)} %tokens_ref.1, s32[10,128]{1,0:T(8,128)} %bitcast.17, bf16[10,128]{1,0:T(8,128)(2,1)} %bitcast.18), custom_call_target="tpu_custom_call" | custom-call | tf_op jit(solution)/shard_map/pallas_call | solution.py:225
  10.7 3.0 %collective-permute-start.4 = (bf16[128,2176]{1,0:T(8,128)(2,1)}, bf16[128,2176]{1,0:T(8,128)(2,1)S(1)}, u32[]{:S(2)}, u32[]{:S(2)}) collective-permute-start(bf16[128,2176]{1,0:T(8,128)(2,1)} %shard_map.91.refs_0_), channel_id=1, source_target_pairs={{0,4},{1,5},{2,6},{3,7},{4,0},{5,1},{6,2},{7,3},{8,12},{9,13},{10,... | collective-permute-start | bytes 1671176 | tf_op jit(solution)/shard_map/ppermute | solution.py:20
  13.7 1.5 collective-permute-start.6
  15.2 1.6 collective-permute-start
  16.8 9.8 %collective-permute-done.4.refs_2_ = bf16[128,2176]{1,0:T(8,128)(2,1)S(1)} collective-permute-done((bf16[128,2176]{1,0:T(8,128)(2,1)}, bf16[128,2176]{1,0:T(8,128)(2,1)S(1)}, u32[]{:S(2)}, u32[]{:S(2)}) %collective-permute-start.4) | collective-permute-done | bytes 557088 | tf_op jit(solution)/shard_map/ppermute | solution.py:20
  26.6 1.8 collective-permute-start.5
  28.3 2.6 %collective-permute-start.26 = (bf16[128,2176]{1,0:T(8,128)(2,1)}, bf16[128,2176]{1,0:T(8,128)(2,1)S(1)}, u32[]{:S(2)}, u32[]{:S(2)}) collective-permute-start(bf16[128,2176]{1,0:T(8,128)(2,1)} %shard_map.91.refs_0_), channel_id=1, source_target_pairs={{0,16},{1,17},{2,18},{3,19},{4,20},{5,21},{6,22},{7,23},{8,0},{9,1... | collective-permute-start | bytes 1671176 | tf_op jit(solution)/shard_map/ppermute | solution.py:20
  31.0 1.6 collective-permute-start.7
  32.5 2.0 %collective-permute-done.5 = bf16[64,2176]{1,0:T(8,128)(2,1)S(1)} collective-permute-done((bf16[64,2176]{1,0:T(8,128)(2,1)S(1)}, bf16[64,2176]{1,0:T(8,128)(2,1)S(1)}, u32[]{:S(2)}, u32[]{:S(2)}) %collective-permute-start.5) | collective-permute-done | bytes 278560 | tf_op jit(solution)/shard_map/ppermute | solution.py:20
  34.6 3.5 %collective-permute-done.7 = bf16[64,2176]{1,0:T(8,128)(2,1)S(1)} collective-permute-done((bf16[64,2176]{1,0:T(8,128)(2,1)S(1)}, bf16[64,2176]{1,0:T(8,128)(2,1)S(1)}, u32[]{:S(2)}, u32[]{:S(2)}) %collective-permute-start.7) | collective-permute-done | bytes 278560 | tf_op jit(solution)/shard_map/ppermute | solution.py:20
  38.2 2.8 %shard_map.93 = (bf16[768,256]{1,0:T(8,128)(2,1)}, bf16[768,256]{1,0:T(8,128)(2,1)}) custom-call(bf16[512,1024]{1,0:T(8,128)(2,1)} %up_ref.1, bf16[512,512]{1,0:T(8,128)(2,1)} %down_ref.1), custom_call_target="tpu_custom_call" | custom-call | tf_op jit(solution)/shard_map/pallas_call | solution.py:230
  41.3 3.0 %collective-permute-done.26.refs_0_ = bf16[128,2176]{1,0:T(8,128)(2,1)S(1)} collective-permute-done((bf16[128,2176]{1,0:T(8,128)(2,1)}, bf16[128,2176]{1,0:T(8,128)(2,1)S(1)}, u32[]{:S(2)}, u32[]{:S(2)}) %collective-permute-start.26) | collective-permute-done | bytes 557088 | tf_op jit(solution)/shard_map/ppermute | solution.py:20
  44.4 1.5 collective-permute-start.28
  46.4 9.9 %collective-permute-done.1.refs_0_ = bf16[128,2176]{1,0:T(8,128)(2,1)} collective-permute-done((bf16[128,2176]{1,0:T(8,128)(2,1)}, bf16[128,2176]{1,0:T(8,128)(2,1)}, u32[]{:S(2)}, u32[]{:S(2)}) %collective-permute-start.1) | collective-permute-done | bytes 557088 | tf_op jit(solution)/shard_map/ppermute | solution.py:20
  56.3 1.5 collective-permute-start.3
  57.8 10.0 %collective-permute-done.8.refs_3_ = bf16[128,2176]{1,0:T(8,128)(2,1)} collective-permute-done((bf16[128,2176]{1,0:T(8,128)(2,1)S(1)}, bf16[128,2176]{1,0:T(8,128)(2,1)}, u32[]{:S(2)}, u32[]{:S(2)}) %collective-permute-start.8) | collective-permute-done | bytes 557088 | tf_op jit(solution)/shard_map/ppermute | solution.py:20
  67.8 0.7 collective-permute-start.9
  69.1 2.6 %all-gather.3 = bf16[1536,256]{1,0:T(8,128)(2,1)S(1)} all-gather(bf16[768,256]{1,0:T(8,128)(2,1)} %get-tuple-element.35), channel_id=5, replica_groups={{0,1},{2,3},{4,5},{6,7},{8,9},{10,11},{12,13},{14,15},{16,17},{18,19},{..., dimensions={0}, use_global_device_ids=true | all-gather | bytes 1179648 | tf_op jit(solution)/shard_map/all_gather | solution.py:234
  71.7 2.6 %all-gather.4 = bf16[1536,256]{1,0:T(8,128)(2,1)S(1)} all-gather(bf16[768,256]{1,0:T(8,128)(2,1)} %collective-permute-done.12), channel_id=6, replica_groups={{0,1},{2,3},{4,5},{6,7},{8,9},{10,11},{12,13},{14,15},{16,17},{18,19},{..., dimensions={0}, use_global_device_ids=true | all-gather | bytes 1179648 | tf_op jit(solution)/shard_map/all_gather | solution.py:234
  74.3 1.5 collective-permute-start.13
  75.8 1.6 collective-permute-start.14
  78.0 5.5 %collective-permute-done.9.refs_3_ = bf16[128,2176]{1,0:T(8,128)(2,1)} collective-permute-done((bf16[128,2176]{1,0:T(8,128)(2,1)}, bf16[128,2176]{1,0:T(8,128)(2,1)}, u32[]{:S(2)}, u32[]{:S(2)}) %collective-permute-start.9) | collective-permute-done | bytes 557088 | tf_op jit(solution)/shard_map/ppermute | solution.py:20
  83.5 1.5 collective-permute-start.30
  85.0 2.2 %copy-done.1 = bf16[2,2048,512]{2,1,0:T(8,128)(2,1)S(1)} copy-done((bf16[2,2048,512]{2,1,0:T(8,128)(2,1)S(1)}, bf16[2,2048,512]{2,1,0:T(8,128)(2,1)}, u32[]{:S(2)}) %copy-start.1) | copy-done | bytes 4194328
  87.2 2.2 %copy-done.3 = bf16[2,2048,512]{2,1,0:T(8,128)(2,1)S(1)} copy-done((bf16[2,2048,512]{2,1,0:T(8,128)(2,1)S(1)}, bf16[2,2048,512]{2,1,0:T(8,128)(2,1)}, u32[]{:S(2)}) %copy-start.3) | copy-done | bytes 4194328
  89.4 9.8 %shard_map.92 = (bf16[128,2048]{1,0:T(8,128)(2,1)S(1)}, bf16[128,2048]{1,0:T(8,128)(2,1)S(1)}, bf16[128,2048]{1,0:T(8,128)(2,1)S(1)}, bf16[64,2048]{1,0:T(8,128)(2,1)S(1)}, bf16[64,2048]{1,0:T(8,128)(2,1)S(1)}) custom-call(bf16[128,2176]{1,0:T(8,128)(2,1)} %collective-permute-done.1.refs_0_, bf16[128,2176]{1,0:T(8,128)(2,1)S(1)} %collective-permute-done.2.refs_1_, ...), custom_call_target="tpu_custom_call" | custom-call | flops 6442450944 | bytes 16777216 | tf_op jit(solution)/shard_map/pallas_call | solution.py:171
  99.9 0.8 collective-permute-start.11
  100.7 9.7 %shard_map.95 = (bf16[128,2048]{1,0:T(8,128)(2,1)S(1)}, bf16[128,2048]{1,0:T(8,128)(2,1)S(1)}, bf16[128,2048]{1,0:T(8,128)(2,1)S(1)}, bf16[128,2048]{1,0:T(8,128)(2,1)S(1)}) custom-call(bf16[128,2176]{1,0:T(8,128)(2,1)} %collective-permute-done.refs_0_, bf16[128,2176]{1,0:T(8,128)(2,1)S(1)} %collective-permute-done.13.refs_1_, ...), custom_call_target="tpu_custom_call" | custom-call | flops 6442450944 | bytes 16777216 | tf_op jit(solution)/shard_map/pallas_call | solution.py:171
  110.4 2.4 %collective-permute-start.15 = (bf16[128,2048]{1,0:T(8,128)(2,1)S(1)}, bf16[128,2048]{1,0:T(8,128)(2,1)S(1)}, u32[]{:S(2)}, u32[]{:S(2)}) collective-permute-start(bf16[128,2048]{1,0:T(8,128)(2,1)S(1)} %get-tuple-element.40), channel_id=1, source_target_pairs={{0,16},{1,17},{2,18},{3,19},{4,20},{5,21},{6,22},{7,23},{8,0},{9,1... | collective-permute-start | bytes 1572872 | tf_op jit(solution)/shard_map/ppermute | solution.py:20
  112.8 1.6 collective-permute-start.20
  114.9 10.8 %shard_map.94 = (bf16[128,2048]{1,0:T(8,128)(2,1)S(1)}, bf16[128,2048]{1,0:T(8,128)(2,1)S(1)}, bf16[128,2048]{1,0:T(8,128)(2,1)S(1)}, bf16[128,2048]{1,0:T(8,128)(2,1)S(1)}) custom-call(bf16[128,2176]{1,0:T(8,128)(2,1)S(1)} %copy-done, bf16[128,2176]{1,0:T(8,128)(2,1)S(1)} %collective-permute-done.6.refs_1_, ...), custom_call_target="tpu_custom_call" | custom-call | flops 6442450944 | bytes 16777216 | tf_op jit(solution)/shard_map/pallas_call | solution.py:171
  125.9 1.6 collective-permute-start.16
  128.4 1.5 collective-permute-start.22
  130.4 2.2 %copy-done.4 = bf16[2,2048,512]{2,1,0:T(8,128)(2,1)S(1)} copy-done((bf16[2,2048,512]{2,1,0:T(8,128)(2,1)S(1)}, bf16[2,2048,512]{2,1,0:T(8,128)(2,1)}, u32[]{:S(2)}) %copy-start.4) | copy-done | bytes 4194328
  132.6 8.4 %shard_map.96 = (bf16[128,2048]{1,0:T(8,128)(2,1)S(1)}, bf16[128,2048]{1,0:T(8,128)(2,1)S(1)}, bf16[128,2048]{1,0:T(8,128)(2,1)S(1)}, bf16[64,2048]{1,0:T(8,128)(2,1)S(1)}, bf16[64,2048]{1,0:T(8,128)(2,1)S(1)}) custom-call(bf16[128,2176]{1,0:T(8,128)(2,1)S(1)} %collective-permute-done.26.refs_0_, bf16[128,2176]{1,0:T(8,128)(2,1)S(1)} %collective-permute-done.27.refs_1_, ...), custom_call_target="tpu_custom_call" | custom-call | flops 6442450944 | bytes 16777216 | tf_op jit(solution)/shard_map/pallas_call | solution.py:171
  141.0 1.6 collective-permute-start.31
  143.4 1.6 collective-permute-start.17
  145.0 1.2 collective-permute-done.22
  146.4 2.0 %collective-permute-start.24 = (bf16[128,2048]{1,0:T(8,128)(2,1)S(1)}, bf16[128,2048]{1,0:T(8,128)(2,1)S(1)}, u32[]{:S(2)}, u32[]{:S(2)}) collective-permute-start(bf16[128,2048]{1,0:T(8,128)(2,1)S(1)} %add_convert_fusion.3), channel_id=1, source_target_pairs={{0,16},{1,17},{2,18},{3,19},{4,20},{5,21},{6,22},{7,23},{8,0},{9,1... | collective-permute-start | bytes 1572872 | tf_op jit(solution)/shard_map/ppermute | solution.py:20
  149.1 2.9 %collective-permute-done.33 = bf16[64,2048]{1,0:T(8,128)(2,1)S(1)} collective-permute-done((bf16[64,2048]{1,0:T(8,128)(2,1)S(1)}, bf16[64,2048]{1,0:T(8,128)(2,1)S(1)}, u32[]{:S(2)}, u32[]{:S(2)}) %collective-permute-start.33) | collective-permute-done | bytes 262176 | tf_op jit(solution)/shard_map/ppermute | solution.py:20
  152.1 1.0 collective-permute-start.34
  153.1 1.2 collective-permute-start.19
  154.3 6.2 %collective-permute-done.24 = bf16[128,2048]{1,0:T(8,128)(2,1)S(1)} collective-permute-done((bf16[128,2048]{1,0:T(8,128)(2,1)S(1)}, bf16[128,2048]{1,0:T(8,128)(2,1)S(1)}, u32[]{:S(2)}, u32[]{:S(2)}) %collective-permute-start.24) | collective-permute-done | bytes 524320 | tf_op jit(solution)/shard_map/ppermute | solution.py:20
  160.9 1.9 %collective-permute-start.25 = (bf16[128,2048]{1,0:T(8,128)(2,1)S(1)}, bf16[128,2048]{1,0:T(8,128)(2,1)S(1)}, u32[]{:S(2)}, u32[]{:S(2)}) collective-permute-start(bf16[128,2048]{1,0:T(8,128)(2,1)S(1)} %add_convert_fusion.2), channel_id=1, source_target_pairs={{0,16},{1,17},{2,18},{3,19},{4,20},{5,21},{6,22},{7,23},{8,0},{9,1... | collective-permute-start | bytes 1572872 | tf_op jit(solution)/shard_map/ppermute | solution.py:20
  162.8 8.5 %collective-permute-done.32 = bf16[128,2048]{1,0:T(8,128)(2,1)S(1)} collective-permute-done((bf16[128,2048]{1,0:T(8,128)(2,1)S(1)}, bf16[128,2048]{1,0:T(8,128)(2,1)S(1)}, u32[]{:S(2)}, u32[]{:S(2)}) %collective-permute-start.32) | collective-permute-done | bytes 524320 | tf_op jit(solution)/shard_map/ppermute | solution.py:20
  171.5 0.9 collective-permute-start.35
  172.5 10.8 %collective-permute-done.35 = bf16[128,2048]{1,0:T(8,128)(2,1)S(1)} collective-permute-done((bf16[128,2048]{1,0:T(8,128)(2,1)S(1)}, bf16[128,2048]{1,0:T(8,128)(2,1)S(1)}, u32[]{:S(2)}, u32[]{:S(2)}) %collective-permute-start.35) | collective-permute-done | bytes 524320 | tf_op jit(solution)/shard_map/ppermute | solution.py:20
  183.2 1.2 add_convert_fusion
  (84 shorter events, 9.7 us)
Async XLA Ops:
  6.5 61.9 %all-gather.9.cloned.1.call-start = ((), (), s32[]{:S(2)}) async-start(), calls=%async_computation | async-start | bytes 6291456 | tf_op jit(solution)/shard_map/all_gather | solution.py:234
  7.3 61.8 %copy-start.5 = (bf16[2048]{0:T(1024)(128)(2,1)S(1)}, bf16[2048]{0:T(1024)(128)(2,1)}, u32[]{:S(2)}) copy-start(bf16[2048]{0:T(1024)(128)(2,1)} %param.17) | copy-start | bytes 12292
  7.3 61.2 %all-gather.11.cloned.1.call-start = ((), (), s32[]{:S(2)}) async-start(), calls=%async_computation.1 | async-start | bytes 6291456 | tf_op jit(solution)/shard_map/all_gather | solution.py:234
  8.0 60.5 %all-gather.13.cloned.1.call-start = ((), (), s32[]{:S(2)}) async-start(), calls=%async_computation.2 | async-start | bytes 6291456 | tf_op jit(solution)/shard_map/all_gather | solution.py:234
  10.7 15.8 %collective-permute-start.4 = (bf16[128,2176]{1,0:T(8,128)(2,1)}, bf16[128,2176]{1,0:T(8,128)(2,1)S(1)}, u32[]{:S(2)}, u32[]{:S(2)}) collective-permute-start(bf16[128,2176]{1,0:T(8,128)(2,1)} %shard_map.91.refs_0_), channel_id=1, source_target_pairs={{0,4},{1,5},{2,6},{3,7},{4,0},{5,1},{6,2},{7,3},{8,12},{9,13},{10,... | collective-permute-start | bytes 1671176 | tf_op jit(solution)/shard_map/ppermute | solution.py:20
  13.7 17.2 %collective-permute-start.6 = (bf16[128,2176]{1,0:T(8,128)(2,1)}, bf16[128,2176]{1,0:T(8,128)(2,1)S(1)}, u32[]{:S(2)}, u32[]{:S(2)}) collective-permute-start(bf16[128,2176]{1,0:T(8,128)(2,1)} %shard_map.91.refs_0_), channel_id=1, source_target_pairs={{0,2},{1,3},{2,0},{3,1},{4,6},{5,7},{6,4},{7,5},{8,10},{9,11},{10,... | collective-permute-start | bytes 1671176 | tf_op jit(solution)/shard_map/ppermute | solution.py:20
  15.2 17.4 %collective-permute-start = (bf16[128,2176]{1,0:T(8,128)(2,1)}, bf16[128,2176]{1,0:T(8,128)(2,1)}, u32[]{:S(2)}, u32[]{:S(2)}) collective-permute-start(bf16[128,2176]{1,0:T(8,128)(2,1)} %shard_map.91.refs_0_), channel_id=1, source_target_pairs={{0,8},{1,9},{2,10},{3,11},{4,12},{5,13},{6,14},{7,15},{8,24},{9,25... | collective-permute-start | bytes 1671176 | tf_op jit(solution)/shard_map/ppermute | solution.py:20
  26.6 8.0 %collective-permute-start.5 = (bf16[64,2176]{1,0:T(8,128)(2,1)S(1)}, bf16[64,2176]{1,0:T(8,128)(2,1)S(1)}, u32[]{:S(2)}, u32[]{:S(2)}) collective-permute-start(bf16[64,2176]{1,0:T(8,128)(2,1)S(1)} %slice.72), channel_id=1, source_target_pairs={{0,2},{1,3},{2,0},{3,1},{4,6},{5,7},{6,4},{7,5},{8,10},{9,11},{10,... | collective-permute-start | bytes 835592 | tf_op jit(solution)/shard_map/ppermute | solution.py:20
  28.3 16.0 %collective-permute-start.26 = (bf16[128,2176]{1,0:T(8,128)(2,1)}, bf16[128,2176]{1,0:T(8,128)(2,1)S(1)}, u32[]{:S(2)}, u32[]{:S(2)}) collective-permute-start(bf16[128,2176]{1,0:T(8,128)(2,1)} %shard_map.91.refs_0_), channel_id=1, source_target_pairs={{0,16},{1,17},{2,18},{3,19},{4,20},{5,21},{6,22},{7,23},{8,0},{9,1... | collective-permute-start | bytes 1671176 | tf_op jit(solution)/shard_map/ppermute | solution.py:20
  31.0 7.1 %collective-permute-start.7 = (bf16[64,2176]{1,0:T(8,128)(2,1)S(1)}, bf16[64,2176]{1,0:T(8,128)(2,1)S(1)}, u32[]{:S(2)}, u32[]{:S(2)}) collective-permute-start(bf16[64,2176]{1,0:T(8,128)(2,1)S(1)} %slice.73), channel_id=1, source_target_pairs={{0,4},{1,5},{2,6},{3,7},{4,0},{5,1},{6,2},{7,3},{8,12},{9,13},{10,... | collective-permute-start | bytes 835592 | tf_op jit(solution)/shard_map/ppermute | solution.py:20
  32.5 23.8 %collective-permute-start.1 = (bf16[128,2176]{1,0:T(8,128)(2,1)}, bf16[128,2176]{1,0:T(8,128)(2,1)}, u32[]{:S(2)}, u32[]{:S(2)}) collective-permute-start(bf16[128,2176]{1,0:T(8,128)(2,1)} %collective-permute-done.refs_0_), channel_id=1, source_target_pairs={{0,8},{1,9},{2,10},{3,11},{4,12},{5,13},{6,14},{7,15},{8,24},{9,25... | collective-permute-start | bytes 1671176 | tf_op jit(solution)/shard_map/ppermute | solution.py:20
  38.1 29.6 %collective-permute-start.8 = (bf16[128,2176]{1,0:T(8,128)(2,1)S(1)}, bf16[128,2176]{1,0:T(8,128)(2,1)}, u32[]{:S(2)}, u32[]{:S(2)}) collective-permute-start(bf16[128,2176]{1,0:T(8,128)(2,1)S(1)} %constant_dynamic-update-slice_fusion.refs_3_), channel_id=1, source_target_pairs={{0,8},{1,9},{2,10},{3,11},{4,12},{5,13},{6,14},{7,15},{8,24},{9,25... | collective-permute-start | bytes 1671176 | tf_op jit(solution)/shard_map/ppermute | solution.py:20
  41.0 27.5 %collective-permute-start.12 = (bf16[768,256]{1,0:T(8,128)(2,1)}, bf16[768,256]{1,0:T(8,128)(2,1)}, u32[]{:S(2)}, u32[]{:S(2)}) collective-permute-start(bf16[768,256]{1,0:T(8,128)(2,1)} %get-tuple-element.36), channel_id=1, source_target_pairs={{0,2},{1,3},{2,0},{3,1},{4,6},{5,7},{6,4},{7,5},{8,10},{9,11},{10,... | collective-permute-start | bytes 1179656 | tf_op jit(solution)/shard_map/ppermute | solution.py:20
  44.4 29.9 %collective-permute-start.28 = (bf16[128,2176]{1,0:T(8,128)(2,1)S(1)}, bf16[128,2176]{1,0:T(8,128)(2,1)S(1)}, u32[]{:S(2)}, u32[]{:S(2)}) collective-permute-start(bf16[128,2176]{1,0:T(8,128)(2,1)S(1)} %collective-permute-done.26.refs_0_), channel_id=1, source_target_pairs={{0,4},{1,5},{2,6},{3,7},{4,0},{5,1},{6,2},{7,3},{8,12},{9,13},{10,... | collective-permute-start | bytes 1671176 | tf_op jit(solution)/shard_map/ppermute | solution.py:20
  45.9 29.9 %collective-permute-start.27 = (bf16[128,2176]{1,0:T(8,128)(2,1)S(1)}, bf16[128,2176]{1,0:T(8,128)(2,1)S(1)}, u32[]{:S(2)}, u32[]{:S(2)}) collective-permute-start(bf16[128,2176]{1,0:T(8,128)(2,1)S(1)} %collective-permute-done.26.refs_0_), channel_id=1, source_target_pairs={{0,2},{1,3},{2,0},{3,1},{4,6},{5,7},{6,4},{7,5},{8,10},{9,11},{10,... | collective-permute-start | bytes 1671176 | tf_op jit(solution)/shard_map/ppermute | solution.py:20
  56.3 21.1 %collective-permute-start.3 = (bf16[128,2176]{1,0:T(8,128)(2,1)}, bf16[128,2176]{1,0:T(8,128)(2,1)}, u32[]{:S(2)}, u32[]{:S(2)}) collective-permute-start(bf16[128,2176]{1,0:T(8,128)(2,1)} %collective-permute-done.1.refs_0_), channel_id=1, source_target_pairs={{0,4},{1,5},{2,6},{3,7},{4,0},{5,1},{6,2},{7,3},{8,12},{9,13},{10,... | collective-permute-start | bytes 1671176 | tf_op jit(solution)/shard_map/ppermute | solution.py:20
  67.8 15.8 %collective-permute-start.9 = (bf16[128,2176]{1,0:T(8,128)(2,1)}, bf16[128,2176]{1,0:T(8,128)(2,1)}, u32[]{:S(2)}, u32[]{:S(2)}) collective-permute-start(bf16[128,2176]{1,0:T(8,128)(2,1)} %collective-permute-done.8.refs_3_), channel_id=1, source_target_pairs={{0,8},{1,9},{2,10},{3,11},{4,12},{5,13},{6,14},{7,15},{8,24},{9,25... | collective-permute-start | bytes 1671176 | tf_op jit(solution)/shard_map/ppermute | solution.py:20
  68.5 16.6 %collective-permute-start.2 = (bf16[128,2176]{1,0:T(8,128)(2,1)}, bf16[128,2176]{1,0:T(8,128)(2,1)S(1)}, u32[]{:S(2)}, u32[]{:S(2)}) collective-permute-start(bf16[128,2176]{1,0:T(8,128)(2,1)} %collective-permute-done.1.refs_0_), channel_id=1, source_target_pairs={{0,2},{1,3},{2,0},{3,1},{4,6},{5,7},{6,4},{7,5},{8,10},{9,11},{10,... | collective-permute-start | bytes 1671176 | tf_op jit(solution)/shard_map/ppermute | solution.py:20
  74.3 25.6 %collective-permute-start.13 = (bf16[128,2176]{1,0:T(8,128)(2,1)}, bf16[128,2176]{1,0:T(8,128)(2,1)S(1)}, u32[]{:S(2)}, u32[]{:S(2)}) collective-permute-start(bf16[128,2176]{1,0:T(8,128)(2,1)} %collective-permute-done.refs_0_), channel_id=1, source_target_pairs={{0,2},{1,3},{2,0},{3,1},{4,6},{5,7},{6,4},{7,5},{8,10},{9,11},{10,... | collective-permute-start | bytes 1671176 | tf_op jit(solution)/shard_map/ppermute | solution.py:20
  75.8 24.9 %collective-permute-start.14 = (bf16[128,2176]{1,0:T(8,128)(2,1)}, bf16[128,2176]{1,0:T(8,128)(2,1)S(1)}, u32[]{:S(2)}, u32[]{:S(2)}) collective-permute-start(bf16[128,2176]{1,0:T(8,128)(2,1)} %collective-permute-done.refs_0_), channel_id=1, source_target_pairs={{0,4},{1,5},{2,6},{3,7},{4,0},{5,1},{6,2},{7,3},{8,12},{9,13},{10,... | collective-permute-start | bytes 1671176 | tf_op jit(solution)/shard_map/ppermute | solution.py:20
  77.4 52.5 %collective-permute-start.29 = (bf16[64,2176]{1,0:T(8,128)(2,1)S(1)}, bf16[64,2176]{1,0:T(8,128)(2,1)S(1)}, u32[]{:S(2)}, u32[]{:S(2)}) collective-permute-start(bf16[64,2176]{1,0:T(8,128)(2,1)S(1)} %slice.76), channel_id=1, source_target_pairs={{0,2},{1,3},{2,0},{3,1},{4,6},{5,7},{6,4},{7,5},{8,10},{9,11},{10,... | collective-permute-start | bytes 835592 | tf_op jit(solution)/shard_map/ppermute | solution.py:20
  83.5 46.9 %collective-permute-start.30 = (bf16[64,2176]{1,0:T(8,128)(2,1)S(1)}, bf16[64,2176]{1,0:T(8,128)(2,1)S(1)}, u32[]{:S(2)}, u32[]{:S(2)}) collective-permute-start(bf16[64,2176]{1,0:T(8,128)(2,1)S(1)} %slice.77), channel_id=1, source_target_pairs={{0,4},{1,5},{2,6},{3,7},{4,0},{5,1},{6,2},{7,3},{8,12},{9,13},{10,... | collective-permute-start | bytes 835592 | tf_op jit(solution)/shard_map/ppermute | solution.py:20
  85.0 2.2 %copy-start.1 = (bf16[2,2048,512]{2,1,0:T(8,128)(2,1)S(1)}, bf16[2,2048,512]{2,1,0:T(8,128)(2,1)}, u32[]{:S(2)}) copy-start(bf16[2,2048,512]{2,1,0:T(8,128)(2,1)} %all-gather.9.cloned.1.call-done) | copy-start | bytes 12582916
  87.2 2.2 %copy-start.3 = (bf16[2,2048,512]{2,1,0:T(8,128)(2,1)S(1)}, bf16[2,2048,512]{2,1,0:T(8,128)(2,1)}, u32[]{:S(2)}) copy-start(bf16[2,2048,512]{2,1,0:T(8,128)(2,1)} %all-gather.11.cloned.1.call-done) | copy-start | bytes 12582916
  99.3 13.5 %collective-permute-start.10 = (bf16[64,2048]{1,0:T(8,128)(2,1)S(1)}, bf16[64,2048]{1,0:T(8,128)(2,1)S(1)}, u32[]{:S(2)}, u32[]{:S(2)}) collective-permute-start(bf16[64,2048]{1,0:T(8,128)(2,1)S(1)} %get-tuple-element.32), channel_id=1, source_target_pairs={{0,2},{1,3},{2,0},{3,1},{4,6},{5,7},{6,4},{7,5},{8,10},{9,11},{10,... | collective-permute-start | bytes 786440 | tf_op jit(solution)/shard_map/ppermute | solution.py:20
  99.9 15.0 %copy-start = (bf16[128,2176]{1,0:T(8,128)(2,1)S(1)}, bf16[128,2176]{1,0:T(8,128)(2,1)}, u32[]{:S(2)}) copy-start(bf16[128,2176]{1,0:T(8,128)(2,1)} %shard_map.91.refs_0_) | copy-start | bytes 1671172
  99.9 14.5 %collective-permute-start.11 = (bf16[64,2048]{1,0:T(8,128)(2,1)S(1)}, bf16[64,2048]{1,0:T(8,128)(2,1)S(1)}, u32[]{:S(2)}, u32[]{:S(2)}) collective-permute-start(bf16[64,2048]{1,0:T(8,128)(2,1)S(1)} %get-tuple-element.33), channel_id=1, source_target_pairs={{0,4},{1,5},{2,6},{3,7},{4,0},{5,1},{6,2},{7,3},{8,12},{9,13},{10,... | collective-permute-start | bytes 786440 | tf_op jit(solution)/shard_map/ppermute | solution.py:20
  110.4 15.3 %collective-permute-start.15 = (bf16[128,2048]{1,0:T(8,128)(2,1)S(1)}, bf16[128,2048]{1,0:T(8,128)(2,1)S(1)}, u32[]{:S(2)}, u32[]{:S(2)}) collective-permute-start(bf16[128,2048]{1,0:T(8,128)(2,1)S(1)} %get-tuple-element.40), channel_id=1, source_target_pairs={{0,16},{1,17},{2,18},{3,19},{4,20},{5,21},{6,22},{7,23},{8,0},{9,1... | collective-permute-start | bytes 1572872 | tf_op jit(solution)/shard_map/ppermute | solution.py:20
  112.8 14.9 %collective-permute-start.20 = (bf16[128,2048]{1,0:T(8,128)(2,1)S(1)}, bf16[128,2048]{1,0:T(8,128)(2,1)S(1)}, u32[]{:S(2)}, u32[]{:S(2)}) collective-permute-start(bf16[128,2048]{1,0:T(8,128)(2,1)S(1)} %get-tuple-element.46), channel_id=1, source_target_pairs={{0,2},{1,3},{2,0},{3,1},{4,6},{5,7},{6,4},{7,5},{8,10},{9,11},{10,... | collective-permute-start | bytes 1572872 | tf_op jit(solution)/shard_map/ppermute | solution.py:20
  114.4 14.0 %collective-permute-start.21 = (bf16[128,2048]{1,0:T(8,128)(2,1)S(1)}, bf16[128,2048]{1,0:T(8,128)(2,1)S(1)}, u32[]{:S(2)}, u32[]{:S(2)}) collective-permute-start(bf16[128,2048]{1,0:T(8,128)(2,1)S(1)} %get-tuple-element.47), channel_id=1, source_target_pairs={{0,4},{1,5},{2,6},{3,7},{4,0},{5,1},{6,2},{7,3},{8,12},{9,13},{10,... | collective-permute-start | bytes 1572872 | tf_op jit(solution)/shard_map/ppermute | solution.py:20
  125.7 4.7 %copy-start.2 = (bf16[2,2048,512]{2,1,0:T(8,128)(2,1)S(1)}, bf16[2,2048,512]{2,1,0:T(8,128)(2,1)}, u32[]{:S(2)}) copy-start(bf16[2,2048,512]{2,1,0:T(8,128)(2,1)} %all-gather.9.cloned.1.call-done) | copy-start | bytes 12582916
  125.9 16.8 %collective-permute-start.16 = (bf16[64,2048]{1,0:T(8,128)(2,1)S(1)}, bf16[64,2048]{1,0:T(8,128)(2,1)S(1)}, u32[]{:S(2)}, u32[]{:S(2)}) collective-permute-start(bf16[64,2048]{1,0:T(8,128)(2,1)S(1)} %get-tuple-element.57), channel_id=1, source_target_pairs={{0,4},{1,5},{2,6},{3,7},{4,0},{5,1},{6,2},{7,3},{8,12},{9,13},{10,... | collective-permute-start | bytes 786440 | tf_op jit(solution)/shard_map/ppermute | solution.py:20
  127.8 15.6 %collective-permute-start.18 = (bf16[64,2048]{1,0:T(8,128)(2,1)S(1)}, bf16[64,2048]{1,0:T(8,128)(2,1)S(1)}, u32[]{:S(2)}, u32[]{:S(2)}) collective-permute-start(bf16[64,2048]{1,0:T(8,128)(2,1)S(1)} %get-tuple-element.58), channel_id=1, source_target_pairs={{0,2},{1,3},{2,0},{3,1},{4,6},{5,7},{6,4},{7,5},{8,10},{9,11},{10,... | collective-permute-start | bytes 786440 | tf_op jit(solution)/shard_map/ppermute | solution.py:20
  128.4 17.8 %collective-permute-start.22 = (bf16[128,2048]{1,0:T(8,128)(2,1)S(1)}, bf16[128,2048]{1,0:T(8,128)(2,1)S(1)}, u32[]{:S(2)}, u32[]{:S(2)}) collective-permute-start(bf16[128,2048]{1,0:T(8,128)(2,1)S(1)} %pad_maximum_fusion.2), channel_id=1, source_target_pairs={{0,2},{1,3},{2,0},{3,1},{4,6},{5,7},{6,4},{7,5},{8,10},{9,11},{10,... | collective-permute-start | bytes 1572872 | tf_op jit(solution)/shard_map/ppermute | solution.py:20
  129.9 16.3 %collective-permute-start.23 = (bf16[128,2048]{1,0:T(8,128)(2,1)S(1)}, bf16[128,2048]{1,0:T(8,128)(2,1)S(1)}, u32[]{:S(2)}, u32[]{:S(2)}) collective-permute-start(bf16[128,2048]{1,0:T(8,128)(2,1)S(1)} %pad_maximum_fusion.3), channel_id=1, source_target_pairs={{0,4},{1,5},{2,6},{3,7},{4,0},{5,1},{6,2},{7,3},{8,12},{9,13},{10,... | collective-permute-start | bytes 1572872 | tf_op jit(solution)/shard_map/ppermute | solution.py:20
  130.4 2.2 %copy-start.4 = (bf16[2,2048,512]{2,1,0:T(8,128)(2,1)S(1)}, bf16[2,2048,512]{2,1,0:T(8,128)(2,1)}, u32[]{:S(2)}) copy-start(bf16[2,2048,512]{2,1,0:T(8,128)(2,1)} %all-gather.11.cloned.1.call-done) | copy-start | bytes 12582916
  141.0 7.4 %collective-permute-start.31 = (bf16[64,2048]{1,0:T(8,128)(2,1)S(1)}, bf16[64,2048]{1,0:T(8,128)(2,1)S(1)}, u32[]{:S(2)}, u32[]{:S(2)}) collective-permute-start(bf16[64,2048]{1,0:T(8,128)(2,1)S(1)} %get-tuple-element.54), channel_id=1, source_target_pairs={{0,4},{1,5},{2,6},{3,7},{4,0},{5,1},{6,2},{7,3},{8,12},{9,13},{10,... | collective-permute-start | bytes 786440 | tf_op jit(solution)/shard_map/ppermute | solution.py:20
  142.7 9.3 %collective-permute-start.33 = (bf16[64,2048]{1,0:T(8,128)(2,1)S(1)}, bf16[64,2048]{1,0:T(8,128)(2,1)S(1)}, u32[]{:S(2)}, u32[]{:S(2)}) collective-permute-start(bf16[64,2048]{1,0:T(8,128)(2,1)S(1)} %get-tuple-element.56), channel_id=1, source_target_pairs={{0,2},{1,3},{2,0},{3,1},{4,6},{5,7},{6,4},{7,5},{8,10},{9,11},{10,... | collective-permute-start | bytes 786440 | tf_op jit(solution)/shard_map/ppermute | solution.py:20
  143.4 29.1 %collective-permute-start.17 = (bf16[128,2048]{1,0:T(8,128)(2,1)S(1)}, bf16[128,2048]{1,0:T(8,128)(2,1)S(1)}, u32[]{:S(2)}, u32[]{:S(2)}) collective-permute-start(bf16[128,2048]{1,0:T(8,128)(2,1)S(1)} %pad_maximum_fusion), channel_id=1, source_target_pairs={{0,2},{1,3},{2,0},{3,1},{4,6},{5,7},{6,4},{7,5},{8,10},{9,11},{10,... | collective-permute-start | bytes 1572872 | tf_op jit(solution)/shard_map/ppermute | solution.py:20
  146.4 14.1 %collective-permute-start.24 = (bf16[128,2048]{1,0:T(8,128)(2,1)S(1)}, bf16[128,2048]{1,0:T(8,128)(2,1)S(1)}, u32[]{:S(2)}, u32[]{:S(2)}) collective-permute-start(bf16[128,2048]{1,0:T(8,128)(2,1)S(1)} %add_convert_fusion.3), channel_id=1, source_target_pairs={{0,16},{1,17},{2,18},{3,19},{4,20},{5,21},{6,22},{7,23},{8,0},{9,1... | collective-permute-start | bytes 1572872 | tf_op jit(solution)/shard_map/ppermute | solution.py:20
  148.5 22.8 %collective-permute-start.32 = (bf16[128,2048]{1,0:T(8,128)(2,1)S(1)}, bf16[128,2048]{1,0:T(8,128)(2,1)S(1)}, u32[]{:S(2)}, u32[]{:S(2)}) collective-permute-start(bf16[128,2048]{1,0:T(8,128)(2,1)S(1)} %pad_maximum_fusion.4), channel_id=1, source_target_pairs={{0,2},{1,3},{2,0},{3,1},{4,6},{5,7},{6,4},{7,5},{8,10},{9,11},{10,... | collective-permute-start | bytes 1572872 | tf_op jit(solution)/shard_map/ppermute | solution.py:20
  152.1 19.2 %collective-permute-start.34 = (bf16[128,2048]{1,0:T(8,128)(2,1)S(1)}, bf16[128,2048]{1,0:T(8,128)(2,1)S(1)}, u32[]{:S(2)}, u32[]{:S(2)}) collective-permute-start(bf16[128,2048]{1,0:T(8,128)(2,1)S(1)} %pad_maximum_fusion.5), channel_id=1, source_target_pairs={{0,4},{1,5},{2,6},{3,7},{4,0},{5,1},{6,2},{7,3},{8,12},{9,13},{10,... | collective-permute-start | bytes 1572872 | tf_op jit(solution)/shard_map/ppermute | solution.py:20
  153.1 19.4 %collective-permute-start.19 = (bf16[128,2048]{1,0:T(8,128)(2,1)S(1)}, bf16[128,2048]{1,0:T(8,128)(2,1)S(1)}, u32[]{:S(2)}, u32[]{:S(2)}) collective-permute-start(bf16[128,2048]{1,0:T(8,128)(2,1)S(1)} %pad_maximum_fusion.1), channel_id=1, source_target_pairs={{0,4},{1,5},{2,6},{3,7},{4,0},{5,1},{6,2},{7,3},{8,12},{9,13},{10,... | collective-permute-start | bytes 1572872 | tf_op jit(solution)/shard_map/ppermute | solution.py:20
  160.9 11.6 %collective-permute-start.25 = (bf16[128,2048]{1,0:T(8,128)(2,1)S(1)}, bf16[128,2048]{1,0:T(8,128)(2,1)S(1)}, u32[]{:S(2)}, u32[]{:S(2)}) collective-permute-start(bf16[128,2048]{1,0:T(8,128)(2,1)S(1)} %add_convert_fusion.2), channel_id=1, source_target_pairs={{0,16},{1,17},{2,18},{3,19},{4,20},{5,21},{6,22},{7,23},{8,0},{9,1... | collective-permute-start | bytes 1572872 | tf_op jit(solution)/shard_map/ppermute | solution.py:20
  171.5 11.7 %collective-permute-start.35 = (bf16[128,2048]{1,0:T(8,128)(2,1)S(1)}, bf16[128,2048]{1,0:T(8,128)(2,1)S(1)}, u32[]{:S(2)}, u32[]{:S(2)}) collective-permute-start(bf16[128,2048]{1,0:T(8,128)(2,1)S(1)} %add_convert_fusion.1), channel_id=1, source_target_pairs={{0,8},{1,9},{2,10},{3,11},{4,12},{5,13},{6,14},{7,15},{8,24},{9,25... | collective-permute-start | bytes 1572872 | tf_op jit(solution)/shard_map/ppermute | solution.py:20
Sparse Core Ops, SparseCore 0:
  8.9 16.3 all-gather.8
  26.8 14.8 all-gather.10
  43.3 14.8 all-gather.12
